TPU v7x, 32 devices: a whole 2x2x4 slice. The times are simulated.
32 devices in a mesh: conf: 2 (over y), row: 4 (over z), col: 4 (over x, core).
Axes of the slice: x: 2, y: 2, z: 4, core: 2. Of those that a mesh axis runs over, the one named last changes fastest.
Arguments:
- pair_state: bfloat16 [512, 256, 128], P(('conf', 'row'), 'col'), parts along dimension 0, may hold values from -6 to 6
- token_kinds: int32 [512], P('conf'), parts along dimension 0, may hold values from 0 to 31
- first_type_table: bfloat16 [32, 128], replicated, may hold values from -3 to 3
- second_type_table: bfloat16 [32, 128], replicated, may hold values from -3 to 3
- alignment_state: bfloat16 [64, 16384], P(None, ('conf', 'row', 'col')), parts along dimension 1, may hold values from -6 to 6
- alignment_index: int32 [64, 512], P(None, ('conf', 'row', 'col')), parts along dimension 1, may hold values from 0 to 31
- alignment_table: bfloat16 [32, 32], replicated, may hold values from -3 to 3
- first_weight: bfloat16 [32, 32], replicated, may hold values from -1 to 1
- second_weight: bfloat16 [32, 32], replicated, may hold values from -1 to 1
- outer_product_weight: bfloat16 [1024, 128], replicated, may hold values from -1.5 to 1.5
- outer_product_bias: bfloat16 [128], replicated, may hold values from -4 to 4
- pair_block_mask: int32 [32, 16], P(('conf', 'row'), 'col'), parts along dimension 0, may hold values 0 or 1
- transition_gain: float32 [128], replicated, may hold values from 0.25 to 1.75
- transition_gate_up: bfloat16 [128, 1024], replicated, may hold values from -0.5 to 0.5
- transition_down: bfloat16 [512, 128], replicated, may hold values from -0.25 to 0.25
- distance_weight: bfloat16 [128, 64], replicated, may hold values from -0.5 to 0.5
- distance_bias: float32 [64], replicated, may hold values from -4 to 4
Outputs:
- pair_out: bfloat16 [512, 256, 128], P(('conf', 'row'), 'col'), parts along dimension 0
- distogram: bfloat16 [512, 16384], P(('conf', 'row'), 'col'), parts along dimension 0
There are 2 independent parts, one for each index of `conf`. A program takes and returns all parts, laid end to end along the dimension named above; an argument that names none is the same for every part. Nothing has to cross between parts.
All inputs are finite; a program needn't handle non-finite values. No bound on the sum of `pair_block_mask` on one device may be relied on, other than what follows from the above.
Results may differ from a plain program's by a relative error of at most 0.0071.
Values may be sent and summed in bfloat16 or wider, within the bound.
No kernel may reach another device: no remote copies, remote signals or barrier semaphores. Data moves between devices by JAX's collectives and lax.ppermute only.
A program may use at most 64 MiB of HBM per device.

v0:
```python
import math

import jax
import jax.numpy as jnp
from jax import lax
from jax.sharding import PartitionSpec as P

EPSILON = 1e-05


def from_root(value, axis, source):
    kept = jnp.where(lax.axis_index(axis) == source, value, 0).astype(value.dtype)
    return lax.psum(kept, axis)


def indicator_rows(indices, lookup_table):
    level_values = lookup_table.shape[0]
    onehot = (indices[..., None] == jnp.arange(level_values, dtype=jnp.int32)).astype(jnp.bfloat16)
    return jnp.einsum("...k,kc->...c", onehot, lookup_table, preferred_element_type=jnp.float32)


def local(
    pair_state,
    token_kinds,
    first_type_table,
    second_type_table,
    alignment_state,
    alignment_index,
    alignment_table,
    first_weight,
    second_weight,
    outer_product_weight,
    outer_product_bias,
    pair_block_mask,
    transition_gain,
    transition_gate_up,
    transition_down,
    distance_weight,
    distance_bias,
):
    block_length = pair_state.shape[0]
    alignment_depth = alignment_index.shape[0]
    local_tokens = alignment_index.shape[1]
    alignment_width = alignment_state.shape[1] // local_tokens
    hid_width = transition_down.shape[0]
    pair_width = pair_state.shape[2]
    row_index = lax.axis_index("row")
    col_index = lax.axis_index("col")
    embedded_input = alignment_state.reshape(alignment_depth, local_tokens, alignment_width).astype(
        jnp.float32
    ) + indicator_rows(alignment_index, alignment_table)
    embedded_input = embedded_input.astype(jnp.bfloat16)
    left_proj = jnp.einsum(
        "snm,mc->snc", embedded_input, first_weight, preferred_element_type=jnp.float32
    ).astype(jnp.bfloat16)
    right_proj = jnp.einsum(
        "snm,mc->snc", embedded_input, second_weight, preferred_element_type=jnp.float32
    ).astype(jnp.bfloat16)
    right_rows = lax.all_gather(right_proj, "col", axis=1, tiled=True)
    right_block = from_root(right_rows, "row", col_index)
    row_types = lax.dynamic_slice_in_dim(token_kinds, row_index * block_length, block_length, 0)
    col_types = lax.dynamic_slice_in_dim(token_kinds, col_index * block_length, block_length, 0)
    left_embed = indicator_rows(row_types, first_type_table)
    right_embed = indicator_rows(col_types, second_type_table)
    mask_side = block_length // pair_block_mask.shape[0]
    mask_full = jnp.repeat(
        jnp.repeat(pair_block_mask, mask_side, axis=0), mask_side, axis=1
    ).astype(jnp.float32)
    bias_float = outer_product_bias.astype(jnp.float32)
    fragment = lax.all_gather(left_proj, "col", axis=1, tiled=True)
    row_count = fragment.shape[1]
    rows_per_step = math.gcd(row_count, max(1, 512 // block_length))

    def one_block(block_index):
        first_row = block_index * rows_per_step
        left_part = lax.dynamic_slice_in_dim(fragment, first_row, rows_per_step, 1)
        outer_average = jnp.einsum(
            "sic,sje->ijce", left_part, right_block, preferred_element_type=jnp.float32
        )
        outer_average = (
            (outer_average / alignment_depth)
            .astype(jnp.bfloat16)
            .reshape(rows_per_step * block_length, -1)
        )
        update = jnp.dot(
            outer_average, outer_product_weight, preferred_element_type=jnp.float32
        ).reshape(rows_per_step, block_length, pair_width)
        update = update + bias_float
        pair_part = lax.dynamic_slice_in_dim(pair_state, first_row, rows_per_step, 0).astype(
            jnp.float32
        )
        embed_part = lax.dynamic_slice_in_dim(left_embed, first_row, rows_per_step, 0)
        mask_part = lax.dynamic_slice_in_dim(mask_full, first_row, rows_per_step, 0)
        start_pair = (
            pair_part
            + embed_part[:, None, :]
            + right_embed[None, :, :]
            + mask_part[:, :, None] * update
        )
        chan_mean = jnp.mean(start_pair, axis=-1, keepdims=True)
        centered = start_pair - chan_mean
        chan_var = jnp.mean(centered * centered, axis=-1, keepdims=True)
        normed = (centered * lax.rsqrt(chan_var + EPSILON) * transition_gain).astype(jnp.bfloat16)
        gate_up = jnp.dot(
            normed.reshape(rows_per_step * block_length, pair_width),
            transition_gate_up,
            preferred_element_type=jnp.float32,
        )
        hidden = (jax.nn.silu(gate_up[:, :hid_width]) * gate_up[:, hid_width:]).astype(jnp.bfloat16)
        branch = jnp.dot(hidden, transition_down, preferred_element_type=jnp.float32).reshape(
            rows_per_step, block_length, pair_width
        )
        return (start_pair + branch).astype(jnp.bfloat16)

    outputs = lax.map(one_block, jnp.arange(row_count // rows_per_step, dtype=jnp.int32))
    pair_out = outputs.reshape(row_count, block_length, pair_width)
    dist_here = jnp.einsum(
        "xyc,cb->xyb", pair_out, distance_weight, preferred_element_type=jnp.float32
    ).astype(jnp.bfloat16)
    width = pair_out.shape[2]
    sectioned = pair_out.reshape(1, 1, block_length, block_length, width)
    sectioned = lax.all_to_all(
        lax.all_to_all(sectioned, "row", split_axis=3, concat_axis=1, tiled=True),
        "col",
        split_axis=1,
        concat_axis=0,
        tiled=True,
    )
    sectioned = lax.all_to_all(sectioned, "row", split_axis=0, concat_axis=3, tiled=True)
    mirror_tile = sectioned.reshape(block_length, block_length, width)
    mirror_part = jnp.einsum(
        "yxc,cb->xyb", mirror_tile, distance_weight, preferred_element_type=jnp.float32
    ).astype(jnp.bfloat16)
    logits = dist_here.astype(jnp.float32) + mirror_part.astype(jnp.float32) + distance_bias
    distogram = logits.astype(jnp.bfloat16).reshape(block_length, -1)
    return (pair_out, distogram)


def solution(mesh):
    in_specs = (
        P(("conf", "row"), "col", None),
        P("conf"),
        P(),
        P(),
        P(None, ("conf", "row", "col")),
        P(None, ("conf", "row", "col")),
        P(),
        P(),
        P(),
        P(),
        P(),
        P(("conf", "row"), "col"),
        P(),
        P(),
        P(),
        P(),
        P(),
    )
    out_specs = (P(("conf", "row"), "col", None), P(("conf", "row"), "col"))
    return jax.shard_map(local, mesh=mesh, in_specs=in_specs, out_specs=out_specs, check_vma=False)
```

profile of v0, /device:TPU:2, one launch (start us, length us, event | category | flops | bytes accessed | tf_op | source)
XLA Modules:
  0.0 190.7 jit_solution(14172722387577988170)
XLA Ops:
  7.3 0.9 copy.38
  8.2 0.9 fusion.16
  9.2 0.9 convolution_convert_fusion.2
  10.2 6.9 %all_gather.7 = bf16[64,64,32]{0,2,1:T(8,128)(2,1)S(1)} all-gather(bf16[64,16,32]{0,2,1:T(8,128)(2,1)S(1)} %convolution_convert_fusion.2), channel_id=1, replica_groups=mesh['conf'=2,'row'=4,'col'=4] {'col'}, dimensions={1}, use_global_device_ids=true | all-gather | bytes 327680 | tf_op jit(solution)/shard_map/all_gather | solution.py:59
  17.1 0.8 broadcast_select_fusion
  18.5 7.3 %all_gather.6 = bf16[64,64,32]{0,2,1:T(8,128)(2,1)S(1)} all-gather(bf16[64,16,32]{0,2,1:T(8,128)(2,1)S(1)} %convolution_convert_fusion.3), channel_id=1, replica_groups=mesh['conf'=2,'row'=4,'col'=4] {'col'}, dimensions={1}, use_global_device_ids=true | all-gather | bytes 327680 | tf_op jit(solution)/shard_map/all_gather | solution.py:70
  26.3 31.3 %all-reduce.2.cloned.1.call-done = bf16[64,64,32]{0,2,1:T(8,128)(2,1)} async-done(((bf16[64,64,32]{0,2,1:T(8,128)(2,1)}), bf16[64,64,32]{0,2,1:T(8,128)(2,1)}) %all-reduce.2.cloned.1.call-update) | async-done | bytes 262160 | tf_op jit(solution)/shard_map/psum | solution.py:13
  57.7 1.6 copy.43
  59.3 47.6 %while.10 = (s32[]{:T(128)}, bf16[8,8,64,128]{3,2,1,0:T(8,128)(2,1)S(1)}, s32[8]{0:T(128)S(1)}, bf16[64,64,128]{2,1,0:T(8,128)(2,1)}, f32[64,128]{1,0:T(8,128)S(...) while((s32[]{:T(128)}, ...), condition=%wide.region_4.5_spmd, body=%wide.region_1.4_spmd.sunk | while | flops 406323712 | bytes 11801843 | solution.py:115
  62.1 1.7 fusion.60
  68.1 1.7 fusion.60
  73.2 0.8 copy.66
  74.0 1.7 fusion.60
  79.1 0.8 copy.66
  80.0 1.7 fusion.60
  85.9 1.7 fusion.60
  91.9 1.7 fusion.60
  97.8 1.7 fusion.60
  102.9 0.8 copy.66
  103.8 1.7 fusion.60
  107.6 27.9 %all_to_all.45 = bf16[1,1,64,64,128]{4,2,1,0,3:T(8,128)(2,1)S(1)} all-to-all(bf16[1,1,64,64,128]{4,2,1,0,3:T(8,128)(2,1)S(1)} %bitcast.109), channel_id=1, replica_groups=mesh['conf'=2,'row'=4,'col'=4] {'row'}, dimensions={3} | all-to-all | bytes 2097152 | tf_op jit(solution)/shard_map/all_to_all | solution.py:123
  136.2 15.9 %all_to_all.46 = bf16[1,4,64,16,128]{4,3,2,0,1:T(8,128)(2,1)S(1)} all-to-all(bf16[1,4,64,16,128]{4,3,2,0,1:T(8,128)(2,1)S(1)} %bitcast.105), channel_id=1, replica_groups=mesh['conf'=2,'row'=4,'col'=4] {'col'}, dimensions={1} | all-to-all | bytes 2097152 | tf_op jit(solution)/shard_map/all_to_all | solution.py:122
  152.1 28.5 %all_to_all.47 = bf16[4,1,64,16,128]{4,3,2,1,0:T(8,128)(2,1)S(1)} all-to-all(bf16[4,1,64,16,128]{4,3,2,1,0:T(8,128)(2,1)S(1)} %bitcast.106), channel_id=1, replica_groups=mesh['conf'=2,'row'=4,'col'=4] {'row'}, dimensions={0} | all-to-all | bytes 2097152 | tf_op jit(solution)/shard_map/all_to_all | solution.py:129
  182.2 1.6 reshape.59
  (139 shorter events, 29.3 us)
Async XLA Ops:
  7.2 173.8 %copy-start = (bf16[128,64]{0,1:T(8,128)(2,1)S(1)}, bf16[128,64]{0,1:T(8,128)(2,1)}, u32[]{:S(2)}) copy-start(bf16[128,64]{0,1:T(8,128)(2,1)} %param.34) | copy-start | bytes 49156
  7.2 10.8 %copy-start.5 = (bf16[32,32]{1,0:T(8,128)(2,1)S(1)}, bf16[32,32]{1,0:T(8,128)(2,1)}, u32[]{:S(2)}) copy-start(bf16[32,32]{1,0:T(8,128)(2,1)} %param.26) | copy-start | bytes 6148
  7.2 11.0 %copy-start.7 = (s32[256]{0:T(256)S(1)}, s32[256]{0:T(256)}, u32[]{:S(2)}) copy-start(s32[256]{0:T(256)} %param.20) | copy-start | bytes 3076
  7.2 11.1 %copy-start.10 = (bf16[32,128]{1,0:T(8,128)(2,1)S(1)}, bf16[32,128]{1,0:T(8,128)(2,1)}, u32[]{:S(2)}) copy-start(bf16[32,128]{1,0:T(8,128)(2,1)} %param.21) | copy-start | bytes 24580
  7.2 50.4 %all-reduce.2.cloned.1.call-start = ((), (), s32[]{:S(2)}) async-start(), calls=%async_computation.3 | async-start | bytes 1048576 | tf_op jit(solution)/shard_map/psum | solution.py:13
  7.3 18.5 %copy-start.6 = (s32[4,4]{1,0:T(4,128)S(1)}, s32[4,4]{1,0:T(4,128)}, u32[]{:S(2)}) copy-start(s32[4,4]{1,0:T(4,128)} %param.30) | copy-start | bytes 196
  8.2 17.9 %copy-start.12 = (bf16[128]{0:T(256)(128)(2,1)S(1)}, bf16[128]{0:T(256)(128)(2,1)}, u32[]{:S(2)}) copy-start(bf16[128]{0:T(256)(128)(2,1)} %param.29) | copy-start | bytes 772
  8.2 17.9 %copy-start.11 = (bf16[32,128]{1,0:T(8,128)(2,1)S(1)}, bf16[32,128]{1,0:T(8,128)(2,1)}, u32[]{:S(2)}) copy-start(bf16[32,128]{1,0:T(8,128)(2,1)} %param.22) | copy-start | bytes 24580
  10.1 49.1 %copy-start.1 = (bf16[1024,128]{1,0:T(8,128)(2,1)S(1)}, bf16[1024,128]{1,0:T(8,128)(2,1)}, u32[]{:S(2)}) copy-start(bf16[1024,128]{1,0:T(8,128)(2,1)} %param.28) | copy-start | bytes 786436
  10.1 49.1 %copy-start.2 = (bf16[128,1024]{1,0:T(8,128)(2,1)S(1)}, bf16[128,1024]{1,0:T(8,128)(2,1)}, u32[]{:S(2)}) copy-start(bf16[128,1024]{1,0:T(8,128)(2,1)} %param.32) | copy-start | bytes 786436
  10.2 49.1 %copy-start.4 = (f32[128]{0:T(128)S(1)}, f32[128]{0:T(128)}, u32[]{:S(2)}) copy-start(f32[128]{0:T(128)} %param.31) | copy-start | bytes 1540
  10.2 49.1 %copy-start.9 = (bf16[512,128]{1,0:T(8,128)(2,1)S(1)}, bf16[512,128]{1,0:T(8,128)(2,1)}, u32[]{:S(2)}) copy-start(bf16[512,128]{1,0:T(8,128)(2,1)} %param.33) | copy-start | bytes 393220
  106.9 74.8 %copy-start.3 = (bf16[8,8,64,128]{3,2,1,0:T(8,128)(2,1)}, bf16[8,8,64,128]{3,2,1,0:T(8,128)(2,1)S(1)}, u32[]{:S(2)}) copy-start(bf16[8,8,64,128]{3,2,1,0:T(8,128)(2,1)S(1)} %get-tuple-element.74) | copy-start | bytes 3145732
  180.6 1.2 copy-start.8
Sparse Core Ops, SparseCore 0:
  18.1 39.5 all-reduce.1
where the time goes:
time: 193 us; the launch traced here: 191 us
  blocking collectives  86.5 us (45%)
  waiting for transfers between devices  31.3 us (16%)
  matrix products  29.8 us (15%)
  local copies, waits for them, and re-layouts  17.7 us (9%)
  between operations  14.3 us (7%)
  loops' own time  5.99 us (3%)
  other arithmetic  5 us (3%)
    psum x1, waiting for transfers between devices, from_root(): return lax.psum(kept, axis)  31.3 us
    all_to_all x1, blocking collectives, local(): lax.all_to_all(sectioned, 'row', split_axis=0, concat_axis=3, tiled=True)  28.5 us
    all_to_all x1, blocking collectives, local(): lax.all_to_all(sectioned, 'row', split_axis=3, concat_axis=1, tiled=True)  27.9 us
    all_to_all x1, blocking collectives, local(): lax.all_to_all(lax.all_to_all(sectioned, 'row', split_axis=3, concat_axis...  15.9 us
    dot_general x8, matrix products, one_block(): jnp.dot(outer_average, outer_product_weight, preferred_element_type=jnp.f...  13.9 us
    all_gather x1, blocking collectives, local(): fragment = lax.all_gather(left_proj, 'col', axis=1, tiled=True)  7.28 us
    all_gather x1, blocking collectives, local(): right_rows = lax.all_gather(right_proj, 'col', axis=1, tiled=True)  6.91 us
    convert_element_type x8, local copies, waits for them, and re-layouts, one_block(): outer_average = (outer_average / alignment_depth).astype(jnp.bfloat16).re...  6.54 us
  transfers between devices with their start and end apart: 1, of which 1 were waited for; matrix products, arithmetic and copies ran while one was open for 1% of the time, Pallas kernels for 0%

commit v1 on v0

v1 whole, which is shorter than its diff:
```python
import functools

import jax
import jax.numpy as jnp
from jax import lax
from jax.experimental import pallas as pl
from jax.experimental.pallas import tpu as pltpu
from jax.sharding import PartitionSpec as P

EPSILON = 1e-05
F32 = jnp.float32
BF16 = jnp.bfloat16
NT = (((1,), (1,)), ((), ()))
TN = (((0,), (0,)), ((), ()))
VMEM_BYTES = 48 * 1024 * 1024


def iota(shape, dim):
    return lax.broadcasted_iota(jnp.int32, shape, dim)


def dot(a, b):
    return jnp.dot(a, b, preferred_element_type=F32)


def spread(rows, row_key, weight, columns, column_key, keep):
    left = (row_key(iota((rows, weight.shape[0]), 0)) == iota((rows, weight.shape[0]), 1)).astype(BF16)
    right = (column_key(iota((weight.shape[1], columns), 1)) == iota((weight.shape[1], columns), 0)).astype(BF16)
    full = dot(dot(left, weight).astype(BF16), right)
    at = iota((rows, columns), 0), iota((rows, columns), 1)
    return jnp.where(keep(*at), full, 0.0).astype(BF16)


def embed_kernel(state_ref, index_ref, table_ref, out_ref):
    depth, width = state_ref.shape
    tokens = index_ref.shape[1]
    kinds, features = table_ref.shape
    spread_tokens = (iota((tokens, tokens * kinds), 1) // kinds == iota((tokens, tokens * kinds), 0)).astype(BF16)
    wide = dot(index_ref[...].astype(F32).astype(BF16), spread_tokens)
    onehot = (wide == (iota(wide.shape, 1) % kinds).astype(F32)).astype(BF16)
    group = min(tokens, 256 // features)
    table = spread(
        group * kinds,
        lambda r: r % kinds,
        table_ref[...],
        group * features,
        lambda c: c % features,
        lambda r, c: r // kinds == c // features,
    )
    for start in range(0, tokens, group):
        at = slice(start * features, (start + group) * features)
        rows = dot(onehot[:, start * kinds : (start + group) * kinds], table)
        out_ref[:, at] = (state_ref[:, at].astype(F32) + rows).astype(BF16)


def weights_kernel(
    row_ref,
    kinds_ref,
    first_ref,
    second_ref,
    outer_ref,
    distance_ref,
    first_out,
    second_out,
    outer_out,
    distance_out,
    wide,
    rows,
):
    channels = outer_ref.shape[1]
    length = first_out.shape[0]
    side = wide.shape[0] // 32
    kinds = kinds_ref[...]
    onehot = (iota((first_ref.shape[0], kinds.shape[1]), 0) == kinds).astype(BF16)
    for which, (table, out) in enumerate(((first_ref, first_out), (second_ref, second_out))):
        rows[...] = lax.dot_general(onehot, table[...], TN, preferred_element_type=F32)
        out[...] = rows[pl.ds(pl.multiple_of(row_ref[which] * length, length), length), :]
    wide[...] = outer_ref[...].astype(F32)
    zero = jnp.zeros((side, channels), BF16)
    for e in range(32):
        part = wide[pl.ds(e, side, stride=32), :].astype(BF16)
        outer_out[pl.ds(2 * e * side, side), :] = jnp.concatenate([part, zero], axis=1)
        outer_out[pl.ds((2 * e + 1) * side, side), :] = jnp.concatenate([zero, part], axis=1)
    weight = distance_ref[...]
    none = jnp.zeros_like(weight)
    distance_out[...] = jnp.concatenate(
        [jnp.concatenate([weight, none], axis=1), jnp.concatenate([none, weight], axis=1)], axis=0
    )


def project_kernel(blocks, *refs):
    place_ref = refs[0]
    lefts, rights = refs[1 : 1 + blocks], refs[1 + blocks : 1 + 2 * blocks]
    first_ref, second_ref, left_out, right_out, left_all, right_all = refs[1 + 2 * blocks :]
    width = lefts[0].shape[1]
    depth = lefts[0].shape[0]
    features, c_width = first_ref.shape
    for which, (parts, whole) in enumerate(((lefts, left_all), (rights, right_all))):
        for k, part in enumerate(parts):
            block = lax.rem(place_ref[which] + k, blocks)
            whole[:, pl.ds(pl.multiple_of(block * width, width), width)] = part[...]
    tokens = blocks * width // features
    lanes = 2 * 2 * c_width
    weight = spread(
        8 * features,
        lambda r: r % features,
        first_ref[...],
        4 * lanes,
        lambda c: c % c_width,
        lambda r, c: r // features == 2 * (c // lanes) + c % (lanes // 2) // c_width,
    )
    half = iota((depth, 4 * lanes), 1) % lanes < lanes // 2
    for t in range(tokens // 8):
        both = dot(left_all[:, t * 8 * features : (t + 1) * 8 * features], weight)
        at = slice(t * 4 * lanes, (t + 1) * 4 * lanes)
        left_out[0:depth, at] = jnp.where(half, both, 0.0).astype(BF16)
        left_out[depth : 2 * depth, at] = jnp.where(half, 0.0, both).astype(BF16)
    e_width = second_ref.shape[1]
    turned = lax.dot_general(
        (iota((8 * e_width, e_width), 0) // 8 == iota((8 * e_width, e_width), 1)).astype(BF16),
        second_ref[...],
        NT,
        preferred_element_type=F32,
    ).astype(BF16)
    repeat = (iota((features, 8 * features), 1) % features == iota((features, 8 * features), 0)).astype(BF16)
    shape = (8 * e_width, 8 * features)
    weight = jnp.where(
        iota(shape, 0) % 8 == iota(shape, 1) // features, dot(turned, repeat), 0.0
    ).astype(BF16)
    low = iota((8, 2 * depth), 1) < depth
    for t in range(0, tokens // 8, 2):
        sides = []
        for u in (t, t + 1):
            part = right_all[:, u * 8 * features : (u + 1) * 8 * features]
            twice = jnp.concatenate([part, part], axis=0)
            sides.append(lax.dot_general(weight, twice, NT, preferred_element_type=F32))
        for g in range(e_width // 2):
            rows = [
                jnp.where(low, s[16 * g : 16 * g + 8], s[16 * g + 8 : 16 * g + 16]) for s in sides
            ]
            right_out[pl.ds(g * tokens + t * 8, 16), :] = jnp.concatenate(rows, axis=0).astype(BF16)


def pair_kernel(
    first_block,
    mask_ref,
    left_ref,
    right_ref,
    pair_ref,
    first_ref,
    second_ref,
    bias_ref,
    gain_ref,
    outer_ref,
    gate_up_ref,
    down_ref,
    distance_ref,
    *rest,
):
    pair_out, dist_out, outer, start = rest[-4:]
    rows, length, channels = pair_ref.shape
    pairs = rows // 2
    depth = right_ref.shape[1] // 2
    lanes = right_ref.shape[1]
    groups = right_ref.shape[0] // length
    hid = down_ref.shape[0]
    block = pl.program_id(0) + first_block
    for p in range(0, pairs, 2):
        weight = left_ref[:, p * lanes : (p + 2) * lanes]
        for g in range(0, groups, 4):
            got = dot(right_ref[g * length : (g + 4) * length, :], weight).astype(BF16)
            for q in range(2):
                for h in range(4):
                    outer[(p + q) * length : (p + q + 1) * length, (g + h) * lanes : (g + h + 1) * lanes] = got[
                        h * length : (h + 1) * length, q * lanes : (q + 1) * lanes
                    ]
    update = dot(outer[...], outer_ref[...])
    mask_columns = mask_ref.shape[1]
    mask = jnp.concatenate(
        [
            jnp.full((length // mask_columns, channels), mask_ref[block, m].astype(F32), F32)
            for m in range(mask_columns)
        ],
        axis=0,
    )
    bias = second_ref[...] + mask * bias_ref[...].astype(F32)
    mask = mask * (1.0 / depth)
    normed = []
    for p in range(pairs):
        for q in range(2):
            i = 2 * p + q
            value = (
                pair_ref[i].astype(F32)
                + (first_ref[i : i + 1, :] + bias)
                + mask * update[p * length : (p + 1) * length, q * channels : (q + 1) * channels]
            )
            start[q, p * length : (p + 1) * length, :] = value
    for q in range(2):
        value = start[q]
        mean = jnp.mean(value, axis=-1, keepdims=True)
        centered = value - mean
        variance = jnp.mean(centered * centered, axis=-1, keepdims=True)
        normed = (centered * lax.rsqrt(variance + EPSILON) * gain_ref[...]).astype(BF16)
        for n in range(0, hid, 256):
            gate = dot(normed, gate_up_ref[:, n : n + 256])
            up = dot(normed, gate_up_ref[:, hid + n : hid + n + 256])
            hidden = (0.5 * gate * (1.0 + jnp.tanh(0.5 * gate)) * up).astype(BF16)
            value = value + dot(hidden, down_ref[n : n + 256, :])
        start[q] = value
    result = [start[q].astype(BF16) for q in range(2)]
    for p in range(pairs):
        for q in range(2):
            pair_out[2 * p + q] = result[q][p * length : (p + 1) * length]
    dist = dot(jnp.concatenate(result, axis=1), distance_ref[...]).astype(BF16)
    width = dist.shape[1]
    for p in range(pairs):
        dist_out[:, p * width : (p + 1) * width] = dist[p * length : (p + 1) * length]


def final_kernel(own_ref, mirror_ref, bias_ref, out_ref):
    out_ref[...] = (own_ref[...].astype(F32) + mirror_ref[...].astype(F32) + bias_ref[...]).astype(BF16)


def params():
    return pltpu.CompilerParams(vmem_limit_bytes=VMEM_BYTES)


VMEM = pl.BlockSpec(memory_space=pltpu.VMEM)
SMEM = pl.BlockSpec(memory_space=pltpu.SMEM)


def local(
    row_count,
    col_count,
    pair_state,
    token_kinds,
    first_type_table,
    second_type_table,
    alignment_state,
    alignment_index,
    alignment_table,
    first_weight,
    second_weight,
    outer_product_weight,
    outer_product_bias,
    pair_block_mask,
    transition_gain,
    transition_gate_up,
    transition_down,
    distance_weight,
    distance_bias,
):
    length = pair_state.shape[0]
    channels = pair_state.shape[2]
    depth = alignment_index.shape[0]
    c_width, e_width = first_weight.shape[1], second_weight.shape[1]
    bins = distance_weight.shape[1]
    axes = ("row", "col")
    place = jnp.stack([lax.axis_index("col"), lax.axis_index("row")]).astype(jnp.int32)

    embedded = pl.pallas_call(
        embed_kernel,
        out_shape=jax.ShapeDtypeStruct(alignment_state.shape, BF16),
        in_specs=[VMEM] * 3,
        out_specs=VMEM,
        compiler_params=params(),
        name="embed",
    )(alignment_state, alignment_index, alignment_table)

    def moved(value, target):
        pairs = [
            (r * col_count + c, target(r, c)[0] * col_count + target(r, c)[1])
            for r in range(row_count)
            for c in range(col_count)
        ]
        return lax.ppermute(value, axes, pairs)

    rights = [
        moved(embedded, lambda r, c, k=k: ((c - k) % row_count, r)) for k in range(col_count)
    ]
    lefts = [embedded] + [
        moved(embedded, lambda r, c, k=k: (r, (c - k) % col_count)) for k in range(1, col_count)
    ]

    first_rows, second_rows, outer_weight, pair_distance = pl.pallas_call(
        weights_kernel,
        out_shape=(
            jax.ShapeDtypeStruct((length, channels), F32),
            jax.ShapeDtypeStruct((length, channels), F32),
            jax.ShapeDtypeStruct((2 * c_width * e_width, 2 * channels), BF16),
            jax.ShapeDtypeStruct((2 * channels, 2 * bins), BF16),
        ),
        in_specs=[SMEM] + [VMEM] * 5,
        out_specs=(VMEM,) * 4,
        scratch_shapes=[
            pltpu.VMEM(outer_product_weight.shape, F32),
            pltpu.VMEM((token_kinds.shape[0], channels), F32),
        ],
        compiler_params=params(),
        name="weights",
    )(
        place[::-1],
        token_kinds.reshape(1, -1),
        first_type_table,
        second_type_table,
        outer_product_weight,
        distance_weight,
    )

    left_tiles, right_tiles = pl.pallas_call(
        functools.partial(project_kernel, col_count),
        out_shape=(
            jax.ShapeDtypeStruct((2 * depth, 2 * length * c_width), BF16),
            jax.ShapeDtypeStruct((e_width // 2 * length, 2 * depth), BF16),
        ),
        in_specs=[SMEM] + [VMEM] * (2 * col_count + 2),
        out_specs=(VMEM,) * 2,
        scratch_shapes=[pltpu.VMEM((depth, col_count * alignment_state.shape[1]), BF16)] * 2,
        compiler_params=params(),
        name="project",
    )(place, *lefts, *rights, first_weight, second_weight)

    blocks = pair_block_mask.shape[0]
    rows = length // blocks
    fixed = lambda shape: pl.BlockSpec(shape, lambda b: (0,) * len(shape))
    pair_out, dist = pl.pallas_call(
        functools.partial(pair_kernel, 0),
        grid=(blocks,),
        out_shape=(
            jax.ShapeDtypeStruct(pair_state.shape, BF16),
            jax.ShapeDtypeStruct((length, length * bins), BF16),
        ),
        in_specs=[
            SMEM,
            pl.BlockSpec((2 * depth, 2 * rows * c_width), lambda b: (0, b)),
            fixed(right_tiles.shape),
            pl.BlockSpec((rows, length, channels), lambda b: (b, 0, 0)),
            pl.BlockSpec((rows, channels), lambda b: (b, 0)),
            fixed(second_rows.shape),
            fixed((1, channels)),
            fixed((1, channels)),
            fixed(outer_weight.shape),
            fixed(transition_gate_up.shape),
            fixed(transition_down.shape),
            fixed(pair_distance.shape),
        ],
        out_specs=(
            pl.BlockSpec((rows, length, channels), lambda b: (b, 0, 0)),
            pl.BlockSpec((length, rows * bins), lambda b: (0, b)),
        ),
        scratch_shapes=[
            pltpu.VMEM((rows // 2 * length, 2 * c_width * e_width), BF16),
            pltpu.VMEM((2, rows // 2 * length, channels), F32),
        ],
        compiler_params=params(),
        name="pairs",
    )(
        pair_block_mask,
        left_tiles,
        right_tiles,
        pair_state,
        first_rows,
        second_rows,
        outer_product_bias.reshape(1, -1),
        transition_gain.reshape(1, -1),
        outer_weight,
        transition_gate_up,
        transition_down,
        pair_distance,
    )
    mirror = moved(dist, lambda r, c: (c, r))
    own = dist.reshape(length, length, bins).transpose(1, 0, 2).reshape(length, length * bins)
    distogram = pl.pallas_call(
        final_kernel,
        out_shape=jax.ShapeDtypeStruct((length, length * bins), BF16),
        in_specs=[VMEM] * 3,
        out_specs=VMEM,
        compiler_params=params(),
        name="final",
    )(own, mirror, jnp.tile(distance_bias, length).reshape(1, -1))
    return pair_out, distogram


def solution(mesh):
    split = P(("conf", "row"), "col")
    tokens = P(None, ("conf", "row", "col"))
    in_specs = (
        P(("conf", "row"), "col", None),
        P("conf"),
        P(),
        P(),
        tokens,
        tokens,
        P(),
        P(),
        P(),
        P(),
        P(),
        split,
        P(),
        P(),
        P(),
        P(),
        P(),
    )
    return jax.shard_map(
        functools.partial(local, mesh.shape["row"], mesh.shape["col"]),
        mesh=mesh,
        in_specs=in_specs,
        out_specs=(P(("conf", "row"), "col", None), split),
        check_vma=False,
    )
```

time: 193 us -> 70.7 us (0.37)
  blocking collectives: 86.5 us -> 0 us
  matrix products: 29.8 us -> 0 us
  Pallas kernels: 0 us -> 20.1 us
  between operations: 14.3 us -> 0.79 us
  starting transfers between devices: 0.04 us -> 11.8 us
  waiting for transfers between devices: 31.3 us -> 22 us
  loops' own time: 5.99 us -> 0 us
  other arithmetic: 5 us -> 0.07 us
  local copies, waits for them, and re-layouts: 17.7 us -> 15.2 us
    all_to_all x3 -> x0, blocking collectives: 72.3 us -> none  [the longest x1 28.5 us: local(): lax.all_to_all(sectioned, 'row', split_axis=0, concat_axis=3, tiled=True)]
    psum x1 -> x0, waiting for transfers between devices: 31.3 us -> none  [from_root(): return lax.psum(kept, axis)]
    dot_general x39 -> x0, matrix products: 29.8 us -> none  [the longest x8 13.9 us: one_block(): jnp.dot(outer_average, outer_product_weight, preferred_element_type=jnp.f...]
    ppermute x0 -> x8, waiting for transfers between devices: none -> 22 us  [moved(): return lax.ppermute(value, axes, pairs)]
    pallas_call x0 -> x5, Pallas kernels: none -> 20.1 us  [the longest x1 15.7 us: local(): pl.pallas_call(functools.partial(pair_kernel, 0), grid=(blocks,), out_sha...]
    all_gather x2 -> x0, blocking collectives: 14.2 us -> none  [the longest x1 7.28 us: local(): fragment = lax.all_gather(left_proj, 'col', axis=1, tiled=True)]
    ppermute x0 -> x8, starting transfers between devices: none -> 11.8 us  [moved(): return lax.ppermute(value, axes, pairs)]
    unnamed x26 -> x32, local copies, waits for them, and re-layouts: 0.08 us -> 10.2 us
  transfers between devices with their start and end apart: 1 -> 8, of which waited for: 1 -> 3; matrix products, arithmetic and copies ran while one was open for 1% -> 8% of each run, Pallas kernels for 0% -> 1%
where the time goes in v1:
time: 70.7 us; the launch traced here: 70 us
  waiting for transfers between devices  22 us (31%)
  Pallas kernels  20.1 us (28%)
  local copies, waits for them, and re-layouts  15.2 us (21%)
  starting transfers between devices  11.8 us (17%)
  between operations  0.79 us (1%)
    ppermute x8, waiting for transfers between devices, moved(): return lax.ppermute(value, axes, pairs)  22 us
    pallas_call x1, Pallas kernels, local(): pl.pallas_call(functools.partial(pair_kernel, 0), grid=(blocks,), out_sha...  15.7 us
    ppermute x8, starting transfers between devices, moved(): return lax.ppermute(value, axes, pairs)  11.8 us
    unnamed x32, local copies, waits for them, and re-layouts  10.2 us
    reshape x3, local copies, waits for them, and re-layouts, local(): dist.reshape(length, length, bins).transpose(1, 0, 2)  4.83 us
    pallas_call x1, Pallas kernels, local(): pl.pallas_call(functools.partial(project_kernel, col_count), out_shape=(j...  1.86 us
  transfers between devices with their start and end apart: 8, of which 3 were waited for; matrix products, arithmetic and copies ran while one was open for 8% of the time, Pallas kernels for 1%

profile of v1, /device:TPU:2, one launch (start us, length us, event | category | flops | bytes accessed | tf_op | source)
XLA Modules:
  0.0 70.0 jit_solution(12766832042506622242)
XLA Ops:
  0.6 0.9 %copy.19.index_ref = s32[64,16]{1,0:T(8,128)S(1)} copy(s32[64,16]{0,1:T(8,128)} %param.22) | data formatting | bytes 8192 | tf_op args[5]
  1.5 0.8 %copy-done.4 = bf16[64,512]{1,0:T(8,128)(2,1)S(1)} copy-done((bf16[64,512]{1,0:T(8,128)(2,1)S(1)}, bf16[64,512]{1,0:T(8,128)(2,1)}, u32[]{:S(2)}) %copy-start.4) | copy-done | bytes 65560
  2.4 0.7 copy-done.9
  3.6 1.5 %collective-permute-start.1 = (bf16[64,512]{1,0:T(8,128)(2,1)S(1)}, bf16[64,512]{1,0:T(8,128)(2,1)S(1)}, u32[]{:S(2)}, u32[]{:S(2)}) collective-permute-start(bf16[64,512]{1,0:T(8,128)(2,1)S(1)} %embed.1.refs_1_), channel_id=1, source_target_pairs={{0,2},{1,3},{2,0},{3,1},{4,6},{5,7},{6,4},{7,5},{8,10},{9,11},{10,... | collective-permute-start | bytes 196616 | tf_op jit(solution)/shard_map/ppermute | solution.py:276
  5.1 4.7 %collective-permute-start.3 = (bf16[64,512]{1,0:T(8,128)(2,1)S(1)}, bf16[64,512]{1,0:T(8,128)(2,1)S(1)}, u32[]{:S(2)}, u32[]{:S(2)}) collective-permute-start(bf16[64,512]{1,0:T(8,128)(2,1)S(1)} %embed.1.refs_1_), channel_id=1, source_target_pairs={{0,0},{1,4},{2,8},{3,12},{4,1},{5,5},{6,9},{7,13},{8,2},{9,6},{10,... | collective-permute-start | bytes 196616 | tf_op jit(solution)/shard_map/ppermute | solution.py:276
  10.2 2.4 %collective-permute-start.5 = (bf16[64,512]{1,0:T(8,128)(2,1)S(1)}, bf16[64,512]{1,0:T(8,128)(2,1)S(1)}, u32[]{:S(2)}, u32[]{:S(2)}) collective-permute-start(bf16[64,512]{1,0:T(8,128)(2,1)S(1)} %embed.1.refs_1_), channel_id=1, source_target_pairs={{0,8},{1,12},{2,0},{3,4},{4,9},{5,13},{6,1},{7,5},{8,10},{9,14},{1... | collective-permute-start | bytes 196616 | tf_op jit(solution)/shard_map/ppermute | solution.py:276
  12.7 0.7 collective-permute-start.6
  13.5 0.8 %copy.20.distance_ref = bf16[128,64]{1,0:T(8,128)(2,1)S(1)} copy(bf16[128,64]{0,1:T(8,128)(2,1)} %param.32) | data formatting | bytes 32768 | tf_op args[15]
  14.4 0.9 %copy-done.2 = bf16[1024,128]{1,0:T(8,128)(2,1)S(1)} copy-done((bf16[1024,128]{1,0:T(8,128)(2,1)S(1)}, bf16[1024,128]{1,0:T(8,128)(2,1)}, u32[]{:S(2)}) %copy-start.2) | copy-done | bytes 262168
  15.3 0.7 copy-done.7
  16.0 0.7 copy-done.8
  17.4 1.0 %weights.1 = (f32[64,128]{1,0:T(8,128)S(1)}, f32[64,128]{1,0:T(8,128)S(1)}, bf16[2048,256]{1,0:T(8,128)(2,1)S(1)}, bf16[256,128]{1,0:T(8,128)(2,1)S(1)}) custom-call(s32[2]{0:T(128)S(1)} %rev.3.row_ref, s32[1,256]{1,0:T(1,128)S(1)} %bitcast.8, bf16[32,128]{1,0:T(8,128)(2,1)S(1)} %copy-done.7, bf16[32,128]{1,0:T(8,128)(2,1)S(1)} %copy-done.8, ...), custom_call_target="tpu_custom_call" | custom-call | tf_op jit(solution)/shard_map/weights/pallas_call | solution.py:285
  19.5 0.7 copy-done.5
  20.2 0.7 copy-done.6
  20.9 1.9 %project.1 = (bf16[128,4096]{1,0:T(8,128)(2,1)S(1)}, bf16[1024,128]{1,0:T(8,128)(2,1)S(1)}) custom-call(s32[2]{0:T(128)S(1)} %pad_add_fusion.refs_0_, bf16[64,512]{1,0:T(8,128)(2,1)S(1)} %embed.1.refs_1_, bf16[64,512]{1,0:T(8,128)(2,1)S(1)} %collective-permute-done.refs_2_, bf16[64,512]{1,0:T(8,128)(2,1)S(1)} %collective-permute-done.1.refs_3_, ...), custom_call_target="tpu_custom_call" | custom-call | tf_op jit(solution)/shard_map/project/pallas_call | solution.py:310
  23.4 0.9 %copy-done.1 = bf16[128,1024]{1,0:T(8,128)(2,1)S(1)} copy-done((bf16[128,1024]{1,0:T(8,128)(2,1)S(1)}, bf16[128,1024]{1,0:T(8,128)(2,1)}, u32[]{:S(2)}) %copy-start.1) | copy-done | bytes 262168
  24.4 0.9 %copy-done.3 = bf16[512,128]{1,0:T(8,128)(2,1)S(1)} copy-done((bf16[512,128]{1,0:T(8,128)(2,1)S(1)}, bf16[512,128]{1,0:T(8,128)(2,1)}, u32[]{:S(2)}) %copy-start.3) | copy-done | bytes 131096
  25.3 15.7 %pairs.1 = (bf16[64,64,128]{2,1,0:T(8,128)(2,1)}, bf16[64,4096]{1,0:T(8,128)(2,1)S(1)}) custom-call(s32[4,4]{1,0:T(4,128)S(1)} %copy-done.10, bf16[128,4096]{1,0:T(8,128)(2,1)S(1)} %get-tuple-element.10.left_ref, bf16[1024,128]{1,0:T(8,128)(2,1)S(1)} %get-tuple-element.11.right_ref, bf16[64,64,128]{2,1,0:T(8,128)(2,1)S(1)} %copy-done, ...), custom_call_target="tpu_custom_call" | custom-call | tf_op jit(solution)/shard_map/pairs/pallas_call | solution.py:326
  41.0 2.0 %collective-permute-start.7 = (bf16[64,4096]{1,0:T(8,128)(2,1)S(1)}, bf16[64,4096]{1,0:T(8,128)(2,1)S(1)}, u32[]{:S(2)}, u32[]{:S(2)}) collective-permute-start(bf16[64,4096]{1,0:T(8,128)(2,1)S(1)} %get-tuple-element.17), channel_id=1, source_target_pairs={{0,0},{1,4},{2,8},{3,12},{4,1},{5,5},{6,9},{7,13},{8,2},{9,6},{10,... | collective-permute-start | bytes 1572872 | tf_op jit(solution)/shard_map/ppermute | solution.py:276
  43.2 2.1 %reshape.23 = bf16[64,64,64]{2,1,0:T(8,128)(2,1)} reshape(bf16[64,4096]{1,0:T(8,128)(2,1)S(1)} %get-tuple-element.17) | data formatting | bytes 1048576 | tf_op jit(solution)/shard_map/reshape | solution.py:372
  45.3 1.9 %copy.23 = bf16[64,64,64]{2,0,1:T(8,128)(2,1)S(1)} copy(bf16[64,64,64]{2,1,0:T(8,128)(2,1)} %reshape.23) | data formatting | bytes 1048576 | tf_op jit(solution)/shard_map/reshape | solution.py:372
  47.2 0.8 %reshape.24.own_ref = bf16[64,4096]{1,0:T(8,128)(2,1)S(1)} reshape(bf16[64,64,64]{2,1,0:T(8,128)(2,1)S(1)} %bitcast.11) | data formatting | bytes 1048576 | tf_op jit(solution)/shard_map/reshape | solution.py:372
  48.0 21.0 %collective-permute-done.7.mirror_ref = bf16[64,4096]{1,0:T(8,128)(2,1)S(1)} collective-permute-done((bf16[64,4096]{1,0:T(8,128)(2,1)S(1)}, bf16[64,4096]{1,0:T(8,128)(2,1)S(1)}, u32[]{:S(2)}, u32[]{:S(2)}) %collective-permute-start.7) | collective-permute-done | bytes 524320 | tf_op jit(solution)/shard_map/ppermute | solution.py:276
  69.0 0.9 %final.1 = bf16[64,4096]{1,0:T(8,128)(2,1)} custom-call(bf16[64,4096]{1,0:T(8,128)(2,1)S(1)} %reshape.24.own_ref, bf16[64,4096]{1,0:T(8,128)(2,1)S(1)} %collective-permute-done.7.mirror_ref, f32[1,4096]{1,0:T(1,128)S(1)} %reshape_tile.3.bias_ref), custom_call_target="tpu_custom_call" | custom-call | tf_op jit(solution)/shard_map/final/pallas_call | solution.py:373
  (36 shorter events, 3.7 us)
Async XLA Ops:
  0.6 22.2 %copy-start = (bf16[64,64,128]{2,1,0:T(8,128)(2,1)S(1)}, bf16[64,64,128]{2,1,0:T(8,128)(2,1)}, u32[]{:S(2)}) copy-start(bf16[64,64,128]{2,1,0:T(8,128)(2,1)} %pair_ref.1) | copy-start | bytes 3145732
  1.5 0.8 %copy-start.4 = (bf16[64,512]{1,0:T(8,128)(2,1)S(1)}, bf16[64,512]{1,0:T(8,128)(2,1)}, u32[]{:S(2)}) copy-start(bf16[64,512]{1,0:T(8,128)(2,1)} %state_ref.1) | copy-start | bytes 196612
  2.3 0.7 copy-start.9
  3.5 6.7 %collective-permute-start = (bf16[64,512]{1,0:T(8,128)(2,1)S(1)}, bf16[64,512]{1,0:T(8,128)(2,1)S(1)}, u32[]{:S(2)}, u32[]{:S(2)}) collective-permute-start(bf16[64,512]{1,0:T(8,128)(2,1)S(1)} %embed.1.refs_1_), channel_id=1, source_target_pairs={{0,3},{1,0},{2,1},{3,2},{4,7},{5,4},{6,5},{7,6},{8,11},{9,8},{10,9... | collective-permute-start | bytes 196616 | tf_op jit(solution)/shard_map/ppermute | solution.py:276
  3.6 9.1 %collective-permute-start.1 = (bf16[64,512]{1,0:T(8,128)(2,1)S(1)}, bf16[64,512]{1,0:T(8,128)(2,1)S(1)}, u32[]{:S(2)}, u32[]{:S(2)}) collective-permute-start(bf16[64,512]{1,0:T(8,128)(2,1)S(1)} %embed.1.refs_1_), channel_id=1, source_target_pairs={{0,2},{1,3},{2,0},{3,1},{4,6},{5,7},{6,4},{7,5},{8,10},{9,11},{10,... | collective-permute-start | bytes 196616 | tf_op jit(solution)/shard_map/ppermute | solution.py:276
  5.1 13.4 %collective-permute-start.2 = (bf16[64,512]{1,0:T(8,128)(2,1)S(1)}, bf16[64,512]{1,0:T(8,128)(2,1)S(1)}, u32[]{:S(2)}, u32[]{:S(2)}) collective-permute-start(bf16[64,512]{1,0:T(8,128)(2,1)S(1)} %embed.1.refs_1_), channel_id=1, source_target_pairs={{0,1},{1,2},{2,3},{3,0},{4,5},{5,6},{6,7},{7,4},{8,9},{9,10},{10,1... | collective-permute-start | bytes 196616 | tf_op jit(solution)/shard_map/ppermute | solution.py:276
  5.1 13.4 %collective-permute-start.3 = (bf16[64,512]{1,0:T(8,128)(2,1)S(1)}, bf16[64,512]{1,0:T(8,128)(2,1)S(1)}, u32[]{:S(2)}, u32[]{:S(2)}) collective-permute-start(bf16[64,512]{1,0:T(8,128)(2,1)S(1)} %embed.1.refs_1_), channel_id=1, source_target_pairs={{0,0},{1,4},{2,8},{3,12},{4,1},{5,5},{6,9},{7,13},{8,2},{9,6},{10,... | collective-permute-start | bytes 196616 | tf_op jit(solution)/shard_map/ppermute | solution.py:276
  9.8 8.6 %collective-permute-start.4 = (bf16[64,512]{1,0:T(8,128)(2,1)S(1)}, bf16[64,512]{1,0:T(8,128)(2,1)S(1)}, u32[]{:S(2)}, u32[]{:S(2)}) collective-permute-start(bf16[64,512]{1,0:T(8,128)(2,1)S(1)} %embed.1.refs_1_), channel_id=1, source_target_pairs={{0,12},{1,0},{2,4},{3,8},{4,13},{5,1},{6,5},{7,9},{8,14},{9,2},{10... | collective-permute-start | bytes 196616 | tf_op jit(solution)/shard_map/ppermute | solution.py:276
  10.2 8.8 %collective-permute-start.5 = (bf16[64,512]{1,0:T(8,128)(2,1)S(1)}, bf16[64,512]{1,0:T(8,128)(2,1)S(1)}, u32[]{:S(2)}, u32[]{:S(2)}) collective-permute-start(bf16[64,512]{1,0:T(8,128)(2,1)S(1)} %embed.1.refs_1_), channel_id=1, source_target_pairs={{0,8},{1,12},{2,0},{3,4},{4,9},{5,13},{6,1},{7,5},{8,10},{9,14},{1... | collective-permute-start | bytes 196616 | tf_op jit(solution)/shard_map/ppermute | solution.py:276
  12.7 6.8 %collective-permute-start.6 = (bf16[64,512]{1,0:T(8,128)(2,1)S(1)}, bf16[64,512]{1,0:T(8,128)(2,1)S(1)}, u32[]{:S(2)}, u32[]{:S(2)}) collective-permute-start(bf16[64,512]{1,0:T(8,128)(2,1)S(1)} %embed.1.refs_1_), channel_id=1, source_target_pairs={{0,4},{1,8},{2,12},{3,0},{4,5},{5,9},{6,13},{7,1},{8,6},{9,10},{10... | collective-permute-start | bytes 196616 | tf_op jit(solution)/shard_map/ppermute | solution.py:276
  14.4 1.0 %copy-start.2 = (bf16[1024,128]{1,0:T(8,128)(2,1)S(1)}, bf16[1024,128]{1,0:T(8,128)(2,1)}, u32[]{:S(2)}) copy-start(bf16[1024,128]{1,0:T(8,128)(2,1)} %outer_ref.1) | copy-start | bytes 786436
  15.3 0.7 copy-start.7
  16.0 0.7 copy-start.8
  16.7 0.7 copy-start.11
  19.5 0.7 copy-start.5
  20.2 0.7 copy-start.6
  22.8 0.7 copy-start.10
  22.8 0.7 copy-start.12
  22.8 0.7 copy-start.13
  23.4 1.0 %copy-start.1 = (bf16[128,1024]{1,0:T(8,128)(2,1)S(1)}, bf16[128,1024]{1,0:T(8,128)(2,1)}, u32[]{:S(2)}) copy-start(bf16[128,1024]{1,0:T(8,128)(2,1)} %gate_up_ref.1) | copy-start | bytes 786436
  24.4 0.9 %copy-start.3 = (bf16[512,128]{1,0:T(8,128)(2,1)S(1)}, bf16[512,128]{1,0:T(8,128)(2,1)}, u32[]{:S(2)}) copy-start(bf16[512,128]{1,0:T(8,128)(2,1)} %down_ref.1) | copy-start | bytes 393220
  41.0 2.1 %copy-start.14 = (f32[64]{0:T(128)S(1)}, f32[64]{0:T(128)}, u32[]{:S(2)}) copy-start(f32[64]{0:T(128)} %param.33) | copy-start | bytes 772
  41.0 28.0 %collective-permute-start.7 = (bf16[64,4096]{1,0:T(8,128)(2,1)S(1)}, bf16[64,4096]{1,0:T(8,128)(2,1)S(1)}, u32[]{:S(2)}, u32[]{:S(2)}) collective-permute-start(bf16[64,4096]{1,0:T(8,128)(2,1)S(1)} %get-tuple-element.17), channel_id=1, source_target_pairs={{0,0},{1,4},{2,8},{3,12},{4,1},{5,5},{6,9},{7,13},{8,2},{9,6},{10,... | collective-permute-start | bytes 1572872 | tf_op jit(solution)/shard_map/ppermute | solution.py:276

commit v2 on v1

v2 whole, which is shorter than its diff:
```python
import functools

import jax
import jax.numpy as jnp
from jax import lax
from jax.experimental import pallas as pl
from jax.experimental.pallas import tpu as pltpu
from jax.sharding import PartitionSpec as P

EPSILON = 1e-05
F32 = jnp.float32
BF16 = jnp.bfloat16
NT = (((1,), (1,)), ((), ()))
TN = (((0,), (0,)), ((), ()))
MIB = 1024 * 1024


def iota(shape, dim):
    return lax.broadcasted_iota(jnp.int32, shape, dim)


def dot(a, b):
    return jnp.dot(a, b, preferred_element_type=F32)


def spread(rows, row_key, weight, columns, column_key, keep):
    left = (row_key(iota((rows, weight.shape[0]), 0)) == iota((rows, weight.shape[0]), 1)).astype(BF16)
    right = (column_key(iota((weight.shape[1], columns), 1)) == iota((weight.shape[1], columns), 0)).astype(BF16)
    full = dot(dot(left, weight).astype(BF16), right)
    at = iota((rows, columns), 0), iota((rows, columns), 1)
    return jnp.where(keep(*at), full, 0.0).astype(BF16)


def fetch(sources, targets, sems):
    copies = [pltpu.make_async_copy(s, t, sems.at[n]) for n, (s, t) in enumerate(zip(sources, targets, strict=True))]
    for copy in copies:
        copy.start()
    return copies


def embed_kernel(state_hbm, index_hbm, table_hbm, out_ref, state_ref, index_ref, table_ref, sems):
    copies = fetch((index_hbm, table_hbm, state_hbm), (index_ref, table_ref, state_ref), sems)
    tokens = index_ref.shape[0]
    kinds, features = table_ref.shape
    group = min(tokens, 256 // features)
    copies[1].wait()
    table = spread(
        group * kinds,
        lambda r: r % kinds,
        table_ref[...],
        group * features,
        lambda c: c % features,
        lambda r, c: r // kinds == c // features,
    )
    spread_tokens = (iota((tokens, tokens * kinds), 1) // kinds == iota((tokens, tokens * kinds), 0)).astype(BF16)
    copies[0].wait()
    wide = lax.dot_general(
        index_ref[...].astype(F32).astype(BF16), spread_tokens, TN, preferred_element_type=F32
    )
    onehot = (wide == (iota(wide.shape, 1) % kinds).astype(F32)).astype(BF16)
    copies[2].wait()
    for start in range(0, tokens, group):
        at = slice(start * features, (start + group) * features)
        rows = dot(onehot[:, start * kinds : (start + group) * kinds], table)
        out_ref[:, at] = (state_ref[:, at].astype(F32) + rows).astype(BF16)


def weights_kernel(
    place_ref,
    kinds_hbm,
    first_hbm,
    second_hbm,
    outer_hbm,
    bias_hbm,
    mask_hbm,
    pair_hbm,
    gate_up_hbm,
    down_hbm,
    left_hbm,
    right_hbm,
    gain_hbm,
    distance_hbm,
    last_hbm,
    first_out,
    mask_out,
    base_out,
    outer_out,
    pair_out,
    gate_up_out,
    down_out,
    gain_out,
    left_out,
    right_out,
    distance_out,
    last_out,
    kinds_ref,
    first_ref,
    second_ref,
    outer_ref,
    bias_ref,
    mask_ref,
    left_ref,
    right_ref,
    distance_ref,
    last_ref,
    wide,
    rows,
    sems,
):
    copies = fetch(
        (left_hbm, right_hbm, kinds_hbm, first_hbm, second_hbm, bias_hbm, mask_hbm, distance_hbm, last_hbm)
        + (outer_hbm, pair_hbm, gate_up_hbm, down_hbm, gain_hbm),
        (left_ref, right_ref, kinds_ref, first_ref, second_ref, bias_ref, mask_ref, distance_ref, last_ref)
        + (outer_ref, pair_out, gate_up_out, down_out, gain_out),
        sems,
    )
    channels = outer_ref.shape[1]
    length = first_out.shape[0]
    side = left_hbm.shape[1]
    steps = outer_ref.shape[0] // side
    for copy in copies[:9]:
        copy.wait()
    features, c_width = left_ref.shape
    lanes = 4 * c_width
    left_out[...] = spread(
        8 * features,
        lambda r: r % features,
        left_ref[...],
        4 * lanes,
        lambda c: c % c_width,
        lambda r, c: r // features == 2 * (c // lanes) + c % (lanes // 2) // c_width,
    )
    e_width = right_ref.shape[1]
    turned = lax.dot_general(
        (iota((8 * e_width, e_width), 0) // 8 == iota((8 * e_width, e_width), 1)).astype(BF16),
        right_ref[...],
        NT,
        preferred_element_type=F32,
    ).astype(BF16)
    repeat = (iota((features, 8 * features), 1) % features == iota((features, 8 * features), 0)).astype(BF16)
    shape = right_out.shape
    right_out[...] = jnp.where(
        iota(shape, 0) % 8 == iota(shape, 1) // features, dot(turned, repeat), 0.0
    ).astype(BF16)
    weight = distance_ref[...]
    none = jnp.zeros_like(weight)
    distance_out[...] = jnp.concatenate(
        [jnp.concatenate([weight, none], axis=1), jnp.concatenate([none, weight], axis=1)], axis=0
    )
    last_out[...] = jnp.concatenate([last_ref[...], last_ref[...]], axis=1)
    kinds = kinds_ref[...]
    onehot = (iota((first_ref.shape[0], kinds.shape[1]), 0) == kinds).astype(BF16)
    rows[...] = lax.dot_general(onehot, first_ref[...], TN, preferred_element_type=F32)
    first_out[...] = rows[pl.ds(pl.multiple_of(place_ref[1] * length, length), length), :]
    rows[...] = lax.dot_general(onehot, second_ref[...], TN, preferred_element_type=F32)
    second = rows[pl.ds(pl.multiple_of(place_ref[0] * length, length), length), :]
    blocks, columns = mask_ref.shape
    reach = (iota((length, columns), 0) // (length // columns) == iota((length, columns), 1)).astype(BF16)
    mask = lax.dot_general(
        reach, mask_ref[...].astype(F32).astype(BF16), NT, preferred_element_type=F32
    )
    bias = bias_ref[...].astype(F32)
    for b in range(blocks):
        part = jnp.broadcast_to(mask[:, b : b + 1], (length, channels))
        mask_out[b] = part
        base_out[b] = second + part * bias
    copies[9].wait()
    wide[...] = outer_ref[...].astype(F32)
    zero = jnp.zeros((side, channels), BF16)
    for e in range(steps):
        part = wide[pl.ds(e, side, stride=steps), :].astype(BF16)
        outer_out[pl.ds(2 * e * side, side), :] = jnp.concatenate([part, zero], axis=1)
        outer_out[pl.ds((2 * e + 1) * side, side), :] = jnp.concatenate([zero, part], axis=1)
    for copy in copies[10:]:
        copy.wait()


def project_kernel(blocks, features, *refs):
    place_ref = refs[0]
    lefts, rights = refs[1 : 1 + blocks], refs[1 + blocks : 1 + 2 * blocks]
    first_ref, second_ref, left_out, right_out, left_all, right_all = refs[1 + 2 * blocks :]
    depth, width = lefts[0].shape
    for which, (parts, whole) in enumerate(((lefts, left_all), (rights, right_all))):
        for k, part in enumerate(parts):
            block = lax.rem(place_ref[which] + k, blocks)
            whole[:, pl.ds(pl.multiple_of(block * width, width), width)] = part[...]
    tokens = blocks * width // features
    group, columns = first_ref.shape
    half = iota((depth, columns), 1) % (columns // 4) < columns // 8
    for t in range(tokens // 8):
        both = dot(left_all[:, t * group : (t + 1) * group], first_ref[...])
        at = slice(t * columns, (t + 1) * columns)
        left_out[0:depth, at] = jnp.where(half, both, 0.0).astype(BF16)
        left_out[depth : 2 * depth, at] = jnp.where(half, 0.0, both).astype(BF16)
    low = iota((8, 2 * depth), 1) < depth
    for t in range(0, tokens // 8, 2):
        sides = []
        for u in (t, t + 1):
            part = right_all[:, u * group : (u + 1) * group]
            twice = jnp.concatenate([part, part], axis=0)
            sides.append(lax.dot_general(second_ref[...], twice, NT, preferred_element_type=F32))
        for g in range(second_ref.shape[0] // 16):
            rows = [
                jnp.where(low, s[16 * g : 16 * g + 8], s[16 * g + 8 : 16 * g + 16]) for s in sides
            ]
            right_out[pl.ds(g * tokens + t * 8, 16), :] = jnp.concatenate(rows, axis=0).astype(BF16)


def pair_kernel(
    block,
    left_ref,
    right_ref,
    pair_ref,
    first_ref,
    mask_ref,
    base_ref,
    gain_ref,
    outer_ref,
    gate_up_ref,
    down_ref,
    distance_ref,
    *rest,
):
    pair_out, dist_out, outer, start = rest[-4:]
    rows, length, channels = pair_out.shape
    first_row = block * rows
    pairs = rows // 2
    depth = right_ref.shape[1] // 2
    lanes = right_ref.shape[1]
    groups = right_ref.shape[0] // length
    hid = down_ref.shape[0]
    bins = distance_ref.shape[0] // 2
    for p in range(0, pairs, 2):
        tile = block * pairs + p
        weight = left_ref[:, tile * lanes : (tile + 2) * lanes]
        for g in range(0, groups, 4):
            got = dot(right_ref[g * length : (g + 4) * length, :], weight).astype(BF16)
            for q in range(2):
                for h in range(4):
                    outer[(p + q) * length : (p + q + 1) * length, (g + h) * lanes : (g + h + 1) * lanes] = got[
                        h * length : (h + 1) * length, q * lanes : (q + 1) * lanes
                    ]
    update = dot(outer[...], outer_ref[...])
    mask = mask_ref[block] * (1.0 / depth)
    base = base_ref[block]
    for p in range(pairs):
        for q in range(2):
            i = first_row + 2 * p + q
            value = (
                pair_ref[i].astype(F32)
                + (first_ref[i : i + 1, :] + base)
                + mask * update[p * length : (p + 1) * length, q * channels : (q + 1) * channels]
            )
            start[q, p * length : (p + 1) * length, :] = value
    for q in range(2):
        value = start[q]
        mean = jnp.mean(value, axis=-1, keepdims=True)
        centered = value - mean
        variance = jnp.mean(centered * centered, axis=-1, keepdims=True)
        normed = (centered * lax.rsqrt(variance + EPSILON) * gain_ref[...]).astype(BF16)
        for n in range(0, hid, 256):
            gate = dot(normed, gate_up_ref[:, n : n + 256])
            up = dot(normed, gate_up_ref[:, hid + n : hid + n + 256])
            hidden = (0.5 * gate * (1.0 + jnp.tanh(0.5 * gate)) * up).astype(BF16)
            value = value + dot(hidden, down_ref[n : n + 256, :])
        start[q] = value
    result = [start[q].astype(BF16) for q in range(2)]
    for p in range(pairs):
        for q in range(2):
            pair_out[2 * p + q] = result[q][p * length : (p + 1) * length]
    dist = lax.dot_general(
        jnp.concatenate(result, axis=1), distance_ref[...], NT, preferred_element_type=F32
    ).astype(BF16)
    for p in range(pairs):
        dist_out[:, 2 * p * bins : 2 * (p + 1) * bins] = dist[p * length : (p + 1) * length]


def own_kernel(blocks, *refs):
    parts, dists = refs[:blocks], refs[blocks : 2 * blocks]
    pair_out, own_ref, sems = refs[2 * blocks :]
    rows = parts[0].shape[0]
    copies = fetch(parts, [pair_out.at[pl.ds(n * rows, rows)] for n in range(blocks)], sems)
    pairs = rows // 2
    lanes = dists[0].shape[1] // pairs
    low = iota((pairs, lanes), 1) < lanes // 2
    for n, dist in enumerate(dists):
        tiles = jnp.stack([dist[:, p * lanes : (p + 1) * lanes].astype(F32) for p in range(pairs)])
        turned = jnp.swapaxes(tiles, 0, 1)
        for j in range(0, turned.shape[0], 2):
            first, second = turned[j], turned[j + 1]
            own_ref[j // 2, pl.ds(n * rows, pairs, stride=2), :] = jnp.where(
                low, first, pltpu.roll(second, lanes // 2, 1)
            )
            own_ref[j // 2, pl.ds(n * rows + 1, pairs, stride=2), :] = jnp.where(
                low, pltpu.roll(first, lanes // 2, 1), second
            )
    for copy in copies:
        copy.wait()


def final_kernel(blocks, own_ref, bias_ref, *refs):
    out_ref = refs[blocks]
    for n in range(blocks):
        width = refs[n].shape[1]
        lanes = bias_ref.shape[1]
        for t in range(0, width, lanes):
            at = slice(n * width + t, n * width + t + lanes)
            value = own_ref[at.start // lanes] + refs[n][:, t : t + lanes].astype(F32) + bias_ref[...]
            out_ref[:, at] = value.astype(BF16)


COST = pl.CostEstimate(flops=0, bytes_accessed=0, transcendentals=0)


def params(mib):
    return pltpu.CompilerParams(vmem_limit_bytes=mib * MIB)


def in_hbm(*arrays):
    return [pltpu.with_memory_space_constraint(a, pltpu.HBM) for a in arrays]


VMEM = pl.BlockSpec(memory_space=pltpu.VMEM)
SMEM = pl.BlockSpec(memory_space=pltpu.SMEM)
HBM = pl.BlockSpec(memory_space=pltpu.HBM)


def local(
    row_count,
    col_count,
    pair_state,
    token_kinds,
    first_type_table,
    second_type_table,
    alignment_state,
    alignment_index,
    alignment_table,
    first_weight,
    second_weight,
    outer_product_weight,
    outer_product_bias,
    pair_block_mask,
    transition_gain,
    transition_gate_up,
    transition_down,
    distance_weight,
    distance_bias,
):
    length = pair_state.shape[0]
    channels = pair_state.shape[2]
    depth = alignment_index.shape[0]
    features, c_width = first_weight.shape
    e_width = second_weight.shape[1]
    bins = distance_weight.shape[1]
    axes = ("row", "col")
    place = jnp.stack([lax.axis_index("col"), lax.axis_index("row")]).astype(jnp.int32)

    turned_index = alignment_index.T
    embedded = pl.pallas_call(
        embed_kernel,
        out_shape=jax.ShapeDtypeStruct(alignment_state.shape, BF16),
        in_specs=[HBM] * 3,
        out_specs=VMEM,
        scratch_shapes=[
            pltpu.VMEM(alignment_state.shape, BF16),
            pltpu.VMEM(turned_index.shape, jnp.int32),
            pltpu.VMEM(alignment_table.shape, BF16),
            pltpu.SemaphoreType.DMA((3,)),
        ],
        compiler_params=params(4),
        cost_estimate=COST,
        name="embed",
    )(*in_hbm(alignment_state, turned_index, alignment_table))

    def moved(value, target):
        pairs = [
            (r * col_count + c, target(r, c)[0] * col_count + target(r, c)[1])
            for r in range(row_count)
            for c in range(col_count)
        ]
        return lax.ppermute(value, axes, pairs)

    rights = [
        moved(embedded, lambda r, c, k=k: ((c - k) % row_count, r)) for k in range(col_count)
    ]
    lefts = [embedded] + [
        moved(embedded, lambda r, c, k=k: (r, (c - k) % col_count)) for k in range(1, col_count)
    ]

    blocks = pair_block_mask.shape[0]
    rows = length // blocks
    maps = jax.ShapeDtypeStruct((blocks, length, channels), F32)
    first_rows, masks, bases, outer_weight, pair_in, gate_up, down, gain, left_weight, right_weight, turned_distance, last = pl.pallas_call(
        weights_kernel,
        out_shape=(
            jax.ShapeDtypeStruct((length, channels), F32),
            maps,
            maps,
            jax.ShapeDtypeStruct((2 * c_width * e_width, 2 * channels), BF16),
            jax.ShapeDtypeStruct(pair_state.shape, BF16),
            jax.ShapeDtypeStruct(transition_gate_up.shape, BF16),
            jax.ShapeDtypeStruct(transition_down.shape, BF16),
            jax.ShapeDtypeStruct((1, channels), F32),
            jax.ShapeDtypeStruct((8 * features, 16 * c_width), BF16),
            jax.ShapeDtypeStruct((8 * e_width, 8 * features), BF16),
            jax.ShapeDtypeStruct((2 * bins, 2 * channels), BF16),
            jax.ShapeDtypeStruct((1, 2 * bins), F32),
        ),
        in_specs=[SMEM] + [HBM] * 14,
        out_specs=(VMEM,) * 12,
        scratch_shapes=[
            pltpu.VMEM((1, token_kinds.shape[0]), jnp.int32),
            pltpu.VMEM(first_type_table.shape, BF16),
            pltpu.VMEM(second_type_table.shape, BF16),
            pltpu.VMEM(outer_product_weight.shape, BF16),
            pltpu.VMEM((1, channels), BF16),
            pltpu.VMEM(pair_block_mask.shape, jnp.int32),
            pltpu.VMEM(first_weight.shape, BF16),
            pltpu.VMEM(second_weight.shape, BF16),
            pltpu.VMEM((bins, channels), BF16),
            pltpu.VMEM((1, bins), F32),
            pltpu.VMEM(outer_product_weight.shape, F32),
            pltpu.VMEM((token_kinds.shape[0], channels), F32),
            pltpu.SemaphoreType.DMA((14,)),
        ],
        compiler_params=params(8),
        cost_estimate=COST,
        name="weights",
    )(
        place,
        *in_hbm(
            token_kinds.reshape(1, -1),
            first_type_table,
            second_type_table,
            outer_product_weight,
            outer_product_bias.reshape(1, -1),
            pair_block_mask,
            pair_state,
            transition_gate_up,
            transition_down,
            first_weight,
            second_weight,
            transition_gain.reshape(1, -1),
            distance_weight.T,
            distance_bias.reshape(1, -1),
        ),
    )

    left_tiles, right_tiles = pl.pallas_call(
        functools.partial(project_kernel, col_count, features),
        out_shape=(
            jax.ShapeDtypeStruct((2 * depth, 2 * length * c_width), BF16),
            jax.ShapeDtypeStruct((e_width // 2 * length, 2 * depth), BF16),
        ),
        in_specs=[SMEM] + [VMEM] * (2 * col_count + 2),
        out_specs=(VMEM,) * 2,
        scratch_shapes=[pltpu.VMEM((depth, col_count * alignment_state.shape[1]), BF16)] * 2,
        compiler_params=params(8),
        cost_estimate=COST,
        name="project",
    )(place, *lefts, *rights, left_weight, right_weight)

    pair_parts, dist_parts, mirror_parts = [], [], []
    crossed = None
    for block in range(blocks):
        before = dist_parts[-1:]
        if block % 2 == 0 and crossed is not None:
            before = before + [crossed]
        pair_part, dist_part = pl.pallas_call(
            functools.partial(pair_kernel, block),
            out_shape=(
                jax.ShapeDtypeStruct((rows, length, channels), BF16),
                jax.ShapeDtypeStruct((length, rows * bins), BF16),
            ),
            in_specs=[VMEM] * 11 + [pl.BlockSpec(memory_space=pl.ANY)] * len(before),
            out_specs=(VMEM,) * 2,
            scratch_shapes=[
                pltpu.VMEM((rows // 2 * length, 2 * c_width * e_width), BF16),
                pltpu.VMEM((2, rows // 2 * length, channels), F32),
            ],
            compiler_params=params(16),
            cost_estimate=COST,
            name="pairs",
        )(
            left_tiles,
            right_tiles,
            pair_in,
            first_rows,
            masks,
            bases,
            gain,
            outer_weight,
            gate_up,
            down,
            turned_distance,
            *before,
        )
        pair_parts.append(pair_part)
        dist_parts.append(dist_part)
        if block % 2 == 0:
            crossed = moved(dist_part, lambda r, c: (r, (c + col_count // 2) % col_count))
            mirror_parts.append(moved(crossed, lambda r, c: ((c + col_count // 2) % col_count, r)))
        else:
            mirror_parts.append(moved(dist_part, lambda r, c: (c, r)))
    pair_out, own = pl.pallas_call(
        functools.partial(own_kernel, blocks),
        out_shape=(
            jax.ShapeDtypeStruct(pair_state.shape, BF16),
            jax.ShapeDtypeStruct((length // 2, length, 2 * bins), F32),
        ),
        in_specs=[VMEM] * (2 * blocks),
        out_specs=(HBM, VMEM),
        scratch_shapes=[pltpu.SemaphoreType.DMA((blocks,))],
        compiler_params=params(8),
        cost_estimate=COST,
        name="own",
    )(*pair_parts, *dist_parts)
    distogram = pl.pallas_call(
        functools.partial(final_kernel, blocks),
        out_shape=jax.ShapeDtypeStruct((length, length * bins), BF16),
        in_specs=[VMEM] * (blocks + 2),
        out_specs=VMEM,
        compiler_params=params(8),
        cost_estimate=COST,
        name="final",
    )(own, last, *mirror_parts)
    return pair_out, distogram


def solution(mesh):
    split = P(("conf", "row"), "col")
    tokens = P(None, ("conf", "row", "col"))
    in_specs = (
        P(("conf", "row"), "col", None),
        P("conf"),
        P(),
        P(),
        tokens,
        tokens,
        P(),
        P(),
        P(),
        P(),
        P(),
        split,
        P(),
        P(),
        P(),
        P(),
        P(),
    )
    return jax.shard_map(
        functools.partial(local, mesh.shape["row"], mesh.shape["col"]),
        mesh=mesh,
        in_specs=in_specs,
        out_specs=(P(("conf", "row"), "col", None), split),
        check_vma=False,
    )
```

time: 70.7 us -> 57.7 us (0.82)
  local copies, waits for them, and re-layouts: 15.2 us -> 0 us
  starting transfers between devices: 11.8 us -> 20.5 us
  waiting for transfers between devices: 22 us -> 14.5 us
  Pallas kernels: 20.1 us -> 21.6 us
    unnamed x32 -> x0, local copies, waits for them, and re-layouts: 10.2 us -> none
    ppermute x8 -> x13, starting transfers between devices: 11.8 us -> 20.5 us  [moved(): return lax.ppermute(value, axes, pairs)]
    ppermute x8 -> x13, waiting for transfers between devices: 22 us -> 14.5 us  [moved(): return lax.ppermute(value, axes, pairs)]
    reshape x3 -> x0, local copies, waits for them, and re-layouts: 4.83 us -> none  [local(): dist.reshape(length, length, bins).transpose(1, 0, 2)]
    pallas_call x1, Pallas kernels: 1.02 us -> 2.49 us  [local(): pl.pallas_call(weights_kernel, out_shape=(jax.ShapeDtypeStruct((length, c...]
    pallas_call x1, Pallas kernels: 0.49 us -> 1.42 us  [local(): pl.pallas_call(embed_kernel, out_shape=jax.ShapeDtypeStruct(alignment_sta...]
    pallas_call x3 -> x7, Pallas kernels: 18.5 us -> 17.7 us  [the longest x4 14.4 us: local(): pl.pallas_call(functools.partial(pair_kernel, block), out_shape=(jax.Shap...]
  transfers between devices with their start and end apart: 8 -> 13, of which waited for: 3 -> 5; matrix products, arithmetic and copies ran while one was open for 8% -> 0% of each run, Pallas kernels for 1% -> 19%
where the time goes in v2:
time: 57.7 us; the launch traced here: 57.5 us
  Pallas kernels  21.6 us (37%)
  starting transfers between devices  20.5 us (36%)
  waiting for transfers between devices  14.5 us (25%)
  between operations  0.77 us (1%)
    ppermute x13, starting transfers between devices, moved(): return lax.ppermute(value, axes, pairs)  20.5 us
    ppermute x13, waiting for transfers between devices, moved(): return lax.ppermute(value, axes, pairs)  14.5 us
    pallas_call x4, Pallas kernels, local(): pl.pallas_call(functools.partial(pair_kernel, block), out_shape=(jax.Shap...  14.4 us
    pallas_call x1, Pallas kernels, local(): pl.pallas_call(weights_kernel, out_shape=(jax.ShapeDtypeStruct((length, c...  2.49 us
    pallas_call x1, Pallas kernels, local(): pl.pallas_call(embed_kernel, out_shape=jax.ShapeDtypeStruct(alignment_sta...  1.42 us
    pallas_call x1, Pallas kernels, local(): pl.pallas_call(functools.partial(project_kernel, col_count, features), ou...  1.36 us
  transfers between devices with their start and end apart: 13, of which 5 were waited for; matrix products, arithmetic and copies ran while one was open for 0% of the time, Pallas kernels for 19%

profile of v2, /device:TPU:2, one launch (start us, length us, event | category | flops | bytes accessed | tf_op | source)
XLA Modules:
  0.0 57.5 jit_solution(8731199367393446205)
XLA Ops:
  0.6 1.4 %embed.1.refs_1_ = bf16[64,512]{1,0:T(8,128)(2,1)S(1)} custom-call(bf16[64,512]{1,0:T(8,128)(2,1)} %state_hbm.1, s32[16,64]{1,0:T(8,128)} %bitcast.9, bf16[32,32]{1,0:T(8,128)(2,1)} %table_hbm.1), custom_call_target="tpu_custom_call" | custom-call | tf_op jit(solution)/shard_map/embed/pallas_call | solution.py:359
  2.1 1.5 %collective-permute-start.1 = (bf16[64,512]{1,0:T(8,128)(2,1)S(1)}, bf16[64,512]{1,0:T(8,128)(2,1)S(1)}, u32[]{:S(2)}, u32[]{:S(2)}) collective-permute-start(bf16[64,512]{1,0:T(8,128)(2,1)S(1)} %embed.1.refs_1_), channel_id=1, source_target_pairs={{0,2},{1,3},{2,0},{3,1},{4,6},{5,7},{6,4},{7,5},{8,10},{9,11},{10,... | collective-permute-start | bytes 196616 | tf_op jit(solution)/shard_map/ppermute | solution.py:381
  3.6 4.7 %collective-permute-start.3 = (bf16[64,512]{1,0:T(8,128)(2,1)S(1)}, bf16[64,512]{1,0:T(8,128)(2,1)S(1)}, u32[]{:S(2)}, u32[]{:S(2)}) collective-permute-start(bf16[64,512]{1,0:T(8,128)(2,1)S(1)} %embed.1.refs_1_), channel_id=1, source_target_pairs={{0,0},{1,4},{2,8},{3,12},{4,1},{5,5},{6,9},{7,13},{8,2},{9,6},{10,... | collective-permute-start | bytes 196616 | tf_op jit(solution)/shard_map/ppermute | solution.py:381
  8.3 0.4 collective-permute-start.4
  8.8 2.4 %collective-permute-start.5 = (bf16[64,512]{1,0:T(8,128)(2,1)S(1)}, bf16[64,512]{1,0:T(8,128)(2,1)S(1)}, u32[]{:S(2)}, u32[]{:S(2)}) collective-permute-start(bf16[64,512]{1,0:T(8,128)(2,1)S(1)} %embed.1.refs_1_), channel_id=1, source_target_pairs={{0,8},{1,12},{2,0},{3,4},{4,9},{5,13},{6,1},{7,5},{8,10},{9,14},{1... | collective-permute-start | bytes 196616 | tf_op jit(solution)/shard_map/ppermute | solution.py:381
  11.2 0.7 %collective-permute-start.6 = (bf16[64,512]{1,0:T(8,128)(2,1)S(1)}, bf16[64,512]{1,0:T(8,128)(2,1)S(1)}, u32[]{:S(2)}, u32[]{:S(2)}) collective-permute-start(bf16[64,512]{1,0:T(8,128)(2,1)S(1)} %embed.1.refs_1_), channel_id=1, source_target_pairs={{0,4},{1,8},{2,12},{3,0},{4,5},{5,9},{6,13},{7,1},{8,6},{9,10},{10... | collective-permute-start | bytes 196616 | tf_op jit(solution)/shard_map/ppermute | solution.py:381
  11.9 0.1 pad_add_fusion.place_ref.refs_0_
  12.0 2.5 %weights.1 = (f32[64,128]{1,0:T(8,128)S(1)}, f32[4,64,128]{2,1,0:T(8,128)S(1)}, f32[4,64,128]{2,1,0:T(8,128)S(1)}, bf16[2048,256]{1,0:T(8,128)(2,1)S(1)}, bf16[6...) custom-call(s32[2]{0:T(128)S(1)} %pad_add_fusion.place_ref.refs_0_, ...), custom_call_target="tpu_custom_call" | custom-call | tf_op jit(solution)/shard_map/weights/pallas_call | solution.py:393
  14.5 3.1 %collective-permute-done.5.refs_7_ = bf16[64,512]{1,0:T(8,128)(2,1)S(1)} collective-permute-done((bf16[64,512]{1,0:T(8,128)(2,1)S(1)}, bf16[64,512]{1,0:T(8,128)(2,1)S(1)}, u32[]{:S(2)}, u32[]{:S(2)}) %collective-permute-start.5) | collective-permute-done | bytes 65568 | tf_op jit(solution)/shard_map/ppermute | solution.py:381
  17.6 0.4 collective-permute-done.6.refs_8_
  18.0 1.4 %project.1 = (bf16[128,4096]{1,0:T(8,128)(2,1)S(1)}, bf16[1024,128]{1,0:T(8,128)(2,1)S(1)}) custom-call(s32[2]{0:T(128)S(1)} %pad_add_fusion.place_ref.refs_0_, bf16[64,512]{1,0:T(8,128)(2,1)S(1)} %embed.1.refs_1_, bf16[64,512]{1,0:T(8,128)(2,1)S(1)} %collective-permute-done.refs_2_, bf16[64,512]{1,0:T(8,128)(2,1)S(1)} %collective-permute-done.1.refs_3_, ...), custom_call_target="tpu_custom_call" | custom-call | tf_op jit(solution)/shard_map/project/pallas_call | solution.py:449
  19.4 3.6 %pairs.4 = (bf16[16,64,128]{2,1,0:T(8,128)(2,1)S(1)}, bf16[64,1024]{1,0:T(8,128)(2,1)S(1)}) custom-call(bf16[128,4096]{1,0:T(8,128)(2,1)S(1)} %get-tuple-element.28.left_ref, bf16[1024,128]{1,0:T(8,128)(2,1)S(1)} %get-tuple-element.29.right_ref, bf16[64,64,128]{2,1,0:T(8,128)(2,1)S(1)} %get-tuple-element.30.pair_ref, ...), custom_call_target="tpu_custom_call" | custom-call | tf_op jit(solution)/shard_map/pairs/pallas_call | solution.py:469
  23.1 3.6 %pairs.5 = (bf16[16,64,128]{2,1,0:T(8,128)(2,1)S(1)}, bf16[64,1024]{1,0:T(8,128)(2,1)S(1)}) custom-call(bf16[128,4096]{1,0:T(8,128)(2,1)S(1)} %get-tuple-element.28.left_ref, bf16[1024,128]{1,0:T(8,128)(2,1)S(1)} %get-tuple-element.29.right_ref, bf16[64,64,128]{2,1,0:T(8,128)(2,1)S(1)} %get-tuple-element.30.pair_ref, ...), custom_call_target="tpu_custom_call" | custom-call | tf_op jit(solution)/shard_map/pairs/pallas_call | solution.py:469
  26.7 1.4 %collective-permute-done.7.rest_1_ = bf16[64,1024]{1,0:T(8,128)(2,1)S(1)} collective-permute-done((bf16[64,1024]{1,0:T(8,128)(2,1)S(1)}, bf16[64,1024]{1,0:T(8,128)(2,1)S(1)}, u32[]{:S(2)}, u32[]{:S(2)}) %collective-permute-start.7) | collective-permute-done | bytes 131104 | tf_op jit(solution)/shard_map/ppermute | solution.py:381
  28.0 3.6 %pairs.6 = (bf16[16,64,128]{2,1,0:T(8,128)(2,1)S(1)}, bf16[64,1024]{1,0:T(8,128)(2,1)S(1)}) custom-call(bf16[128,4096]{1,0:T(8,128)(2,1)S(1)} %get-tuple-element.28.left_ref, bf16[1024,128]{1,0:T(8,128)(2,1)S(1)} %get-tuple-element.29.right_ref, bf16[64,64,128]{2,1,0:T(8,128)(2,1)S(1)} %get-tuple-element.30.pair_ref, ...), custom_call_target="tpu_custom_call" | custom-call | tf_op jit(solution)/shard_map/pairs/pallas_call | solution.py:469
  31.6 0.7 %collective-permute-start.10 = (bf16[64,1024]{1,0:T(8,128)(2,1)S(1)}, bf16[64,1024]{1,0:T(8,128)(2,1)S(1)}, u32[]{:S(2)}, u32[]{:S(2)}) collective-permute-start(bf16[64,1024]{1,0:T(8,128)(2,1)S(1)} %get-tuple-element.44.rest_0_.refs_6_), channel_id=1, source_target_pairs={{0,2},{1,3},{2,0},{3,1},{4,6},{5,7},{6,4},{7,5},{8,10},{9,11},{10,... | collective-permute-start | bytes 393224 | tf_op jit(solution)/shard_map/ppermute | solution.py:381
  32.4 3.6 %collective-permute-start.9 = (bf16[64,1024]{1,0:T(8,128)(2,1)S(1)}, bf16[64,1024]{1,0:T(8,128)(2,1)S(1)}, u32[]{:S(2)}, u32[]{:S(2)}) collective-permute-start(bf16[64,1024]{1,0:T(8,128)(2,1)S(1)} %get-tuple-element.42.rest_0_.refs_5_), channel_id=1, source_target_pairs={{0,0},{1,4},{2,8},{3,12},{4,1},{5,5},{6,9},{7,13},{8,2},{9,6},{10,... | collective-permute-start | bytes 393224 | tf_op jit(solution)/shard_map/ppermute | solution.py:381
  35.9 3.6 %pairs.7 = (bf16[16,64,128]{2,1,0:T(8,128)(2,1)S(1)}, bf16[64,1024]{1,0:T(8,128)(2,1)S(1)}) custom-call(bf16[128,4096]{1,0:T(8,128)(2,1)S(1)} %get-tuple-element.28.left_ref, bf16[1024,128]{1,0:T(8,128)(2,1)S(1)} %get-tuple-element.29.right_ref, bf16[64,64,128]{2,1,0:T(8,128)(2,1)S(1)} %get-tuple-element.30.pair_ref, ...), custom_call_target="tpu_custom_call" | custom-call | tf_op jit(solution)/shard_map/pairs/pallas_call | solution.py:469
  39.5 4.2 %collective-permute-start.12 = (bf16[64,1024]{1,0:T(8,128)(2,1)S(1)}, bf16[64,1024]{1,0:T(8,128)(2,1)S(1)}, u32[]{:S(2)}, u32[]{:S(2)}) collective-permute-start(bf16[64,1024]{1,0:T(8,128)(2,1)S(1)} %get-tuple-element.46.refs_7_), channel_id=1, source_target_pairs={{0,0},{1,4},{2,8},{3,12},{4,1},{5,5},{6,9},{7,13},{8,2},{9,6},{10,... | collective-permute-start | bytes 393224 | tf_op jit(solution)/shard_map/ppermute | solution.py:381
  43.9 2.0 %collective-permute-start.11 = (bf16[64,1024]{1,0:T(8,128)(2,1)S(1)}, bf16[64,1024]{1,0:T(8,128)(2,1)S(1)}, u32[]{:S(2)}, u32[]{:S(2)}) collective-permute-start(bf16[64,1024]{1,0:T(8,128)(2,1)S(1)} %collective-permute-done.10), channel_id=1, source_target_pairs={{0,8},{1,12},{2,0},{3,4},{4,9},{5,13},{6,1},{7,5},{8,10},{9,14},{1... | collective-permute-start | bytes 393224 | tf_op jit(solution)/shard_map/ppermute | solution.py:381
  45.9 1.0 %own.1 = (bf16[64,64,128]{2,1,0:T(8,128)(2,1)}, f32[32,64,128]{2,1,0:T(8,128)S(1)}) custom-call(bf16[16,64,128]{2,1,0:T(8,128)(2,1)S(1)} %get-tuple-element.39.refs_0_, bf16[16,64,128]{2,1,0:T(8,128)(2,1)S(1)} %get-tuple-element.41.refs_1_, bf16[16,64,128]{2,1,0:T(8,128)(2,1)S(1)} %get-tuple-element.43.refs_2_, ...), custom_call_target="tpu_custom_call" | custom-call | tf_op jit(solution)/shard_map/own/pallas_call | solution.py:505
  46.9 8.2 %collective-permute-done.8.refs_0_ = bf16[64,1024]{1,0:T(8,128)(2,1)S(1)} collective-permute-done((bf16[64,1024]{1,0:T(8,128)(2,1)S(1)}, bf16[64,1024]{1,0:T(8,128)(2,1)S(1)}, u32[]{:S(2)}, u32[]{:S(2)}) %collective-permute-start.8) | collective-permute-done | bytes 131104 | tf_op jit(solution)/shard_map/ppermute | solution.py:381
  55.1 1.4 %collective-permute-done.11.refs_2_ = bf16[64,1024]{1,0:T(8,128)(2,1)S(1)} collective-permute-done((bf16[64,1024]{1,0:T(8,128)(2,1)S(1)}, bf16[64,1024]{1,0:T(8,128)(2,1)S(1)}, u32[]{:S(2)}, u32[]{:S(2)}) %collective-permute-start.11) | collective-permute-done | bytes 131104 | tf_op jit(solution)/shard_map/ppermute | solution.py:381
  56.5 0.9 %final.1 = bf16[64,4096]{1,0:T(8,128)(2,1)} custom-call(f32[32,64,128]{2,1,0:T(8,128)S(1)} %get-tuple-element.48.own_ref, f32[1,128]{1,0:T(1,128)S(1)} %get-tuple-element.49.bias_ref, bf16[64,1024]{1,0:T(8,128)(2,1)S(1)} %collective-permute-done.8.refs_0_, bf16[64,1024]{1,0:T(8,128)(2,1)S(1)} %collective-permute-done.9.refs_1_, ...), custom_call_target="tpu_custom_call" | custom-call | tf_op jit(solution)/shard_map/final/pallas_call | solution.py:518
  (12 shorter events, 0.2 us)
Async XLA Ops:
  2.1 6.7 %collective-permute-start = (bf16[64,512]{1,0:T(8,128)(2,1)S(1)}, bf16[64,512]{1,0:T(8,128)(2,1)S(1)}, u32[]{:S(2)}, u32[]{:S(2)}) collective-permute-start(bf16[64,512]{1,0:T(8,128)(2,1)S(1)} %embed.1.refs_1_), channel_id=1, source_target_pairs={{0,3},{1,0},{2,1},{3,2},{4,7},{5,4},{6,5},{7,6},{8,11},{9,8},{10,9... | collective-permute-start | bytes 196616 | tf_op jit(solution)/shard_map/ppermute | solution.py:381
  2.1 9.1 %collective-permute-start.1 = (bf16[64,512]{1,0:T(8,128)(2,1)S(1)}, bf16[64,512]{1,0:T(8,128)(2,1)S(1)}, u32[]{:S(2)}, u32[]{:S(2)}) collective-permute-start(bf16[64,512]{1,0:T(8,128)(2,1)S(1)} %embed.1.refs_1_), channel_id=1, source_target_pairs={{0,2},{1,3},{2,0},{3,1},{4,6},{5,7},{6,4},{7,5},{8,10},{9,11},{10,... | collective-permute-start | bytes 196616 | tf_op jit(solution)/shard_map/ppermute | solution.py:381
  3.6 10.9 %collective-permute-start.2 = (bf16[64,512]{1,0:T(8,128)(2,1)S(1)}, bf16[64,512]{1,0:T(8,128)(2,1)S(1)}, u32[]{:S(2)}, u32[]{:S(2)}) collective-permute-start(bf16[64,512]{1,0:T(8,128)(2,1)S(1)} %embed.1.refs_1_), channel_id=1, source_target_pairs={{0,1},{1,2},{2,3},{3,0},{4,5},{5,6},{6,7},{7,4},{8,9},{9,10},{10,1... | collective-permute-start | bytes 196616 | tf_op jit(solution)/shard_map/ppermute | solution.py:381
  3.6 10.9 %collective-permute-start.3 = (bf16[64,512]{1,0:T(8,128)(2,1)S(1)}, bf16[64,512]{1,0:T(8,128)(2,1)S(1)}, u32[]{:S(2)}, u32[]{:S(2)}) collective-permute-start(bf16[64,512]{1,0:T(8,128)(2,1)S(1)} %embed.1.refs_1_), channel_id=1, source_target_pairs={{0,0},{1,4},{2,8},{3,12},{4,1},{5,5},{6,9},{7,13},{8,2},{9,6},{10,... | collective-permute-start | bytes 196616 | tf_op jit(solution)/shard_map/ppermute | solution.py:381
  8.3 6.2 %collective-permute-start.4 = (bf16[64,512]{1,0:T(8,128)(2,1)S(1)}, bf16[64,512]{1,0:T(8,128)(2,1)S(1)}, u32[]{:S(2)}, u32[]{:S(2)}) collective-permute-start(bf16[64,512]{1,0:T(8,128)(2,1)S(1)} %embed.1.refs_1_), channel_id=1, source_target_pairs={{0,12},{1,0},{2,4},{3,8},{4,13},{5,1},{6,5},{7,9},{8,14},{9,2},{10... | collective-permute-start | bytes 196616 | tf_op jit(solution)/shard_map/ppermute | solution.py:381
  8.8 8.8 %collective-permute-start.5 = (bf16[64,512]{1,0:T(8,128)(2,1)S(1)}, bf16[64,512]{1,0:T(8,128)(2,1)S(1)}, u32[]{:S(2)}, u32[]{:S(2)}) collective-permute-start(bf16[64,512]{1,0:T(8,128)(2,1)S(1)} %embed.1.refs_1_), channel_id=1, source_target_pairs={{0,8},{1,12},{2,0},{3,4},{4,9},{5,13},{6,1},{7,5},{8,10},{9,14},{1... | collective-permute-start | bytes 196616 | tf_op jit(solution)/shard_map/ppermute | solution.py:381
  11.2 6.8 %collective-permute-start.6 = (bf16[64,512]{1,0:T(8,128)(2,1)S(1)}, bf16[64,512]{1,0:T(8,128)(2,1)S(1)}, u32[]{:S(2)}, u32[]{:S(2)}) collective-permute-start(bf16[64,512]{1,0:T(8,128)(2,1)S(1)} %embed.1.refs_1_), channel_id=1, source_target_pairs={{0,4},{1,8},{2,12},{3,0},{4,5},{5,9},{6,13},{7,1},{8,6},{9,10},{10... | collective-permute-start | bytes 196616 | tf_op jit(solution)/shard_map/ppermute | solution.py:381
  23.0 5.0 %collective-permute-start.7 = (bf16[64,1024]{1,0:T(8,128)(2,1)S(1)}, bf16[64,1024]{1,0:T(8,128)(2,1)S(1)}, u32[]{:S(2)}, u32[]{:S(2)}) collective-permute-start(bf16[64,1024]{1,0:T(8,128)(2,1)S(1)} %get-tuple-element.40.rest_0_.refs_4_), channel_id=1, source_target_pairs={{0,2},{1,3},{2,0},{3,1},{4,6},{5,7},{6,4},{7,5},{8,10},{9,11},{10,... | collective-permute-start | bytes 393224 | tf_op jit(solution)/shard_map/ppermute | solution.py:381
  31.6 12.2 %collective-permute-start.10 = (bf16[64,1024]{1,0:T(8,128)(2,1)S(1)}, bf16[64,1024]{1,0:T(8,128)(2,1)S(1)}, u32[]{:S(2)}, u32[]{:S(2)}) collective-permute-start(bf16[64,1024]{1,0:T(8,128)(2,1)S(1)} %get-tuple-element.44.rest_0_.refs_6_), channel_id=1, source_target_pairs={{0,2},{1,3},{2,0},{3,1},{4,6},{5,7},{6,4},{7,5},{8,10},{9,11},{10,... | collective-permute-start | bytes 393224 | tf_op jit(solution)/shard_map/ppermute | solution.py:381
  32.4 14.6 %collective-permute-start.9 = (bf16[64,1024]{1,0:T(8,128)(2,1)S(1)}, bf16[64,1024]{1,0:T(8,128)(2,1)S(1)}, u32[]{:S(2)}, u32[]{:S(2)}) collective-permute-start(bf16[64,1024]{1,0:T(8,128)(2,1)S(1)} %get-tuple-element.42.rest_0_.refs_5_), channel_id=1, source_target_pairs={{0,0},{1,4},{2,8},{3,12},{4,1},{5,5},{6,9},{7,13},{8,2},{9,6},{10,... | collective-permute-start | bytes 393224 | tf_op jit(solution)/shard_map/ppermute | solution.py:381
  39.5 15.6 %collective-permute-start.12 = (bf16[64,1024]{1,0:T(8,128)(2,1)S(1)}, bf16[64,1024]{1,0:T(8,128)(2,1)S(1)}, u32[]{:S(2)}, u32[]{:S(2)}) collective-permute-start(bf16[64,1024]{1,0:T(8,128)(2,1)S(1)} %get-tuple-element.46.refs_7_), channel_id=1, source_target_pairs={{0,0},{1,4},{2,8},{3,12},{4,1},{5,5},{6,9},{7,13},{8,2},{9,6},{10,... | collective-permute-start | bytes 393224 | tf_op jit(solution)/shard_map/ppermute | solution.py:381
  43.8 11.3 %collective-permute-start.8 = (bf16[64,1024]{1,0:T(8,128)(2,1)S(1)}, bf16[64,1024]{1,0:T(8,128)(2,1)S(1)}, u32[]{:S(2)}, u32[]{:S(2)}) collective-permute-start(bf16[64,1024]{1,0:T(8,128)(2,1)S(1)} %collective-permute-done.7.rest_1_), channel_id=1, source_target_pairs={{0,8},{1,12},{2,0},{3,4},{4,9},{5,13},{6,1},{7,5},{8,10},{9,14},{1... | collective-permute-start | bytes 393224 | tf_op jit(solution)/shard_map/ppermute | solution.py:381
  43.9 12.7 %collective-permute-start.11 = (bf16[64,1024]{1,0:T(8,128)(2,1)S(1)}, bf16[64,1024]{1,0:T(8,128)(2,1)S(1)}, u32[]{:S(2)}, u32[]{:S(2)}) collective-permute-start(bf16[64,1024]{1,0:T(8,128)(2,1)S(1)} %collective-permute-done.10), channel_id=1, source_target_pairs={{0,8},{1,12},{2,0},{3,4},{4,9},{5,13},{6,1},{7,5},{8,10},{9,14},{1... | collective-permute-start | bytes 393224 | tf_op jit(solution)/shard_map/ppermute | solution.py:381

commit v3 on v2

--- a/solution.py
+++ b/solution.py
@@ -38,31 +38,53 @@
     return copies
 
 
-def embed_kernel(state_hbm, index_hbm, table_hbm, out_ref, state_ref, index_ref, table_ref, sems):
+def add_embedding(state_ref, index_ref, table, kinds, features, write):
+    tokens = index_ref.shape[0]
+    group = table.shape[0] // kinds
+    spread_tokens = (iota((tokens, tokens * kinds), 1) // kinds == iota((tokens, tokens * kinds), 0)).astype(BF16)
+    wide = lax.dot_general(
+        index_ref[...].astype(F32).astype(BF16), spread_tokens, TN, preferred_element_type=F32
+    )
+    onehot = (wide == (iota(wide.shape, 1) % kinds).astype(F32)).astype(BF16)
+    width = group * features
+    for n in range(tokens // group):
+        rows = dot(onehot[:, n * group * kinds : (n + 1) * group * kinds], table)
+        write(n * width, (state_ref[:, n * width : (n + 1) * width].astype(F32) + rows).astype(BF16))
+
+
+def embed_own_kernel(
+    state_hbm, index_hbm, table_hbm, out_ref, wide_ref, state_ref, index_ref, table_ref, sems
+):
     copies = fetch((index_hbm, table_hbm, state_hbm), (index_ref, table_ref, state_ref), sems)
-    tokens = index_ref.shape[0]
     kinds, features = table_ref.shape
-    group = min(tokens, 256 // features)
     copies[1].wait()
-    table = spread(
-        group * kinds,
+    wide_ref[...] = spread(
+        wide_ref.shape[0],
         lambda r: r % kinds,
         table_ref[...],
-        group * features,
+        wide_ref.shape[1],
         lambda c: c % features,
         lambda r, c: r // kinds == c // features,
     )
-    spread_tokens = (iota((tokens, tokens * kinds), 1) // kinds == iota((tokens, tokens * kinds), 0)).astype(BF16)
     copies[0].wait()
-    wide = lax.dot_general(
-        index_ref[...].astype(F32).astype(BF16), spread_tokens, TN, preferred_element_type=F32
-    )
-    onehot = (wide == (iota(wide.shape, 1) % kinds).astype(F32)).astype(BF16)
     copies[2].wait()
-    for start in range(0, tokens, group):
-        at = slice(start * features, (start + group) * features)
-        rows = dot(onehot[:, start * kinds : (start + group) * kinds], table)
-        out_ref[:, at] = (state_ref[:, at].astype(F32) + rows).astype(BF16)
+
+    def write(at, value):
+        out_ref[:, at : at + value.shape[1]] = value
+
+    add_embedding(state_ref, index_ref, wide_ref[...], kinds, features, write)
+
+
+def embed_couple_kernel(kinds, place_ref, own_ref, wide_ref, state_ref, index_ref, out_ref):
+    width = own_ref.shape[1]
+    place = place_ref[4]
+    out_ref[:, pl.ds(pl.multiple_of(place * width, width), width)] = own_ref[...]
+    first = pl.multiple_of((1 - place) * width, width)
+
+    def write(at, value):
+        out_ref[:, pl.ds(pl.multiple_of(first + at, value.shape[1]), value.shape[1])] = value
+
+    add_embedding(state_ref, index_ref, wide_ref[...], kinds, width // index_ref.shape[0], write)
 
 
 def weights_kernel(
@@ -151,9 +173,9 @@
     kinds = kinds_ref[...]
     onehot = (iota((first_ref.shape[0], kinds.shape[1]), 0) == kinds).astype(BF16)
     rows[...] = lax.dot_general(onehot, first_ref[...], TN, preferred_element_type=F32)
-    first_out[...] = rows[pl.ds(pl.multiple_of(place_ref[1] * length, length), length), :]
+    first_out[...] = rows[pl.ds(pl.multiple_of(place_ref[3] * length, length), length), :]
     rows[...] = lax.dot_general(onehot, second_ref[...], TN, preferred_element_type=F32)
-    second = rows[pl.ds(pl.multiple_of(place_ref[0] * length, length), length), :]
+    second = rows[pl.ds(pl.multiple_of(place_ref[2] * length, length), length), :]
     blocks, columns = mask_ref.shape
     reach = (iota((length, columns), 0) // (length // columns) == iota((length, columns), 1)).astype(BF16)
     mask = lax.dot_general(
@@ -175,40 +197,39 @@
         copy.wait()
 
 
-def project_kernel(blocks, features, *refs):
-    place_ref = refs[0]
-    lefts, rights = refs[1 : 1 + blocks], refs[1 + blocks : 1 + 2 * blocks]
-    first_ref, second_ref, left_out, right_out, left_all, right_all = refs[1 + 2 * blocks :]
-    depth, width = lefts[0].shape
-    for which, (parts, whole) in enumerate(((lefts, left_all), (rights, right_all))):
-        for k, part in enumerate(parts):
-            block = lax.rem(place_ref[which] + k, blocks)
-            whole[:, pl.ds(pl.multiple_of(block * width, width), width)] = part[...]
-    tokens = blocks * width // features
-    group, columns = first_ref.shape
-    half = iota((depth, columns), 1) % (columns // 4) < columns // 8
-    for t in range(tokens // 8):
-        both = dot(left_all[:, t * group : (t + 1) * group], first_ref[...])
-        at = slice(t * columns, (t + 1) * columns)
-        left_out[0:depth, at] = jnp.where(half, both, 0.0).astype(BF16)
-        left_out[depth : 2 * depth, at] = jnp.where(half, 0.0, both).astype(BF16)
+def project_kernel(couples, features, place_ref, *refs):
+    parts, weight_ref, right_out, whole = refs[:couples], refs[couples], refs[couples + 1], refs[couples + 2]
+    depth, width = parts[0].shape
+    for k, part in enumerate(parts):
+        couple = lax.rem(place_ref[1] + k, couples)
+        whole[:, pl.ds(pl.multiple_of(couple * width, width), width)] = part[...]
+    tokens = couples * width // features
+    group = weight_ref.shape[1]
     low = iota((8, 2 * depth), 1) < depth
     for t in range(0, tokens // 8, 2):
         sides = []
         for u in (t, t + 1):
-            part = right_all[:, u * group : (u + 1) * group]
+            part = whole[:, u * group : (u + 1) * group]
             twice = jnp.concatenate([part, part], axis=0)
-            sides.append(lax.dot_general(second_ref[...], twice, NT, preferred_element_type=F32))
-        for g in range(second_ref.shape[0] // 16):
+            sides.append(lax.dot_general(weight_ref[...], twice, NT, preferred_element_type=F32))
+        for g in range(weight_ref.shape[0] // 16):
             rows = [
                 jnp.where(low, s[16 * g : 16 * g + 8], s[16 * g + 8 : 16 * g + 16]) for s in sides
             ]
             right_out[pl.ds(g * tokens + t * 8, 16), :] = jnp.concatenate(rows, axis=0).astype(BF16)
 
 
+def row_of(couple, couples, piece, rows, couple_rows):
+    return pl.multiple_of(lax.rem(couple, couples) * couple_rows + piece * rows, rows)
+
+
 def pair_kernel(
-    block,
+    k,
+    piece,
+    couples,
+    place_ref,
     left_ref,
+    left_weight_ref,
     right_ref,
     pair_ref,
     first_ref,
@@ -223,16 +244,24 @@
 ):
     pair_out, dist_out, outer, start = rest[-4:]
     rows, length, channels = pair_out.shape
-    first_row = block * rows
+    block_rows = length // mask_ref.shape[0]
+    first_row = row_of(place_ref[0] + k, couples, piece, rows, length // couples)
     pairs = rows // 2
-    depth = right_ref.shape[1] // 2
-    lanes = right_ref.shape[1]
+    depth, lanes = right_ref.shape[1] // 2, right_ref.shape[1]
     groups = right_ref.shape[0] // length
     hid = down_ref.shape[0]
     bins = distance_ref.shape[0] // 2
+    group, columns = left_weight_ref.shape
+    half = iota((depth, columns), 1) % lanes < lanes // 2
+    weights = []
+    for t in range(rows // 8):
+        at = (piece * rows // 8 + t) * group
+        both = dot(left_ref[:, at : at + group], left_weight_ref[...])
+        weights.append(
+            jnp.concatenate([jnp.where(half, both, 0.0), jnp.where(half, 0.0, both)], axis=0).astype(BF16)
+        )
     for p in range(0, pairs, 2):
-        tile = block * pairs + p
-        weight = left_ref[:, tile * lanes : (tile + 2) * lanes]
+        weight = weights[p // 4][:, p % 4 * lanes : (p % 4 + 2) * lanes]
         for g in range(0, groups, 4):
             got = dot(right_ref[g * length : (g + 4) * length, :], weight).astype(BF16)
             for q in range(2):
@@ -240,30 +269,33 @@
                     outer[(p + q) * length : (p + q + 1) * length, (g + h) * lanes : (g + h + 1) * lanes] = got[
                         h * length : (h + 1) * length, q * lanes : (q + 1) * lanes
                     ]
-    update = dot(outer[...], outer_ref[...])
-    mask = mask_ref[block] * (1.0 / depth)
-    base = base_ref[block]
+    half = outer.shape[0] // 2
+    update = [dot(outer[n * half : (n + 1) * half], outer_ref[...]) for n in range(2)]
+    first = first_ref[pl.ds(first_row, rows), :]
     for p in range(pairs):
+        block = lax.div(first_row + 2 * p, block_rows)
+        mask = mask_ref[block] * (1.0 / depth)
+        base = base_ref[block]
+        at = p * length % half
+        part = update[p * length // half][at : at + length]
         for q in range(2):
-            i = first_row + 2 * p + q
-            value = (
-                pair_ref[i].astype(F32)
-                + (first_ref[i : i + 1, :] + base)
-                + mask * update[p * length : (p + 1) * length, q * channels : (q + 1) * channels]
+            i = 2 * p + q
+            start[q, p * length : (p + 1) * length, :] = (
+                pair_ref[first_row + i].astype(F32)
+                + (first[i : i + 1, :] + base)
+                + mask * part[:, q * channels : (q + 1) * channels]
             )
-            start[q, p * length : (p + 1) * length, :] = value
-    for q in range(2):
-        value = start[q]
+    half = min(start.shape[1], 512)
+    for q, at in ((q, slice(n, n + half)) for q in range(2) for n in range(0, start.shape[1], half)):
+        value = start[q, at]
         mean = jnp.mean(value, axis=-1, keepdims=True)
         centered = value - mean
         variance = jnp.mean(centered * centered, axis=-1, keepdims=True)
         normed = (centered * lax.rsqrt(variance + EPSILON) * gain_ref[...]).astype(BF16)
-        for n in range(0, hid, 256):
-            gate = dot(normed, gate_up_ref[:, n : n + 256])
-            up = dot(normed, gate_up_ref[:, hid + n : hid + n + 256])
-            hidden = (0.5 * gate * (1.0 + jnp.tanh(0.5 * gate)) * up).astype(BF16)
-            value = value + dot(hidden, down_ref[n : n + 256, :])
-        start[q] = value
+        gate_up = dot(normed, gate_up_ref[...])
+        gate, up = gate_up[:, :hid], gate_up[:, hid:]
+        hidden = (0.5 * gate * (1.0 + jnp.tanh(0.5 * gate)) * up).astype(BF16)
+        start[q, at] = value + dot(hidden, down_ref[...])
     result = [start[q].astype(BF16) for q in range(2)]
     for p in range(pairs):
         for q in range(2):
@@ -275,38 +307,45 @@
         dist_out[:, 2 * p * bins : 2 * (p + 1) * bins] = dist[p * length : (p + 1) * length]
 
 
-def own_kernel(blocks, *refs):
-    parts, dists = refs[:blocks], refs[blocks : 2 * blocks]
-    pair_out, own_ref, sems = refs[2 * blocks :]
-    rows = parts[0].shape[0]
-    copies = fetch(parts, [pair_out.at[pl.ds(n * rows, rows)] for n in range(blocks)], sems)
+def own_kernel(couples, pieces, place_ref, *refs):
+    count = couples * pieces
+    parts, dists = refs[:count], refs[count : 2 * count]
+    pair_out, own_ref, sems = refs[2 * count :]
+    rows, length, _ = parts[0].shape
+    firsts = [
+        row_of(place_ref[0] + n // pieces, couples, n % pieces, rows, length // couples)
+        for n in range(count)
+    ]
+    copies = fetch(parts, [pair_out.at[pl.ds(first, rows)] for first in firsts], sems)
     pairs = rows // 2
     lanes = dists[0].shape[1] // pairs
     low = iota((pairs, lanes), 1) < lanes // 2
-    for n, dist in enumerate(dists):
+    for first, dist in zip(firsts, dists, strict=True):
         tiles = jnp.stack([dist[:, p * lanes : (p + 1) * lanes].astype(F32) for p in range(pairs)])
         turned = jnp.swapaxes(tiles, 0, 1)
-        for j in range(0, turned.shape[0], 2):
-            first, second = turned[j], turned[j + 1]
-            own_ref[j // 2, pl.ds(n * rows, pairs, stride=2), :] = jnp.where(
-                low, first, pltpu.roll(second, lanes // 2, 1)
+        for j in range(0, length, 2):
+            one, two = turned[j], turned[j + 1]
+            own_ref[j // 2, pl.ds(first, pairs, stride=2), :] = jnp.where(
+                low, one, pltpu.roll(two, lanes // 2, 1)
             )
-            own_ref[j // 2, pl.ds(n * rows + 1, pairs, stride=2), :] = jnp.where(
-                low, pltpu.roll(first, lanes // 2, 1), second
+            own_ref[j // 2, pl.ds(first + 1, pairs, stride=2), :] = jnp.where(
+                low, pltpu.roll(one, lanes // 2, 1), two
             )
     for copy in copies:
         copy.wait()
 
 
-def final_kernel(blocks, own_ref, bias_ref, *refs):
-    out_ref = refs[blocks]
-    for n in range(blocks):
-        width = refs[n].shape[1]
-        lanes = bias_ref.shape[1]
-        for t in range(0, width, lanes):
-            at = slice(n * width + t, n * width + t + lanes)
-            value = own_ref[at.start // lanes] + refs[n][:, t : t + lanes].astype(F32) + bias_ref[...]
-            out_ref[:, at] = value.astype(BF16)
+def final_kernel(couples, pieces, place_ref, own_ref, bias_ref, *refs):
+    count = couples * pieces
+    out_ref = refs[count]
+    lanes = bias_ref.shape[1]
+    length = out_ref.shape[0]
+    tiles = refs[0].shape[1] // lanes
+    for n in range(count):
+        first = lax.rem(place_ref[1] + n // pieces, couples) * (pieces * tiles) + n % pieces * tiles
+        for t in range(tiles):
+            value = own_ref[first + t] + refs[n][:, t * lanes : (t + 1) * lanes].astype(F32) + bias_ref[...]
+            out_ref[:, pl.ds(pl.multiple_of((first + t) * lanes, lanes), lanes)] = value.astype(BF16)
 
 
 COST = pl.CostEstimate(flops=0, bytes_accessed=0, transcendentals=0)
@@ -353,14 +392,32 @@
     e_width = second_weight.shape[1]
     bins = distance_weight.shape[1]
     axes = ("row", "col")
-    place = jnp.stack([lax.axis_index("col"), lax.axis_index("row")]).astype(jnp.int32)
+    row, col = lax.axis_index("row"), lax.axis_index("col")
+    place = jnp.stack([col // 2, row // 2, col, row, col % 2]).astype(jnp.int32)
+    couples = col_count // 2
+
+    def moved(value, target):
+        pairs = [
+            (r * col_count + c, target(r, c)[0] * col_count + target(r, c)[1])
+            for r in range(row_count)
+            for c in range(col_count)
+        ]
+        return lax.ppermute(value, axes, pairs)
 
     turned_index = alignment_index.T
-    embedded = pl.pallas_call(
-        embed_kernel,
-        out_shape=jax.ShapeDtypeStruct(alignment_state.shape, BF16),
+    other_index = moved(turned_index, lambda r, c: (r, c ^ 1))
+    other_state = moved(alignment_state, lambda r, c: (r, c ^ 1))
+    couple = (alignment_state.shape[0], 2 * alignment_state.shape[1])
+    kinds = alignment_table.shape[0]
+    group = min(alignment_index.shape[1], 256 // features)
+    own_embedded, wide_table = pl.pallas_call(
+        embed_own_kernel,
+        out_shape=(
+            jax.ShapeDtypeStruct(alignment_state.shape, BF16),
+            jax.ShapeDtypeStruct((group * kinds, group * features), BF16),
+        ),
         in_specs=[HBM] * 3,
-        out_specs=VMEM,
+        out_specs=(VMEM,) * 2,
         scratch_shapes=[
             pltpu.VMEM(alignment_state.shape, BF16),
             pltpu.VMEM(turned_index.shape, jnp.int32),
@@ -369,26 +426,26 @@
         ],
         compiler_params=params(4),
         cost_estimate=COST,
-        name="embed",
+        name="embed_own",
     )(*in_hbm(alignment_state, turned_index, alignment_table))
-
-    def moved(value, target):
-        pairs = [
-            (r * col_count + c, target(r, c)[0] * col_count + target(r, c)[1])
-            for r in range(row_count)
-            for c in range(col_count)
-        ]
-        return lax.ppermute(value, axes, pairs)
+    embedded = pl.pallas_call(
+        functools.partial(embed_couple_kernel, kinds),
+        out_shape=jax.ShapeDtypeStruct(couple, BF16),
+        in_specs=[SMEM] + [VMEM] * 4,
+        out_specs=VMEM,
+        compiler_params=params(4),
+        cost_estimate=COST,
+        name="embed_couple",
+    )(place, own_embedded, wide_table, other_state, other_index)
 
     rights = [
-        moved(embedded, lambda r, c, k=k: ((c - k) % row_count, r)) for k in range(col_count)
+        moved(embedded, lambda r, c, k=k: ((c - 2 * k) % row_count, r)) for k in range(couples)
     ]
     lefts = [embedded] + [
-        moved(embedded, lambda r, c, k=k: (r, (c - k) % col_count)) for k in range(1, col_count)
+        moved(embedded, lambda r, c, k=k: (r, (c - 2 * k) % col_count)) for k in range(1, couples)
     ]
 
     blocks = pair_block_mask.shape[0]
-    rows = length // blocks
     maps = jax.ShapeDtypeStruct((blocks, length, channels), F32)
     first_rows, masks, bases, outer_weight, pair_in, gate_up, down, gain, left_weight, right_weight, turned_distance, last = pl.pallas_call(
         weights_kernel,
@@ -446,33 +503,32 @@
         ),
     )
 
-    left_tiles, right_tiles = pl.pallas_call(
-        functools.partial(project_kernel, col_count, features),
-        out_shape=(
-            jax.ShapeDtypeStruct((2 * depth, 2 * length * c_width), BF16),
-            jax.ShapeDtypeStruct((e_width // 2 * length, 2 * depth), BF16),
-        ),
-        in_specs=[SMEM] + [VMEM] * (2 * col_count + 2),
-        out_specs=(VMEM,) * 2,
-        scratch_shapes=[pltpu.VMEM((depth, col_count * alignment_state.shape[1]), BF16)] * 2,
+    right_tiles = pl.pallas_call(
+        functools.partial(project_kernel, couples, features),
+        out_shape=jax.ShapeDtypeStruct((e_width // 2 * length, 2 * depth), BF16),
+        in_specs=[SMEM] + [VMEM] * (couples + 1),
+        out_specs=VMEM,
+        scratch_shapes=[pltpu.VMEM((depth, couples * couple[1]), BF16)],
         compiler_params=params(8),
         cost_estimate=COST,
         name="project",
-    )(place, *lefts, *rights, left_weight, right_weight)
-
-    pair_parts, dist_parts, mirror_parts = [], [], []
-    crossed = None
-    for block in range(blocks):
-        before = dist_parts[-1:]
-        if block % 2 == 0 and crossed is not None:
-            before = before + [crossed]
+    )(place, *rights, right_weight)
+
+    couple_rows = length // couples
+    pieces = 1
+    rows = couple_rows // pieces
+    pair_parts, dist_parts, crossed, mirror_parts = [], [], [], []
+    for n in range(couples * pieces):
+        before = dist_parts[-1:] if n else lefts[1:]
+        if n >= 2:
+            before = before + (crossed[-1:] if n % 2 == 0 else mirror_parts[n - 3 : n - 1])
         pair_part, dist_part = pl.pallas_call(
-            functools.partial(pair_kernel, block),
+            functools.partial(pair_kernel, n // pieces, n % pieces, couples),
             out_shape=(
                 jax.ShapeDtypeStruct((rows, length, channels), BF16),
                 jax.ShapeDtypeStruct((length, rows * bins), BF16),
             ),
-            in_specs=[VMEM] * 11 + [pl.BlockSpec(memory_space=pl.ANY)] * len(before),
+            in_specs=[SMEM] + [VMEM] * (12 + len(before)),
             out_specs=(VMEM,) * 2,
             scratch_shapes=[
                 pltpu.VMEM((rows // 2 * length, 2 * c_width * e_width), BF16),
@@ -482,7 +538,9 @@
             cost_estimate=COST,
             name="pairs",
         )(
-            left_tiles,
+            place,
+            lefts[n // pieces],
+            left_weight,
             right_tiles,
             pair_in,
             first_rows,
@@ -497,33 +555,33 @@
         )
         pair_parts.append(pair_part)
         dist_parts.append(dist_part)
-        if block % 2 == 0:
-            crossed = moved(dist_part, lambda r, c: (r, (c + col_count // 2) % col_count))
-            mirror_parts.append(moved(crossed, lambda r, c: ((c + col_count // 2) % col_count, r)))
+        if n % 2 == 0:
+            crossed.append(moved(dist_part, lambda r, c: (r, (c + col_count // 2) % col_count)))
+            mirror_parts.append(moved(crossed[-1], lambda r, c: ((c + col_count // 2) % col_count, r)))
         else:
             mirror_parts.append(moved(dist_part, lambda r, c: (c, r)))
     pair_out, own = pl.pallas_call(
-        functools.partial(own_kernel, blocks),
+        functools.partial(own_kernel, couples, pieces),
         out_shape=(
             jax.ShapeDtypeStruct(pair_state.shape, BF16),
             jax.ShapeDtypeStruct((length // 2, length, 2 * bins), F32),
         ),
-        in_specs=[VMEM] * (2 * blocks),
+        in_specs=[SMEM] + [VMEM] * (2 * len(pair_parts)),
         out_specs=(HBM, VMEM),
-        scratch_shapes=[pltpu.SemaphoreType.DMA((blocks,))],
+        scratch_shapes=[pltpu.SemaphoreType.DMA((len(pair_parts),))],
         compiler_params=params(8),
         cost_estimate=COST,
         name="own",
-    )(*pair_parts, *dist_parts)
+    )(place, *pair_parts, *dist_parts)
     distogram = pl.pallas_call(
-        functools.partial(final_kernel, blocks),
+        functools.partial(final_kernel, couples, pieces),
         out_shape=jax.ShapeDtypeStruct((length, length * bins), BF16),
-        in_specs=[VMEM] * (blocks + 2),
+        in_specs=[SMEM] + [VMEM] * (len(mirror_parts) + 2),
         out_specs=VMEM,
         compiler_params=params(8),
         cost_estimate=COST,
         name="final",
-    )(own, last, *mirror_parts)
+    )(place, own, last, *mirror_parts)
     return pair_out, distogram
 
 

time: 57.7 us -> 49 us (0.85)
  starting transfers between devices: 20.5 us -> 9.52 us
  waiting for transfers between devices: 14.5 us -> 18.3 us
  Pallas kernels: 21.6 us -> 20.1 us
    ppermute x13 -> x8, starting transfers between devices: 20.5 us -> 9.52 us  [moved(): return lax.ppermute(value, axes, pairs)]
    ppermute x13 -> x8, waiting for transfers between devices: 14.5 us -> 18.3 us  [moved(): return lax.ppermute(value, axes, pairs)]
    pallas_call x8 -> x7, Pallas kernels: 19.1 us -> 17.5 us  [the longest x2 11 us: local(): pl.pallas_call(functools.partial(pair_kernel, n // pieces, n % pieces, co...]
  transfers between devices with their start and end apart: 13 -> 8, of which waited for: 5 -> 6; matrix products, arithmetic and copies ran while one was open for 0% -> 0% of each run, Pallas kernels for 19% -> 25%
where the time goes in v3:
time: 49 us; the launch traced here: 48.7 us
  Pallas kernels  20.1 us (41%)
  waiting for transfers between devices  18.3 us (37%)
  starting transfers between devices  9.52 us (19%)
  between operations  0.75 us (2%)
    ppermute x8, waiting for transfers between devices, moved(): return lax.ppermute(value, axes, pairs)  18.3 us
    pallas_call x2, Pallas kernels, local(): pl.pallas_call(functools.partial(pair_kernel, n // pieces, n % pieces, co...  11 us
    ppermute x8, starting transfers between devices, moved(): return lax.ppermute(value, axes, pairs)  9.52 us
    pallas_call x1, Pallas kernels, local(): pl.pallas_call(weights_kernel, out_shape=(jax.ShapeDtypeStruct((length, c...  2.52 us
    pallas_call x1, Pallas kernels, local(): pl.pallas_call(functools.partial(own_kernel, couples, pieces), out_shape=...  1.78 us
    pallas_call x1, Pallas kernels, local(): pl.pallas_call(functools.partial(final_kernel, couples, pieces), out_shap...  1.5 us
    pallas_call x1, Pallas kernels, local(): pl.pallas_call(embed_own_kernel, out_shape=(jax.ShapeDtypeStruct(alignmen...  1.37 us
    pallas_call x1, Pallas kernels, local(): pl.pallas_call(functools.partial(project_kernel, couples, features), out_...  1 us
  transfers between devices with their start and end apart: 8, of which 6 were waited for; matrix products, arithmetic and copies ran while one was open for 0% of the time, Pallas kernels for 25%

profile of v3, /device:TPU:2, one launch (start us, length us, event | category | flops | bytes accessed | tf_op | source)
XLA Modules:
  0.0 48.7 jit_solution(2588088346771503012)
XLA Ops:
  0.6 0.1 collective-permute-start
  0.7 0.5 %collective-permute-start.1 = (s32[16,64]{1,0:T(8,128)}, s32[16,64]{1,0:T(8,128)S(1)}, u32[]{:S(2)}, u32[]{:S(2)}) collective-permute-start(s32[16,64]{1,0:T(8,128)} %bitcast.12), channel_id=1, source_target_pairs={{0,1},{1,0},{2,3},{3,2},{4,5},{5,4},{6,7},{7,6},{8,9},{9,8},{10,11... | collective-permute-start | bytes 12296 | tf_op jit(solution)/shard_map/ppermute | solution.py:405
  1.2 1.4 %embed_own.1 = (bf16[64,512]{1,0:T(8,128)(2,1)S(1)}, bf16[256,256]{1,0:T(8,128)(2,1)S(1)}) custom-call(bf16[64,512]{1,0:T(8,128)(2,1)} %state_hbm.1, s32[16,64]{1,0:T(8,128)} %bitcast.13, bf16[32,32]{1,0:T(8,128)(2,1)} %table_hbm.1), custom_call_target="tpu_custom_call" | custom-call | tf_op jit(solution)/shard_map/embed_own/pallas_call | solution.py:413
  2.6 0.1 stack.23.place_ref
  2.7 0.0 collective-permute-done.1.index_ref
  2.7 0.9 %embed_couple.1.left_ref = bf16[64,1024]{1,0:T(8,128)(2,1)S(1)} custom-call(s32[5]{0:T(128)S(1)} %stack.23.place_ref, bf16[64,512]{1,0:T(8,128)(2,1)S(1)} %get-tuple-element.22.own_ref, bf16[256,256]{1,0:T(8,128)(2,1)S(1)} %get-tuple-element.23.wide_ref, bf16[64,512]{1,0:T(8,128)(2,1)S(1)} %collective-permute-done.state_ref, ...), custom_call_target="tpu_custom_call" | custom-call | tf_op jit(solution)/shard_map/embed_couple/pallas_call | solution.py:431
  3.6 0.1 collective-permute-start.3
  3.6 5.9 %collective-permute-start.2 = (bf16[64,1024]{1,0:T(8,128)(2,1)S(1)}, bf16[64,1024]{1,0:T(8,128)(2,1)S(1)}, u32[]{:S(2)}, u32[]{:S(2)}) collective-permute-start(bf16[64,1024]{1,0:T(8,128)(2,1)S(1)} %embed_couple.1.left_ref), channel_id=1, source_target_pairs={{0,0},{1,4},{2,8},{3,12},{4,1},{5,5},{6,9},{7,13},{8,2},{9,6},{10,... | collective-permute-start | bytes 393224 | tf_op jit(solution)/shard_map/ppermute | solution.py:405
  9.6 0.1 collective-permute-start.4
  9.7 2.5 %weights.1 = (f32[64,128]{1,0:T(8,128)S(1)}, f32[4,64,128]{2,1,0:T(8,128)S(1)}, f32[4,64,128]{2,1,0:T(8,128)S(1)}, bf16[2048,256]{1,0:T(8,128)(2,1)S(1)}, bf16[6...) custom-call(s32[5]{0:T(128)S(1)} %stack.23.place_ref, ...), custom_call_target="tpu_custom_call" | custom-call | tf_op jit(solution)/shard_map/weights/pallas_call | solution.py:450
  12.2 1.1 %collective-permute-done.3.refs_1_ = bf16[64,1024]{1,0:T(8,128)(2,1)S(1)} collective-permute-done((bf16[64,1024]{1,0:T(8,128)(2,1)S(1)}, bf16[64,1024]{1,0:T(8,128)(2,1)S(1)}, u32[]{:S(2)}, u32[]{:S(2)}) %collective-permute-start.3) | collective-permute-done | bytes 131104 | tf_op jit(solution)/shard_map/ppermute | solution.py:405
  13.2 3.3 %collective-permute-done.2.refs_0_ = bf16[64,1024]{1,0:T(8,128)(2,1)S(1)} collective-permute-done((bf16[64,1024]{1,0:T(8,128)(2,1)S(1)}, bf16[64,1024]{1,0:T(8,128)(2,1)S(1)}, u32[]{:S(2)}, u32[]{:S(2)}) %collective-permute-start.2) | collective-permute-done | bytes 131104 | tf_op jit(solution)/shard_map/ppermute | solution.py:405
  16.5 1.0 %project.1.right_ref = bf16[1024,128]{1,0:T(8,128)(2,1)S(1)} custom-call(s32[5]{0:T(128)S(1)} %stack.23.place_ref, bf16[64,1024]{1,0:T(8,128)(2,1)S(1)} %collective-permute-done.2.refs_0_, bf16[64,1024]{1,0:T(8,128)(2,1)S(1)} %collective-permute-done.3.refs_1_, bf16[256,256]{1,0:T(8,128)(2,1)S(1)} %get-tuple-element.25.refs_2_), custom_call_target="tpu_custom_call" | custom-call | tf_op jit(solution)/shard_map/project/pallas_call | solution.py:506
  17.5 0.7 %collective-permute-done.4.rest_0_.left_ref = bf16[64,1024]{1,0:T(8,128)(2,1)S(1)} collective-permute-done((bf16[64,1024]{1,0:T(8,128)(2,1)S(1)}, bf16[64,1024]{1,0:T(8,128)(2,1)S(1)}, u32[]{:S(2)}, u32[]{:S(2)}) %collective-permute-start.4) | collective-permute-done | bytes 131104 | tf_op jit(solution)/shard_map/ppermute | solution.py:405
  18.2 5.5 %pairs.2 = (bf16[32,64,128]{2,1,0:T(8,128)(2,1)S(1)}, bf16[64,2048]{1,0:T(8,128)(2,1)S(1)}) custom-call(s32[5]{0:T(128)S(1)} %stack.23.place_ref, bf16[64,1024]{1,0:T(8,128)(2,1)S(1)} %embed_couple.1.left_ref, bf16[256,512]{1,0:T(8,128)(2,1)S(1)} %get-tuple-element.24.left_weight_ref, bf16[1024,128]{1,0:T(8,128)(2,1)S(1)} %project.1.right_ref, ...), custom_call_target="tpu_custom_call" | custom-call | tf_op jit(solution)/shard_map/pairs/pallas_call | solution.py:525
  23.7 0.1 collective-permute-start.5
  23.8 5.5 %pairs.3 = (bf16[32,64,128]{2,1,0:T(8,128)(2,1)S(1)}, bf16[64,2048]{1,0:T(8,128)(2,1)S(1)}) custom-call(s32[5]{0:T(128)S(1)} %stack.23.place_ref, bf16[64,1024]{1,0:T(8,128)(2,1)S(1)} %collective-permute-done.4.rest_0_.left_ref, bf16[256,512]{1,0:T(8,128)(2,1)S(1)} %get-tuple-element.24.left_weight_ref, bf16[1024,128]{1,0:T(8,128)(2,1)S(1)} %project.1.right_ref, ...), custom_call_target="tpu_custom_call" | custom-call | tf_op jit(solution)/shard_map/pairs/pallas_call | solution.py:525
  29.3 2.5 %collective-permute-start.7 = (bf16[64,2048]{1,0:T(8,128)(2,1)S(1)}, bf16[64,2048]{1,0:T(8,128)(2,1)S(1)}, u32[]{:S(2)}, u32[]{:S(2)}) collective-permute-start(bf16[64,2048]{1,0:T(8,128)(2,1)S(1)} %get-tuple-element.38.refs_3_), channel_id=1, source_target_pairs={{0,0},{1,4},{2,8},{3,12},{4,1},{5,5},{6,9},{7,13},{8,2},{9,6},{10,... | collective-permute-start | bytes 786440 | tf_op jit(solution)/shard_map/ppermute | solution.py:405
  31.9 0.1 collective-permute-done.5
  32.0 0.3 collective-permute-start.6
  32.3 1.8 %own.1 = (bf16[64,64,128]{2,1,0:T(8,128)(2,1)}, f32[32,64,128]{2,1,0:T(8,128)S(1)}) custom-call(s32[5]{0:T(128)S(1)} %stack.23.place_ref, bf16[32,64,128]{2,1,0:T(8,128)(2,1)S(1)} %get-tuple-element.35.refs_0_, bf16[32,64,128]{2,1,0:T(8,128)(2,1)S(1)} %get-tuple-element.37.refs_1_, bf16[64,2048]{1,0:T(8,128)(2,1)S(1)} %get-tuple-element.36.rest_0_.refs_2_, ...), custom_call_target="tpu_custom_call" | custom-call | tf_op jit(solution)/shard_map/own/pallas_call | solution.py:563
  34.0 11.4 %collective-permute-done.7.refs_1_ = bf16[64,2048]{1,0:T(8,128)(2,1)S(1)} collective-permute-done((bf16[64,2048]{1,0:T(8,128)(2,1)S(1)}, bf16[64,2048]{1,0:T(8,128)(2,1)S(1)}, u32[]{:S(2)}, u32[]{:S(2)}) %collective-permute-start.7) | collective-permute-done | bytes 262176 | tf_op jit(solution)/shard_map/ppermute | solution.py:405
  45.5 1.8 %collective-permute-done.6.refs_0_ = bf16[64,2048]{1,0:T(8,128)(2,1)S(1)} collective-permute-done((bf16[64,2048]{1,0:T(8,128)(2,1)S(1)}, bf16[64,2048]{1,0:T(8,128)(2,1)S(1)}, u32[]{:S(2)}, u32[]{:S(2)}) %collective-permute-start.6) | collective-permute-done | bytes 262176 | tf_op jit(solution)/shard_map/ppermute | solution.py:405
  47.2 1.5 %final.1 = bf16[64,4096]{1,0:T(8,128)(2,1)} custom-call(s32[5]{0:T(128)S(1)} %stack.23.place_ref, f32[32,64,128]{2,1,0:T(8,128)S(1)} %get-tuple-element.40.own_ref, f32[1,128]{1,0:T(1,128)S(1)} %get-tuple-element.41.bias_ref, bf16[64,2048]{1,0:T(8,128)(2,1)S(1)} %collective-permute-done.6.refs_0_, bf16[64,2048]{1,0:T(8,128)(2,1)S(1)} %collective-permute-done.7.refs_1_), custom_call_target="tpu_custom_call" | custom-call | tf_op jit(solution)/shard_map/final/pallas_call | solution.py:576
  (1 shorter events, 0.0 us)
Async XLA Ops:
  0.6 2.1 %collective-permute-start = (bf16[64,512]{1,0:T(8,128)(2,1)}, bf16[64,512]{1,0:T(8,128)(2,1)S(1)}, u32[]{:S(2)}, u32[]{:S(2)}) collective-permute-start(bf16[64,512]{1,0:T(8,128)(2,1)} %state_hbm.1), channel_id=1, source_target_pairs={{0,1},{1,0},{2,3},{3,2},{4,5},{5,4},{6,7},{7,6},{8,9},{9,8},{10,11... | collective-permute-start | bytes 196616 | tf_op jit(solution)/shard_map/ppermute | solution.py:405
  0.7 2.0 %collective-permute-start.1 = (s32[16,64]{1,0:T(8,128)}, s32[16,64]{1,0:T(8,128)S(1)}, u32[]{:S(2)}, u32[]{:S(2)}) collective-permute-start(s32[16,64]{1,0:T(8,128)} %bitcast.12), channel_id=1, source_target_pairs={{0,1},{1,0},{2,3},{3,2},{4,5},{5,4},{6,7},{7,6},{8,9},{9,8},{10,11... | collective-permute-start | bytes 12296 | tf_op jit(solution)/shard_map/ppermute | solution.py:405
  3.6 9.7 %collective-permute-start.3 = (bf16[64,1024]{1,0:T(8,128)(2,1)S(1)}, bf16[64,1024]{1,0:T(8,128)(2,1)S(1)}, u32[]{:S(2)}, u32[]{:S(2)}) collective-permute-start(bf16[64,1024]{1,0:T(8,128)(2,1)S(1)} %embed_couple.1.left_ref), channel_id=1, source_target_pairs={{0,8},{1,12},{2,0},{3,4},{4,9},{5,13},{6,1},{7,5},{8,10},{9,14},{1... | collective-permute-start | bytes 393224 | tf_op jit(solution)/shard_map/ppermute | solution.py:405
  3.6 12.9 %collective-permute-start.2 = (bf16[64,1024]{1,0:T(8,128)(2,1)S(1)}, bf16[64,1024]{1,0:T(8,128)(2,1)S(1)}, u32[]{:S(2)}, u32[]{:S(2)}) collective-permute-start(bf16[64,1024]{1,0:T(8,128)(2,1)S(1)} %embed_couple.1.left_ref), channel_id=1, source_target_pairs={{0,0},{1,4},{2,8},{3,12},{4,1},{5,5},{6,9},{7,13},{8,2},{9,6},{10,... | collective-permute-start | bytes 393224 | tf_op jit(solution)/shard_map/ppermute | solution.py:405
  9.6 8.6 %collective-permute-start.4 = (bf16[64,1024]{1,0:T(8,128)(2,1)S(1)}, bf16[64,1024]{1,0:T(8,128)(2,1)S(1)}, u32[]{:S(2)}, u32[]{:S(2)}) collective-permute-start(bf16[64,1024]{1,0:T(8,128)(2,1)S(1)} %embed_couple.1.left_ref), channel_id=1, source_target_pairs={{0,2},{1,3},{2,0},{3,1},{4,6},{5,7},{6,4},{7,5},{8,10},{9,11},{10,... | collective-permute-start | bytes 393224 | tf_op jit(solution)/shard_map/ppermute | solution.py:405
  23.7 8.2 %collective-permute-start.5 = (bf16[64,2048]{1,0:T(8,128)(2,1)S(1)}, bf16[64,2048]{1,0:T(8,128)(2,1)S(1)}, u32[]{:S(2)}, u32[]{:S(2)}) collective-permute-start(bf16[64,2048]{1,0:T(8,128)(2,1)S(1)} %get-tuple-element.36.rest_0_.refs_2_), channel_id=1, source_target_pairs={{0,2},{1,3},{2,0},{3,1},{4,6},{5,7},{6,4},{7,5},{8,10},{9,11},{10,... | collective-permute-start | bytes 786440 | tf_op jit(solution)/shard_map/ppermute | solution.py:405
  29.3 16.1 %collective-permute-start.7 = (bf16[64,2048]{1,0:T(8,128)(2,1)S(1)}, bf16[64,2048]{1,0:T(8,128)(2,1)S(1)}, u32[]{:S(2)}, u32[]{:S(2)}) collective-permute-start(bf16[64,2048]{1,0:T(8,128)(2,1)S(1)} %get-tuple-element.38.refs_3_), channel_id=1, source_target_pairs={{0,0},{1,4},{2,8},{3,12},{4,1},{5,5},{6,9},{7,13},{8,2},{9,6},{10,... | collective-permute-start | bytes 786440 | tf_op jit(solution)/shard_map/ppermute | solution.py:405
  32.0 15.3 %collective-permute-start.6 = (bf16[64,2048]{1,0:T(8,128)(2,1)S(1)}, bf16[64,2048]{1,0:T(8,128)(2,1)S(1)}, u32[]{:S(2)}, u32[]{:S(2)}) collective-permute-start(bf16[64,2048]{1,0:T(8,128)(2,1)S(1)} %collective-permute-done.5), channel_id=1, source_target_pairs={{0,8},{1,12},{2,0},{3,4},{4,9},{5,13},{6,1},{7,5},{8,10},{9,14},{1... | collective-permute-start | bytes 786440 | tf_op jit(solution)/shard_map/ppermute | solution.py:405

commit v4 on v3

--- a/solution.py
+++ b/solution.py
@@ -13,6 +13,7 @@
 NT = (((1,), (1,)), ((), ()))
 TN = (((0,), (0,)), ((), ()))
 MIB = 1024 * 1024
+ORDER = (1, 0)
 
 
 def iota(shape, dim):
@@ -75,16 +76,18 @@
     add_embedding(state_ref, index_ref, wide_ref[...], kinds, features, write)
 
 
-def embed_couple_kernel(kinds, place_ref, own_ref, wide_ref, state_ref, index_ref, out_ref):
+def embed_group_kernel(kinds, size, place_ref, own_ref, wide_ref, *refs):
+    states, indices, out_ref = refs[: size - 1], refs[size - 1 : 2 * size - 2], refs[2 * size - 2]
     width = own_ref.shape[1]
-    place = place_ref[4]
-    out_ref[:, pl.ds(pl.multiple_of(place * width, width), width)] = own_ref[...]
-    first = pl.multiple_of((1 - place) * width, width)
-
-    def write(at, value):
-        out_ref[:, pl.ds(pl.multiple_of(first + at, value.shape[1]), value.shape[1])] = value
-
-    add_embedding(state_ref, index_ref, wide_ref[...], kinds, width // index_ref.shape[0], write)
+    position = place_ref[4]
+    out_ref[:, pl.ds(pl.multiple_of(position * width, width), width)] = own_ref[...]
+    for n, (state, index) in enumerate(zip(states, indices, strict=True)):
+        first = lax.rem(position + n + 1, size) * width
+
+        def write(at, value, first=first):
+            out_ref[:, pl.ds(pl.multiple_of(first + at, value.shape[1]), value.shape[1])] = value
+
+        add_embedding(state, index, wide_ref[...], kinds, width // index.shape[0], write)
 
 
 def weights_kernel(
@@ -103,6 +106,7 @@
     gain_hbm,
     distance_hbm,
     last_hbm,
+    embedded_ref,
     first_out,
     mask_out,
     base_out,
@@ -115,6 +119,7 @@
     right_out,
     distance_out,
     last_out,
+    tiles_out,
     kinds_ref,
     first_ref,
     second_ref,
@@ -152,6 +157,7 @@
         lambda c: c % c_width,
         lambda r, c: r // features == 2 * (c // lanes) + c % (lanes // 2) // c_width,
     )
+    project_left(place_ref, [(0, embedded_ref)], left_out, tiles_out)
     e_width = right_ref.shape[1]
     turned = lax.dot_general(
         (iota((8 * e_width, e_width), 0) // 8 == iota((8 * e_width, e_width), 1)).astype(BF16),
@@ -197,39 +203,58 @@
         copy.wait()
 
 
-def project_kernel(couples, features, place_ref, *refs):
-    parts, weight_ref, right_out, whole = refs[:couples], refs[couples], refs[couples + 1], refs[couples + 2]
-    depth, width = parts[0].shape
-    for k, part in enumerate(parts):
-        couple = lax.rem(place_ref[1] + k, couples)
-        whole[:, pl.ds(pl.multiple_of(couple * width, width), width)] = part[...]
-    tokens = couples * width // features
+def project_left(place_ref, parts, weight_ref, out_ref):
+    group, columns = weight_ref.shape
+    depth, width = parts[0][1].shape
+    lanes = columns // 4
+    half = iota((depth, columns), 1) % lanes < lanes // 2
+    for k, part in parts:
+        first = lax.rem(place_ref[0] + k, 2) * (width // group * columns)
+        for t in range(width // group):
+            both = dot(part[:, t * group : (t + 1) * group], weight_ref[...])
+            at = pl.ds(pl.multiple_of(first + t * columns, columns), columns)
+            out_ref[0:depth, at] = jnp.where(half, both, 0.0).astype(BF16)
+            out_ref[depth : 2 * depth, at] = jnp.where(half, 0.0, both).astype(BF16)
+
+
+def project_right(part_ref, weight_ref, out_ref):
+    depth, width = part_ref.shape
     group = weight_ref.shape[1]
+    tokens = width // group * 8
     low = iota((8, 2 * depth), 1) < depth
     for t in range(0, tokens // 8, 2):
         sides = []
         for u in (t, t + 1):
-            part = whole[:, u * group : (u + 1) * group]
+            part = part_ref[:, u * group : (u + 1) * group]
             twice = jnp.concatenate([part, part], axis=0)
             sides.append(lax.dot_general(weight_ref[...], twice, NT, preferred_element_type=F32))
         for g in range(weight_ref.shape[0] // 16):
             rows = [
                 jnp.where(low, s[16 * g : 16 * g + 8], s[16 * g + 8 : 16 * g + 16]) for s in sides
             ]
-            right_out[pl.ds(g * tokens + t * 8, 16), :] = jnp.concatenate(rows, axis=0).astype(BF16)
-
-
-def row_of(couple, couples, piece, rows, couple_rows):
-    return pl.multiple_of(lax.rem(couple, couples) * couple_rows + piece * rows, rows)
+            out_ref[pl.ds(g * tokens + t * 8, 16), :] = jnp.concatenate(rows, axis=0).astype(BF16)
+
+
+def project_both_kernel(
+    place_ref, other_ref, right_ref, left_weight_ref, right_weight_ref, left_in, left_out, right_out
+):
+    del left_in
+    project_right(right_ref, right_weight_ref, right_out)
+    project_left(place_ref, [(1, other_ref)], left_weight_ref, left_out)
+
+
+def project_right_kernel(right_ref, right_weight_ref, right_out):
+    project_right(right_ref, right_weight_ref, right_out)
+
+
+def half_of(place, k, size):
+    return pl.multiple_of(lax.rem(place + k, 2) * size, size)
 
 
 def pair_kernel(
     k,
-    piece,
-    couples,
     place_ref,
     left_ref,
-    left_weight_ref,
     right_ref,
     pair_ref,
     first_ref,
@@ -243,46 +268,39 @@
     *rest,
 ):
     pair_out, dist_out, outer, start = rest[-4:]
-    rows, length, channels = pair_out.shape
+    length, size, channels = pair_out.shape
     block_rows = length // mask_ref.shape[0]
-    first_row = row_of(place_ref[0] + k, couples, piece, rows, length // couples)
-    pairs = rows // 2
+    second = pl.ds(half_of(place_ref[1], k, size), size)
+    pairs = length // 2
     depth, lanes = right_ref.shape[1] // 2, right_ref.shape[1]
-    groups = right_ref.shape[0] // length
+    groups = right_ref.shape[0] // size
+    step = min(groups, 256 // size)
     hid = down_ref.shape[0]
     bins = distance_ref.shape[0] // 2
-    group, columns = left_weight_ref.shape
-    half = iota((depth, columns), 1) % lanes < lanes // 2
-    weights = []
-    for t in range(rows // 8):
-        at = (piece * rows // 8 + t) * group
-        both = dot(left_ref[:, at : at + group], left_weight_ref[...])
-        weights.append(
-            jnp.concatenate([jnp.where(half, both, 0.0), jnp.where(half, 0.0, both)], axis=0).astype(BF16)
-        )
     for p in range(0, pairs, 2):
-        weight = weights[p // 4][:, p % 4 * lanes : (p % 4 + 2) * lanes]
-        for g in range(0, groups, 4):
-            got = dot(right_ref[g * length : (g + 4) * length, :], weight).astype(BF16)
+        weight = left_ref[:, p * lanes : (p + 2) * lanes]
+        for g in range(0, groups, step):
+            got = dot(right_ref[g * size : (g + step) * size, :], weight).astype(BF16)
             for q in range(2):
-                for h in range(4):
-                    outer[(p + q) * length : (p + q + 1) * length, (g + h) * lanes : (g + h + 1) * lanes] = got[
-                        h * length : (h + 1) * length, q * lanes : (q + 1) * lanes
+                for h in range(step):
+                    outer[(p + q) * size : (p + q + 1) * size, (g + h) * lanes : (g + h + 1) * lanes] = got[
+                        h * size : (h + 1) * size, q * lanes : (q + 1) * lanes
                     ]
-    half = outer.shape[0] // 2
-    update = [dot(outer[n * half : (n + 1) * half], outer_ref[...]) for n in range(2)]
-    first = first_ref[pl.ds(first_row, rows), :]
+    part_rows = max(size, outer.shape[0] // 8)
+    update = [
+        dot(outer[n : n + part_rows], outer_ref[...]) for n in range(0, outer.shape[0], part_rows)
+    ]
     for p in range(pairs):
-        block = lax.div(first_row + 2 * p, block_rows)
-        mask = mask_ref[block] * (1.0 / depth)
-        base = base_ref[block]
-        at = p * length % half
-        part = update[p * length // half][at : at + length]
+        block = 2 * p // block_rows
+        mask = mask_ref[block, second, :] * (1.0 / depth)
+        base = base_ref[block, second, :]
+        at = p * size % part_rows
+        part = update[p * size // part_rows][at : at + size]
         for q in range(2):
             i = 2 * p + q
-            start[q, p * length : (p + 1) * length, :] = (
-                pair_ref[first_row + i].astype(F32)
-                + (first[i : i + 1, :] + base)
+            start[q, p * size : (p + 1) * size, :] = (
+                pair_ref[i, second, :].astype(F32)
+                + (first_ref[i : i + 1, :] + base)
                 + mask * part[:, q * channels : (q + 1) * channels]
             )
     half = min(start.shape[1], 512)
@@ -299,55 +317,59 @@
     result = [start[q].astype(BF16) for q in range(2)]
     for p in range(pairs):
         for q in range(2):
-            pair_out[2 * p + q] = result[q][p * length : (p + 1) * length]
+            pair_out[2 * p + q] = result[q][p * size : (p + 1) * size]
     dist = lax.dot_general(
         jnp.concatenate(result, axis=1), distance_ref[...], NT, preferred_element_type=F32
     ).astype(BF16)
     for p in range(pairs):
-        dist_out[:, 2 * p * bins : 2 * (p + 1) * bins] = dist[p * length : (p + 1) * length]
-
-
-def own_kernel(couples, pieces, place_ref, *refs):
-    count = couples * pieces
+        dist_out[:, 2 * p * bins : 2 * (p + 1) * bins] = dist[p * size : (p + 1) * size]
+
+
+def own_kernel(order, place_ref, *refs):
+    count = len(order)
     parts, dists = refs[:count], refs[count : 2 * count]
     pair_out, own_ref, sems = refs[2 * count :]
-    rows, length, _ = parts[0].shape
-    firsts = [
-        row_of(place_ref[0] + n // pieces, couples, n % pieces, rows, length // couples)
-        for n in range(count)
-    ]
-    copies = fetch(parts, [pair_out.at[pl.ds(first, rows)] for first in firsts], sems)
-    pairs = rows // 2
+    length, size, _ = parts[0].shape
+    firsts = [half_of(place_ref[1], k, size) for k in order]
+    copies = fetch(parts, [pair_out.at[:, pl.ds(first, size)] for first in firsts], sems)
+    pairs = length // 2
     lanes = dists[0].shape[1] // pairs
     low = iota((pairs, lanes), 1) < lanes // 2
-    for first, dist in zip(firsts, dists, strict=True):
+    for k, dist in zip(order, dists, strict=True):
+        first = half_of(place_ref[1], k, size // 2)
         tiles = jnp.stack([dist[:, p * lanes : (p + 1) * lanes].astype(F32) for p in range(pairs)])
         turned = jnp.swapaxes(tiles, 0, 1)
-        for j in range(0, length, 2):
+        for j in range(0, size, 2):
             one, two = turned[j], turned[j + 1]
-            own_ref[j // 2, pl.ds(first, pairs, stride=2), :] = jnp.where(
+            own_ref[first + j // 2, pl.ds(0, pairs, stride=2), :] = jnp.where(
                 low, one, pltpu.roll(two, lanes // 2, 1)
             )
-            own_ref[j // 2, pl.ds(first + 1, pairs, stride=2), :] = jnp.where(
+            own_ref[first + j // 2, pl.ds(1, pairs, stride=2), :] = jnp.where(
                 low, pltpu.roll(one, lanes // 2, 1), two
             )
     for copy in copies:
         copy.wait()
 
 
-def final_kernel(couples, pieces, place_ref, own_ref, bias_ref, *refs):
-    count = couples * pieces
-    out_ref = refs[count]
+def final_kernel(order, place_ref, own_ref, bias_ref, *refs):
+    out_ref = refs[len(order)]
     lanes = bias_ref.shape[1]
-    length = out_ref.shape[0]
-    tiles = refs[0].shape[1] // lanes
-    for n in range(count):
-        first = lax.rem(place_ref[1] + n // pieces, couples) * (pieces * tiles) + n % pieces * tiles
-        for t in range(tiles):
-            value = own_ref[first + t] + refs[n][:, t * lanes : (t + 1) * lanes].astype(F32) + bias_ref[...]
-            out_ref[:, pl.ds(pl.multiple_of((first + t) * lanes, lanes), lanes)] = value.astype(BF16)
-
-
+
+    def write(swapped):
+        for k, part in zip(order, refs, strict=False):
+            size, width = part.shape
+            first = (k + swapped) % 2 * size
+            rows = slice(first, first + size)
+            for t in range(width // lanes):
+                at = slice(t * lanes, (t + 1) * lanes)
+                value = own_ref[t, rows, :] + part[:, at].astype(F32) + bias_ref[...]
+                out_ref[rows, at] = value.astype(BF16)
+
+    pl.when(place_ref[0] == 0)(functools.partial(write, 0))
+    pl.when(place_ref[0] == 1)(functools.partial(write, 1))
+
+
+PAIR_COST = pl.CostEstimate(flops=5_000_000_000, bytes_accessed=16_000_000, transcendentals=0)
 COST = pl.CostEstimate(flops=0, bytes_accessed=0, transcendentals=0)
 
 
@@ -393,8 +415,8 @@
     bins = distance_weight.shape[1]
     axes = ("row", "col")
     row, col = lax.axis_index("row"), lax.axis_index("col")
-    place = jnp.stack([col // 2, row // 2, col, row, col % 2]).astype(jnp.int32)
-    couples = col_count // 2
+    size = col_count // 2
+    place = jnp.stack([col // size, row // size, col, row, col % size]).astype(jnp.int32)
 
     def moved(value, target):
         pairs = [
@@ -404,10 +426,12 @@
         ]
         return lax.ppermute(value, axes, pairs)
 
+    def neighbour(value, k):
+        return moved(value, lambda r, c: (r, c - c % size + (c - k) % size))
+
     turned_index = alignment_index.T
-    other_index = moved(turned_index, lambda r, c: (r, c ^ 1))
-    other_state = moved(alignment_state, lambda r, c: (r, c ^ 1))
-    couple = (alignment_state.shape[0], 2 * alignment_state.shape[1])
+    other_indices = [neighbour(turned_index, k) for k in range(1, size)]
+    other_states = [neighbour(alignment_state, k) for k in range(1, size)]
     kinds = alignment_table.shape[0]
     group = min(alignment_index.shape[1], 256 // features)
     own_embedded, wide_table = pl.pallas_call(
@@ -429,25 +453,38 @@
         name="embed_own",
     )(*in_hbm(alignment_state, turned_index, alignment_table))
     embedded = pl.pallas_call(
-        functools.partial(embed_couple_kernel, kinds),
-        out_shape=jax.ShapeDtypeStruct(couple, BF16),
-        in_specs=[SMEM] + [VMEM] * 4,
+        functools.partial(embed_group_kernel, kinds, size),
+        out_shape=jax.ShapeDtypeStruct((depth, size * alignment_state.shape[1]), BF16),
+        in_specs=[SMEM] + [VMEM] * (2 * size),
         out_specs=VMEM,
         compiler_params=params(4),
         cost_estimate=COST,
-        name="embed_couple",
-    )(place, own_embedded, wide_table, other_state, other_index)
-
-    rights = [
-        moved(embedded, lambda r, c, k=k: ((c - 2 * k) % row_count, r)) for k in range(couples)
-    ]
-    lefts = [embedded] + [
-        moved(embedded, lambda r, c, k=k: (r, (c - 2 * k) % col_count)) for k in range(1, couples)
-    ]
+        name="embed_group",
+    )(place, own_embedded, wide_table, *other_states, *other_indices)
+
+    rights = {
+        k: moved(embedded, lambda r, c, k=k: ((c - size * k) % row_count, r)) for k in ORDER
+    }
+    other = moved(embedded, lambda r, c: (r, (c + size) % col_count))
 
     blocks = pair_block_mask.shape[0]
     maps = jax.ShapeDtypeStruct((blocks, length, channels), F32)
-    first_rows, masks, bases, outer_weight, pair_in, gate_up, down, gain, left_weight, right_weight, turned_distance, last = pl.pallas_call(
+    left_shape = jax.ShapeDtypeStruct((2 * depth, 2 * length * c_width), BF16)
+    (
+        first_rows,
+        masks,
+        bases,
+        outer_weight,
+        pair_in,
+        gate_up,
+        down,
+        gain,
+        left_weight,
+        right_weight,
+        turned_distance,
+        last,
+        left_tiles,
+    ) = pl.pallas_call(
         weights_kernel,
         out_shape=(
             jax.ShapeDtypeStruct((length, channels), F32),
@@ -462,9 +499,10 @@
             jax.ShapeDtypeStruct((8 * e_width, 8 * features), BF16),
             jax.ShapeDtypeStruct((2 * bins, 2 * channels), BF16),
             jax.ShapeDtypeStruct((1, 2 * bins), F32),
+            left_shape,
         ),
-        in_specs=[SMEM] + [HBM] * 14,
-        out_specs=(VMEM,) * 12,
+        in_specs=[SMEM] + [HBM] * 14 + [VMEM],
+        out_specs=(VMEM,) * 13,
         scratch_shapes=[
             pltpu.VMEM((1, token_kinds.shape[0]), jnp.int32),
             pltpu.VMEM(first_type_table.shape, BF16),
@@ -501,46 +539,53 @@
             distance_weight.T,
             distance_bias.reshape(1, -1),
         ),
-    )
-
-    right_tiles = pl.pallas_call(
-        functools.partial(project_kernel, couples, features),
-        out_shape=jax.ShapeDtypeStruct((e_width // 2 * length, 2 * depth), BF16),
-        in_specs=[SMEM] + [VMEM] * (couples + 1),
-        out_specs=VMEM,
-        scratch_shapes=[pltpu.VMEM((depth, couples * couple[1]), BF16)],
-        compiler_params=params(8),
-        cost_estimate=COST,
-        name="project",
-    )(place, *rights, right_weight)
-
-    couple_rows = length // couples
-    pieces = 1
-    rows = couple_rows // pieces
-    pair_parts, dist_parts, crossed, mirror_parts = [], [], [], []
-    for n in range(couples * pieces):
-        before = dist_parts[-1:] if n else lefts[1:]
-        if n >= 2:
-            before = before + (crossed[-1:] if n % 2 == 0 else mirror_parts[n - 3 : n - 1])
+        embedded,
+    )
+
+    half = length // 2
+    right_shape = jax.ShapeDtypeStruct((e_width // 2 * half, 2 * depth), BF16)
+    pair_parts, dist_parts, mirror_parts = [], [], []
+    for n, k in enumerate(ORDER):
+        if n == 0:
+            left_tiles, right_tiles = pl.pallas_call(
+                project_both_kernel,
+                out_shape=(left_shape, right_shape),
+                in_specs=[SMEM] + [VMEM] * 5,
+                out_specs=(VMEM,) * 2,
+                input_output_aliases={5: 0},
+                compiler_params=params(4),
+                cost_estimate=COST,
+                name="project_both",
+            )(place, other, rights[k], left_weight, right_weight, left_tiles)
+        else:
+            right_tiles = pl.pallas_call(
+                project_right_kernel,
+                out_shape=right_shape,
+                in_specs=[VMEM] * 2,
+                out_specs=VMEM,
+                compiler_params=params(4),
+                cost_estimate=COST,
+                name="project_right",
+            )(rights[k], right_weight)
+        before = dist_parts[-1:]
         pair_part, dist_part = pl.pallas_call(
-            functools.partial(pair_kernel, n // pieces, n % pieces, couples),
+            functools.partial(pair_kernel, k),
             out_shape=(
-                jax.ShapeDtypeStruct((rows, length, channels), BF16),
-                jax.ShapeDtypeStruct((length, rows * bins), BF16),
+                jax.ShapeDtypeStruct((length, half, channels), BF16),
+                jax.ShapeDtypeStruct((half, length * bins), BF16),
             ),
-            in_specs=[SMEM] + [VMEM] * (12 + len(before)),
+            in_specs=[SMEM] + [VMEM] * (11 + len(before)),
             out_specs=(VMEM,) * 2,
             scratch_shapes=[
-                pltpu.VMEM((rows // 2 * length, 2 * c_width * e_width), BF16),
-                pltpu.VMEM((2, rows // 2 * length, channels), F32),
+                pltpu.VMEM((length // 2 * half, 2 * c_width * e_width), BF16),
+                pltpu.VMEM((2, length // 2 * half, channels), F32),
             ],
-            compiler_params=params(16),
-            cost_estimate=COST,
+            compiler_params=params(24),
+            cost_estimate=PAIR_COST,
             name="pairs",
         )(
             place,
-            lefts[n // pieces],
-            left_weight,
+            left_tiles,
             right_tiles,
             pair_in,
             first_rows,
@@ -555,13 +600,13 @@
         )
         pair_parts.append(pair_part)
         dist_parts.append(dist_part)
-        if n % 2 == 0:
-            crossed.append(moved(dist_part, lambda r, c: (r, (c + col_count // 2) % col_count)))
-            mirror_parts.append(moved(crossed[-1], lambda r, c: ((c + col_count // 2) % col_count, r)))
+        if n == 0:
+            crossed = moved(dist_part, lambda r, c: (r, (c + size) % col_count))
+            mirror_parts.append(moved(crossed, lambda r, c: ((c + size) % col_count, r)))
         else:
             mirror_parts.append(moved(dist_part, lambda r, c: (c, r)))
     pair_out, own = pl.pallas_call(
-        functools.partial(own_kernel, couples, pieces),
+        functools.partial(own_kernel, ORDER),
         out_shape=(
             jax.ShapeDtypeStruct(pair_state.shape, BF16),
             jax.ShapeDtypeStruct((length // 2, length, 2 * bins), F32),
@@ -574,11 +619,11 @@
         name="own",
     )(place, *pair_parts, *dist_parts)
     distogram = pl.pallas_call(
-        functools.partial(final_kernel, couples, pieces),
+        functools.partial(final_kernel, ORDER),
         out_shape=jax.ShapeDtypeStruct((length, length * bins), BF16),
-        in_specs=[SMEM] + [VMEM] * (len(mirror_parts) + 2),
+        in_specs=[SMEM] + [VMEM] * 4,
         out_specs=VMEM,
-        compiler_params=params(8),
+        compiler_params=params(4),
         cost_estimate=COST,
         name="final",
     )(place, own, last, *mirror_parts)

time: 49 us -> 45 us (0.918)
  waiting for transfers between devices: 18.3 us -> 11.9 us
  starting transfers between devices: 9.52 us -> 12.5 us
  Pallas kernels: 20.1 us -> 19.6 us
    ppermute x8, waiting for transfers between devices: 18.3 us -> 11.9 us  [moved(): return lax.ppermute(value, axes, pairs)]
    ppermute x8, starting transfers between devices: 9.52 us -> 12.5 us  [moved(): return lax.ppermute(value, axes, pairs)]
    pallas_call x6 -> x7, Pallas kernels: 16.2 us -> 15.4 us  [the longest x2 10 us: local(): pl.pallas_call(functools.partial(pair_kernel, k), out_shape=(jax.ShapeDty...]
  transfers between devices with their start and end apart: 8 -> 8, of which waited for: 6 -> 3; matrix products, arithmetic and copies ran while one was open for 0% -> 0% of each run, Pallas kernels for 25% -> 38%
where the time goes in v4:
time: 45 us; the launch traced here: 44.8 us
  Pallas kernels  19.6 us (44%)
  starting transfers between devices  12.5 us (28%)
  waiting for transfers between devices  11.9 us (26%)
  between operations  0.77 us (2%)
    ppermute x8, starting transfers between devices, moved(): return lax.ppermute(value, axes, pairs)  12.5 us
    ppermute x8, waiting for transfers between devices, moved(): return lax.ppermute(value, axes, pairs)  11.9 us
    pallas_call x2, Pallas kernels, local(): pl.pallas_call(functools.partial(pair_kernel, k), out_shape=(jax.ShapeDty...  10 us
    pallas_call x1, Pallas kernels, local(): pl.pallas_call(weights_kernel, out_shape=(jax.ShapeDtypeStruct((length, c...  2.8 us
    pallas_call x1, Pallas kernels, local(): pl.pallas_call(functools.partial(own_kernel, ORDER), out_shape=(jax.Shape...  1.78 us
    pallas_call x1, Pallas kernels, local(): pl.pallas_call(functools.partial(final_kernel, ORDER), out_shape=jax.Shap...  1.48 us
    pallas_call x1, Pallas kernels, local(): pl.pallas_call(embed_own_kernel, out_shape=(jax.ShapeDtypeStruct(alignmen...  1.37 us
    pallas_call x1, Pallas kernels, local(): pl.pallas_call(project_both_kernel, out_shape=(left_shape, right_shape),...  0.98 us
  transfers between devices with their start and end apart: 8, of which 3 were waited for; matrix products, arithmetic and copies ran while one was open for 0% of the time, Pallas kernels for 38%

profile of v4, /device:TPU:2, one launch (start us, length us, event | category | flops | bytes accessed | tf_op | source)
XLA Modules:
  0.0 44.8 jit_solution(9121916830191435646)
XLA Ops:
  0.6 0.1 collective-permute-start
  0.7 0.5 %collective-permute-start.1 = (s32[16,64]{1,0:T(8,128)}, s32[16,64]{1,0:T(8,128)S(1)}, u32[]{:S(2)}, u32[]{:S(2)}) collective-permute-start(s32[16,64]{1,0:T(8,128)} %bitcast.12), channel_id=1, source_target_pairs={{0,1},{1,0},{2,3},{3,2},{4,5},{5,4},{6,7},{7,6},{8,9},{9,8},{10,11... | collective-permute-start | bytes 12296 | tf_op jit(solution)/shard_map/ppermute | solution.py:427
  1.2 1.4 %embed_own.1 = (bf16[64,512]{1,0:T(8,128)(2,1)S(1)}, bf16[256,256]{1,0:T(8,128)(2,1)S(1)}) custom-call(bf16[64,512]{1,0:T(8,128)(2,1)} %state_hbm.1, s32[16,64]{1,0:T(8,128)} %bitcast.13, bf16[32,32]{1,0:T(8,128)(2,1)} %table_hbm.1), custom_call_target="tpu_custom_call" | custom-call | tf_op jit(solution)/shard_map/embed_own/pallas_call | solution.py:437
  2.6 0.1 stack.23.place_ref
  2.7 0.0 collective-permute-done.1.refs_1_
  2.7 0.0 collective-permute-done.refs_0_
  2.7 0.9 %embed_group.1.embedded_ref = bf16[64,1024]{1,0:T(8,128)(2,1)S(1)} custom-call(s32[5]{0:T(128)S(1)} %stack.23.place_ref, bf16[64,512]{1,0:T(8,128)(2,1)S(1)} %get-tuple-element.25.own_ref, bf16[256,256]{1,0:T(8,128)(2,1)S(1)} %get-tuple-element.26.wide_ref, bf16[64,512]{1,0:T(8,128)(2,1)S(1)} %collective-permute-done.refs_0_, ...), custom_call_target="tpu_custom_call" | custom-call | tf_op jit(solution)/shard_map/embed_group/pallas_call | solution.py:455
  3.6 0.1 collective-permute-start.3
  3.6 3.1 %collective-permute-start.2 = (bf16[64,1024]{1,0:T(8,128)(2,1)S(1)}, bf16[64,1024]{1,0:T(8,128)(2,1)S(1)}, u32[]{:S(2)}, u32[]{:S(2)}) collective-permute-start(bf16[64,1024]{1,0:T(8,128)(2,1)S(1)} %embed_group.1.embedded_ref), channel_id=1, source_target_pairs={{0,2},{1,3},{2,0},{3,1},{4,6},{5,7},{6,4},{7,5},{8,10},{9,11},{10,... | collective-permute-start | bytes 393224 | tf_op jit(solution)/shard_map/ppermute | solution.py:427
  6.7 3.2 %collective-permute-start.4 = (bf16[64,1024]{1,0:T(8,128)(2,1)S(1)}, bf16[64,1024]{1,0:T(8,128)(2,1)S(1)}, u32[]{:S(2)}, u32[]{:S(2)}) collective-permute-start(bf16[64,1024]{1,0:T(8,128)(2,1)S(1)} %embed_group.1.embedded_ref), channel_id=1, source_target_pairs={{0,0},{1,4},{2,8},{3,12},{4,1},{5,5},{6,9},{7,13},{8,2},{9,6},{10,... | collective-permute-start | bytes 393224 | tf_op jit(solution)/shard_map/ppermute | solution.py:427
  9.9 2.8 %weights.1 = (f32[64,128]{1,0:T(8,128)S(1)}, f32[4,64,128]{2,1,0:T(8,128)S(1)}, f32[4,64,128]{2,1,0:T(8,128)S(1)}, bf16[2048,256]{1,0:T(8,128)(2,1)S(1)}, bf16[6...) custom-call(s32[5]{0:T(128)S(1)} %stack.23.place_ref, ...), custom_call_target="tpu_custom_call" | custom-call | tf_op jit(solution)/shard_map/weights/pallas_call | solution.py:487
  12.7 0.5 %collective-permute-done.3.right_ref = bf16[64,1024]{1,0:T(8,128)(2,1)S(1)} collective-permute-done((bf16[64,1024]{1,0:T(8,128)(2,1)S(1)}, bf16[64,1024]{1,0:T(8,128)(2,1)S(1)}, u32[]{:S(2)}, u32[]{:S(2)}) %collective-permute-start.3) | collective-permute-done | bytes 131104 | tf_op jit(solution)/shard_map/ppermute | solution.py:427
  13.2 0.0 collective-permute-done.2.other_ref
  13.2 1.0 %project_both.1 = (bf16[128,4096]{1,0:T(8,128)(2,1)S(1)}, bf16[512,128]{1,0:T(8,128)(2,1)S(1)}) custom-call(s32[5]{0:T(128)S(1)} %stack.23.place_ref, bf16[64,1024]{1,0:T(8,128)(2,1)S(1)} %collective-permute-done.2.other_ref, bf16[64,1024]{1,0:T(8,128)(2,1)S(1)} %collective-permute-done.3.right_ref, ...), custom_call_target="tpu_custom_call", output_to_operand_aliasing={{0}: (5, {})} | custom-call | tf_op jit(solution)/shard_map/project_both/pallas_call | solution.py:550
  14.2 5.0 %pairs.2 = (bf16[64,32,128]{2,1,0:T(8,128)(2,1)S(1)}, bf16[32,4096]{1,0:T(8,128)(2,1)S(1)}) custom-call(s32[5]{0:T(128)S(1)} %stack.23.place_ref, bf16[128,4096]{1,0:T(8,128)(2,1)S(1)} %get-tuple-element.30.left_ref, bf16[512,128]{1,0:T(8,128)(2,1)S(1)} %get-tuple-element.31.right_ref, bf16[64,64,128]{2,1,0:T(8,128)(2,1)S(1)} %get-tuple-element.32.pair_ref, ...), custom_call_target="tpu_custom_call" | custom-call | flops 5000000000 | bytes 16000000 | tf_op jit(solution)/shard_map/pairs/pallas_call | solution.py:571
  19.2 0.1 collective-permute-start.5
  19.3 0.3 project_right.1.right_ref
  19.6 5.0 %pairs.3 = (bf16[64,32,128]{2,1,0:T(8,128)(2,1)S(1)}, bf16[32,4096]{1,0:T(8,128)(2,1)S(1)}) custom-call(s32[5]{0:T(128)S(1)} %stack.23.place_ref, bf16[128,4096]{1,0:T(8,128)(2,1)S(1)} %get-tuple-element.30.left_ref, bf16[512,128]{1,0:T(8,128)(2,1)S(1)} %project_right.1.right_ref, bf16[64,64,128]{2,1,0:T(8,128)(2,1)S(1)} %get-tuple-element.32.pair_ref, ...), custom_call_target="tpu_custom_call" | custom-call | flops 5000000000 | bytes 16000000 | tf_op jit(solution)/shard_map/pairs/pallas_call | solution.py:571
  24.6 5.5 %collective-permute-start.7 = (bf16[32,4096]{1,0:T(8,128)(2,1)S(1)}, bf16[32,4096]{1,0:T(8,128)(2,1)S(1)}, u32[]{:S(2)}, u32[]{:S(2)}) collective-permute-start(bf16[32,4096]{1,0:T(8,128)(2,1)S(1)} %get-tuple-element.44.refs_3_), channel_id=1, source_target_pairs={{0,0},{1,4},{2,8},{3,12},{4,1},{5,5},{6,9},{7,13},{8,2},{9,6},{10,... | collective-permute-start | bytes 786440 | tf_op jit(solution)/shard_map/ppermute | solution.py:427
  30.2 0.1 collective-permute-start.6
  30.2 1.8 %own.1 = (bf16[64,64,128]{2,1,0:T(8,128)(2,1)}, f32[32,64,128]{2,1,0:T(8,128)S(1)}) custom-call(s32[5]{0:T(128)S(1)} %stack.23.place_ref, bf16[64,32,128]{2,1,0:T(8,128)(2,1)S(1)} %get-tuple-element.41.refs_0_, bf16[64,32,128]{2,1,0:T(8,128)(2,1)S(1)} %get-tuple-element.43.refs_1_, bf16[32,4096]{1,0:T(8,128)(2,1)S(1)} %get-tuple-element.42.rest_0_.refs_2_, ...), custom_call_target="tpu_custom_call" | custom-call | tf_op jit(solution)/shard_map/own/pallas_call | solution.py:608
  32.0 10.1 %collective-permute-done.7.refs_1_ = bf16[32,4096]{1,0:T(8,128)(2,1)S(1)} collective-permute-done((bf16[32,4096]{1,0:T(8,128)(2,1)S(1)}, bf16[32,4096]{1,0:T(8,128)(2,1)S(1)}, u32[]{:S(2)}, u32[]{:S(2)}) %collective-permute-start.7) | collective-permute-done | bytes 262176 | tf_op jit(solution)/shard_map/ppermute | solution.py:427
  42.1 1.2 %collective-permute-done.6.refs_0_ = bf16[32,4096]{1,0:T(8,128)(2,1)S(1)} collective-permute-done((bf16[32,4096]{1,0:T(8,128)(2,1)S(1)}, bf16[32,4096]{1,0:T(8,128)(2,1)S(1)}, u32[]{:S(2)}, u32[]{:S(2)}) %collective-permute-start.6) | collective-permute-done | bytes 262176 | tf_op jit(solution)/shard_map/ppermute | solution.py:427
  43.3 1.5 %final.1 = bf16[64,4096]{1,0:T(8,128)(2,1)} custom-call(s32[5]{0:T(128)S(1)} %stack.23.place_ref, f32[32,64,128]{2,1,0:T(8,128)S(1)} %get-tuple-element.46.own_ref, f32[1,128]{1,0:T(1,128)S(1)} %get-tuple-element.47.bias_ref, bf16[32,4096]{1,0:T(8,128)(2,1)S(1)} %collective-permute-done.6.refs_0_, bf16[32,4096]{1,0:T(8,128)(2,1)S(1)} %collective-permute-done.7.refs_1_), custom_call_target="tpu_custom_call" | custom-call | tf_op jit(solution)/shard_map/final/pallas_call | solution.py:621
  (2 shorter events, 0.0 us)
Async XLA Ops:
  0.6 2.1 %collective-permute-start = (bf16[64,512]{1,0:T(8,128)(2,1)}, bf16[64,512]{1,0:T(8,128)(2,1)S(1)}, u32[]{:S(2)}, u32[]{:S(2)}) collective-permute-start(bf16[64,512]{1,0:T(8,128)(2,1)} %state_hbm.1), channel_id=1, source_target_pairs={{0,1},{1,0},{2,3},{3,2},{4,5},{5,4},{6,7},{7,6},{8,9},{9,8},{10,11... | collective-permute-start | bytes 196616 | tf_op jit(solution)/shard_map/ppermute | solution.py:427
  0.7 2.0 %collective-permute-start.1 = (s32[16,64]{1,0:T(8,128)}, s32[16,64]{1,0:T(8,128)S(1)}, u32[]{:S(2)}, u32[]{:S(2)}) collective-permute-start(s32[16,64]{1,0:T(8,128)} %bitcast.12), channel_id=1, source_target_pairs={{0,1},{1,0},{2,3},{3,2},{4,5},{5,4},{6,7},{7,6},{8,9},{9,8},{10,11... | collective-permute-start | bytes 12296 | tf_op jit(solution)/shard_map/ppermute | solution.py:427
  3.6 9.7 %collective-permute-start.3 = (bf16[64,1024]{1,0:T(8,128)(2,1)S(1)}, bf16[64,1024]{1,0:T(8,128)(2,1)S(1)}, u32[]{:S(2)}, u32[]{:S(2)}) collective-permute-start(bf16[64,1024]{1,0:T(8,128)(2,1)S(1)} %embed_group.1.embedded_ref), channel_id=1, source_target_pairs={{0,8},{1,12},{2,0},{3,4},{4,9},{5,13},{6,1},{7,5},{8,10},{9,14},{1... | collective-permute-start | bytes 393224 | tf_op jit(solution)/shard_map/ppermute | solution.py:427
  3.6 9.6 %collective-permute-start.2 = (bf16[64,1024]{1,0:T(8,128)(2,1)S(1)}, bf16[64,1024]{1,0:T(8,128)(2,1)S(1)}, u32[]{:S(2)}, u32[]{:S(2)}) collective-permute-start(bf16[64,1024]{1,0:T(8,128)(2,1)S(1)} %embed_group.1.embedded_ref), channel_id=1, source_target_pairs={{0,2},{1,3},{2,0},{3,1},{4,6},{5,7},{6,4},{7,5},{8,10},{9,11},{10,... | collective-permute-start | bytes 393224 | tf_op jit(solution)/shard_map/ppermute | solution.py:427
  6.7 12.6 %collective-permute-start.4 = (bf16[64,1024]{1,0:T(8,128)(2,1)S(1)}, bf16[64,1024]{1,0:T(8,128)(2,1)S(1)}, u32[]{:S(2)}, u32[]{:S(2)}) collective-permute-start(bf16[64,1024]{1,0:T(8,128)(2,1)S(1)} %embed_group.1.embedded_ref), channel_id=1, source_target_pairs={{0,0},{1,4},{2,8},{3,12},{4,1},{5,5},{6,9},{7,13},{8,2},{9,6},{10,... | collective-permute-start | bytes 393224 | tf_op jit(solution)/shard_map/ppermute | solution.py:427
  19.2 10.9 %collective-permute-start.5 = (bf16[32,4096]{1,0:T(8,128)(2,1)S(1)}, bf16[32,4096]{1,0:T(8,128)(2,1)S(1)}, u32[]{:S(2)}, u32[]{:S(2)}) collective-permute-start(bf16[32,4096]{1,0:T(8,128)(2,1)S(1)} %get-tuple-element.42.rest_0_.refs_2_), channel_id=1, source_target_pairs={{0,2},{1,3},{2,0},{3,1},{4,6},{5,7},{6,4},{7,5},{8,10},{9,11},{10,... | collective-permute-start | bytes 786440 | tf_op jit(solution)/shard_map/ppermute | solution.py:427
  24.6 17.5 %collective-permute-start.7 = (bf16[32,4096]{1,0:T(8,128)(2,1)S(1)}, bf16[32,4096]{1,0:T(8,128)(2,1)S(1)}, u32[]{:S(2)}, u32[]{:S(2)}) collective-permute-start(bf16[32,4096]{1,0:T(8,128)(2,1)S(1)} %get-tuple-element.44.refs_3_), channel_id=1, source_target_pairs={{0,0},{1,4},{2,8},{3,12},{4,1},{5,5},{6,9},{7,13},{8,2},{9,6},{10,... | collective-permute-start | bytes 786440 | tf_op jit(solution)/shard_map/ppermute | solution.py:427
  30.2 13.2 %collective-permute-start.6 = (bf16[32,4096]{1,0:T(8,128)(2,1)S(1)}, bf16[32,4096]{1,0:T(8,128)(2,1)S(1)}, u32[]{:S(2)}, u32[]{:S(2)}) collective-permute-start(bf16[32,4096]{1,0:T(8,128)(2,1)S(1)} %collective-permute-done.5), channel_id=1, source_target_pairs={{0,8},{1,12},{2,0},{3,4},{4,9},{5,13},{6,1},{7,5},{8,10},{9,14},{1... | collective-permute-start | bytes 786440 | tf_op jit(solution)/shard_map/ppermute | solution.py:427

commit v5 on v4

--- a/solution.py
+++ b/solution.py
@@ -76,10 +76,10 @@
     add_embedding(state_ref, index_ref, wide_ref[...], kinds, features, write)
 
 
-def embed_group_kernel(kinds, size, place_ref, own_ref, wide_ref, *refs):
+def embed_group_kernel(kinds, size, own_ref, wide_ref, *refs):
     states, indices, out_ref = refs[: size - 1], refs[size - 1 : 2 * size - 2], refs[2 * size - 2]
     width = own_ref.shape[1]
-    position = place_ref[4]
+    position = lax.rem(lax.axis_index("col"), size)
     out_ref[:, pl.ds(pl.multiple_of(position * width, width), width)] = own_ref[...]
     for n, (state, index) in enumerate(zip(states, indices, strict=True)):
         first = lax.rem(position + n + 1, size) * width
@@ -91,7 +91,6 @@
 
 
 def weights_kernel(
-    place_ref,
     kinds_hbm,
     first_hbm,
     second_hbm,
@@ -157,7 +156,7 @@
         lambda c: c % c_width,
         lambda r, c: r // features == 2 * (c // lanes) + c % (lanes // 2) // c_width,
     )
-    project_left(place_ref, [(0, embedded_ref)], left_out, tiles_out)
+    project_left([(0, embedded_ref)], left_out, tiles_out)
     e_width = right_ref.shape[1]
     turned = lax.dot_general(
         (iota((8 * e_width, e_width), 0) // 8 == iota((8 * e_width, e_width), 1)).astype(BF16),
@@ -179,9 +178,9 @@
     kinds = kinds_ref[...]
     onehot = (iota((first_ref.shape[0], kinds.shape[1]), 0) == kinds).astype(BF16)
     rows[...] = lax.dot_general(onehot, first_ref[...], TN, preferred_element_type=F32)
-    first_out[...] = rows[pl.ds(pl.multiple_of(place_ref[3] * length, length), length), :]
+    first_out[...] = rows[pl.ds(pl.multiple_of(lax.axis_index("row") * length, length), length), :]
     rows[...] = lax.dot_general(onehot, second_ref[...], TN, preferred_element_type=F32)
-    second = rows[pl.ds(pl.multiple_of(place_ref[2] * length, length), length), :]
+    second = rows[pl.ds(pl.multiple_of(lax.axis_index("col") * length, length), length), :]
     blocks, columns = mask_ref.shape
     reach = (iota((length, columns), 0) // (length // columns) == iota((length, columns), 1)).astype(BF16)
     mask = lax.dot_general(
@@ -203,13 +202,13 @@
         copy.wait()
 
 
-def project_left(place_ref, parts, weight_ref, out_ref):
+def project_left(parts, weight_ref, out_ref):
     group, columns = weight_ref.shape
     depth, width = parts[0][1].shape
     lanes = columns // 4
     half = iota((depth, columns), 1) % lanes < lanes // 2
     for k, part in parts:
-        first = lax.rem(place_ref[0] + k, 2) * (width // group * columns)
+        first = half_of("col", k, width // group * columns)
         for t in range(width // group):
             both = dot(part[:, t * group : (t + 1) * group], weight_ref[...])
             at = pl.ds(pl.multiple_of(first + t * columns, columns), columns)
@@ -235,25 +234,22 @@
             out_ref[pl.ds(g * tokens + t * 8, 16), :] = jnp.concatenate(rows, axis=0).astype(BF16)
 
 
-def project_both_kernel(
-    place_ref, other_ref, right_ref, left_weight_ref, right_weight_ref, left_in, left_out, right_out
-):
+def project_left_kernel(other_ref, weight_ref, left_in, left_out):
     del left_in
+    project_left([(1, other_ref)], weight_ref, left_out)
+
+
+def project_right_kernel(right_ref, right_weight_ref, *rest):
+    right_out = rest[-1]
     project_right(right_ref, right_weight_ref, right_out)
-    project_left(place_ref, [(1, other_ref)], left_weight_ref, left_out)
-
-
-def project_right_kernel(right_ref, right_weight_ref, right_out):
-    project_right(right_ref, right_weight_ref, right_out)
-
-
-def half_of(place, k, size):
-    return pl.multiple_of(lax.rem(place + k, 2) * size, size)
+
+
+def half_of(axis, k, size):
+    return pl.multiple_of(lax.rem(lax.axis_index(axis) // (lax.axis_size(axis) // 2) + k, 2) * size, size)
 
 
 def pair_kernel(
     k,
-    place_ref,
     left_ref,
     right_ref,
     pair_ref,
@@ -270,7 +266,7 @@
     pair_out, dist_out, outer, start = rest[-4:]
     length, size, channels = pair_out.shape
     block_rows = length // mask_ref.shape[0]
-    second = pl.ds(half_of(place_ref[1], k, size), size)
+    second = pl.ds(half_of("row", k, size), size)
     pairs = length // 2
     depth, lanes = right_ref.shape[1] // 2, right_ref.shape[1]
     groups = right_ref.shape[0] // size
@@ -325,18 +321,18 @@
         dist_out[:, 2 * p * bins : 2 * (p + 1) * bins] = dist[p * size : (p + 1) * size]
 
 
-def own_kernel(order, place_ref, *refs):
+def own_kernel(order, *refs):
     count = len(order)
     parts, dists = refs[:count], refs[count : 2 * count]
     pair_out, own_ref, sems = refs[2 * count :]
     length, size, _ = parts[0].shape
-    firsts = [half_of(place_ref[1], k, size) for k in order]
+    firsts = [half_of("row", k, size) for k in order]
     copies = fetch(parts, [pair_out.at[:, pl.ds(first, size)] for first in firsts], sems)
     pairs = length // 2
     lanes = dists[0].shape[1] // pairs
     low = iota((pairs, lanes), 1) < lanes // 2
     for k, dist in zip(order, dists, strict=True):
-        first = half_of(place_ref[1], k, size // 2)
+        first = half_of("row", k, size // 2)
         tiles = jnp.stack([dist[:, p * lanes : (p + 1) * lanes].astype(F32) for p in range(pairs)])
         turned = jnp.swapaxes(tiles, 0, 1)
         for j in range(0, size, 2):
@@ -351,7 +347,7 @@
         copy.wait()
 
 
-def final_kernel(order, place_ref, own_ref, bias_ref, *refs):
+def final_kernel(order, own_ref, bias_ref, *refs):
     out_ref = refs[len(order)]
     lanes = bias_ref.shape[1]
 
@@ -365,8 +361,9 @@
                 value = own_ref[t, rows, :] + part[:, at].astype(F32) + bias_ref[...]
                 out_ref[rows, at] = value.astype(BF16)
 
-    pl.when(place_ref[0] == 0)(functools.partial(write, 0))
-    pl.when(place_ref[0] == 1)(functools.partial(write, 1))
+    half = lax.axis_index("col") // (lax.axis_size("col") // 2)
+    pl.when(half == 0)(functools.partial(write, 0))
+    pl.when(half == 1)(functools.partial(write, 1))
 
 
 PAIR_COST = pl.CostEstimate(flops=5_000_000_000, bytes_accessed=16_000_000, transcendentals=0)
@@ -382,7 +379,6 @@
 
 
 VMEM = pl.BlockSpec(memory_space=pltpu.VMEM)
-SMEM = pl.BlockSpec(memory_space=pltpu.SMEM)
 HBM = pl.BlockSpec(memory_space=pltpu.HBM)
 
 
@@ -414,9 +410,7 @@
     e_width = second_weight.shape[1]
     bins = distance_weight.shape[1]
     axes = ("row", "col")
-    row, col = lax.axis_index("row"), lax.axis_index("col")
     size = col_count // 2
-    place = jnp.stack([col // size, row // size, col, row, col % size]).astype(jnp.int32)
 
     def moved(value, target):
         pairs = [
@@ -455,12 +449,12 @@
     embedded = pl.pallas_call(
         functools.partial(embed_group_kernel, kinds, size),
         out_shape=jax.ShapeDtypeStruct((depth, size * alignment_state.shape[1]), BF16),
-        in_specs=[SMEM] + [VMEM] * (2 * size),
+        in_specs=[VMEM] * (2 * size),
         out_specs=VMEM,
         compiler_params=params(4),
         cost_estimate=COST,
         name="embed_group",
-    )(place, own_embedded, wide_table, *other_states, *other_indices)
+    )(own_embedded, wide_table, *other_states, *other_indices)
 
     rights = {
         k: moved(embedded, lambda r, c, k=k: ((c - size * k) % row_count, r)) for k in ORDER
@@ -501,7 +495,7 @@
             jax.ShapeDtypeStruct((1, 2 * bins), F32),
             left_shape,
         ),
-        in_specs=[SMEM] + [HBM] * 14 + [VMEM],
+        in_specs=[HBM] * 14 + [VMEM],
         out_specs=(VMEM,) * 13,
         scratch_shapes=[
             pltpu.VMEM((1, token_kinds.shape[0]), jnp.int32),
@@ -522,7 +516,6 @@
         cost_estimate=COST,
         name="weights",
     )(
-        place,
         *in_hbm(
             token_kinds.reshape(1, -1),
             first_type_table,
@@ -545,28 +538,27 @@
     half = length // 2
     right_shape = jax.ShapeDtypeStruct((e_width // 2 * half, 2 * depth), BF16)
     pair_parts, dist_parts, mirror_parts = [], [], []
+    left_tiles = pl.pallas_call(
+        project_left_kernel,
+        out_shape=left_shape,
+        in_specs=[VMEM] * 3,
+        out_specs=VMEM,
+        input_output_aliases={2: 0},
+        compiler_params=params(4),
+        cost_estimate=COST,
+        name="project_left",
+    )(other, left_weight, left_tiles)
     for n, k in enumerate(ORDER):
-        if n == 0:
-            left_tiles, right_tiles = pl.pallas_call(
-                project_both_kernel,
-                out_shape=(left_shape, right_shape),
-                in_specs=[SMEM] + [VMEM] * 5,
-                out_specs=(VMEM,) * 2,
-                input_output_aliases={5: 0},
-                compiler_params=params(4),
-                cost_estimate=COST,
-                name="project_both",
-            )(place, other, rights[k], left_weight, right_weight, left_tiles)
-        else:
-            right_tiles = pl.pallas_call(
-                project_right_kernel,
-                out_shape=right_shape,
-                in_specs=[VMEM] * 2,
-                out_specs=VMEM,
-                compiler_params=params(4),
-                cost_estimate=COST,
-                name="project_right",
-            )(rights[k], right_weight)
+        after = [left_tiles] if n == 0 else []
+        right_tiles = pl.pallas_call(
+            project_right_kernel,
+            out_shape=right_shape,
+            in_specs=[VMEM] * (2 + len(after)),
+            out_specs=VMEM,
+            compiler_params=params(4),
+            cost_estimate=COST,
+            name="project_right",
+        )(rights[k], right_weight, *after)
         before = dist_parts[-1:]
         pair_part, dist_part = pl.pallas_call(
             functools.partial(pair_kernel, k),
@@ -574,7 +566,7 @@
                 jax.ShapeDtypeStruct((length, half, channels), BF16),
                 jax.ShapeDtypeStruct((half, length * bins), BF16),
             ),
-            in_specs=[SMEM] + [VMEM] * (11 + len(before)),
+            in_specs=[VMEM] * (11 + len(before)),
             out_specs=(VMEM,) * 2,
             scratch_shapes=[
                 pltpu.VMEM((length // 2 * half, 2 * c_width * e_width), BF16),
@@ -584,7 +576,6 @@
             cost_estimate=PAIR_COST,
             name="pairs",
         )(
-            place,
             left_tiles,
             right_tiles,
             pair_in,
@@ -611,22 +602,22 @@
             jax.ShapeDtypeStruct(pair_state.shape, BF16),
             jax.ShapeDtypeStruct((length // 2, length, 2 * bins), F32),
         ),
-        in_specs=[SMEM] + [VMEM] * (2 * len(pair_parts)),
+        in_specs=[VMEM] * (2 * len(pair_parts)),
         out_specs=(HBM, VMEM),
         scratch_shapes=[pltpu.SemaphoreType.DMA((len(pair_parts),))],
         compiler_params=params(8),
         cost_estimate=COST,
         name="own",
-    )(place, *pair_parts, *dist_parts)
+    )(*pair_parts, *dist_parts)
     distogram = pl.pallas_call(
         functools.partial(final_kernel, ORDER),
         out_shape=jax.ShapeDtypeStruct((length, length * bins), BF16),
-        in_specs=[SMEM] + [VMEM] * 4,
+        in_specs=[VMEM] * 4,
         out_specs=VMEM,
         compiler_params=params(4),
         cost_estimate=COST,
         name="final",
-    )(place, own, last, *mirror_parts)
+    )(own, last, *mirror_parts)
     return pair_out, distogram
 
 

time: 45 us -> 41.8 us (0.929)
  Pallas kernels: 19.6 us -> 15.8 us
  waiting for transfers between devices: 11.9 us -> 13.7 us
  starting transfers between devices: 12.5 us -> 11.3 us
    ppermute x8, waiting for transfers between devices: 11.9 us -> 13.7 us  [moved(): return lax.ppermute(value, axes, pairs)]
    pallas_call x2, Pallas kernels: 10 us -> 8.77 us  [local(): pl.pallas_call(functools.partial(pair_kernel, k), out_shape=(jax.ShapeDty...]
    ppermute x8, starting transfers between devices: 12.5 us -> 11.3 us  [moved(): return lax.ppermute(value, axes, pairs)]
    pallas_call x1, Pallas kernels: 0.98 us -> 0.3 us  [local(): pl.pallas_call(project_left_kernel, out_shape=left_shape, in_specs=[VMEM]...]
    pallas_call x1, Pallas kernels: 1.48 us -> 0.93 us  [local(): pl.pallas_call(functools.partial(final_kernel, ORDER), out_shape=jax.Shap...]
    pallas_call x1, Pallas kernels: 2.8 us -> 2.25 us  [local(): pl.pallas_call(weights_kernel, out_shape=(jax.ShapeDtypeStruct((length, c...]
    pallas_call x1, Pallas kernels: 1.78 us -> 1.24 us  [local(): pl.pallas_call(functools.partial(own_kernel, ORDER), out_shape=(jax.Shape...]
    pallas_call x1, Pallas kernels: 0.86 us -> 0.31 us  [local(): pl.pallas_call(functools.partial(embed_group_kernel, kinds, size), out_sh...]
  transfers between devices with their start and end apart: 8 -> 8, of which waited for: 3 -> 3; matrix products, arithmetic and copies ran while one was open for 0% -> 0% of each run, Pallas kernels for 38% -> 35%
where the time goes in v5:
time: 41.8 us; the launch traced here: 41.6 us
  Pallas kernels  15.8 us (38%)
  waiting for transfers between devices  13.7 us (33%)
  starting transfers between devices  11.3 us (27%)
  between operations  0.77 us (2%)
    ppermute x8, waiting for transfers between devices, moved(): return lax.ppermute(value, axes, pairs)  13.7 us
    ppermute x8, starting transfers between devices, moved(): return lax.ppermute(value, axes, pairs)  11.3 us
    pallas_call x2, Pallas kernels, local(): pl.pallas_call(functools.partial(pair_kernel, k), out_shape=(jax.ShapeDty...  8.77 us
    pallas_call x1, Pallas kernels, local(): pl.pallas_call(weights_kernel, out_shape=(jax.ShapeDtypeStruct((length, c...  2.25 us
    pallas_call x1, Pallas kernels, local(): pl.pallas_call(embed_own_kernel, out_shape=(jax.ShapeDtypeStruct(alignmen...  1.37 us
    pallas_call x1, Pallas kernels, local(): pl.pallas_call(functools.partial(own_kernel, ORDER), out_shape=(jax.Shape...  1.24 us
    pallas_call x1, Pallas kernels, local(): pl.pallas_call(functools.partial(final_kernel, ORDER), out_shape=jax.Shap...  0.93 us
  transfers between devices with their start and end apart: 8, of which 3 were waited for; matrix products, arithmetic and copies ran while one was open for 0% of the time, Pallas kernels for 35%

profile of v5, /device:TPU:2, one launch (start us, length us, event | category | flops | bytes accessed | tf_op | source)
XLA Modules:
  0.0 41.6 jit_solution(12611939428041585878)
XLA Ops:
  0.6 0.1 collective-permute-start
  0.7 0.5 %collective-permute-start.1 = (s32[16,64]{1,0:T(8,128)}, s32[16,64]{1,0:T(8,128)S(1)}, u32[]{:S(2)}, u32[]{:S(2)}) collective-permute-start(s32[16,64]{1,0:T(8,128)} %bitcast.7), channel_id=1, source_target_pairs={{0,1},{1,0},{2,3},{3,2},{4,5},{5,4},{6,7},{7,6},{8,9},{9,8},{10,11... | collective-permute-start | bytes 12296 | tf_op jit(solution)/shard_map/ppermute | solution.py:421
  1.2 1.4 %embed_own.1 = (bf16[64,512]{1,0:T(8,128)(2,1)S(1)}, bf16[256,256]{1,0:T(8,128)(2,1)S(1)}) custom-call(bf16[64,512]{1,0:T(8,128)(2,1)} %state_hbm.1, s32[16,64]{1,0:T(8,128)} %bitcast.8, bf16[32,32]{1,0:T(8,128)(2,1)} %table_hbm.1), custom_call_target="tpu_custom_call" | custom-call | tf_op jit(solution)/shard_map/embed_own/pallas_call | solution.py:431
  2.6 0.0 collective-permute-done.1.refs_1_
  2.6 0.0 collective-permute-done.refs_0_
  2.6 0.3 embed_group.1.embedded_ref
  2.9 0.1 collective-permute-start.2
  3.0 2.0 %collective-permute-start.3 = (bf16[64,1024]{1,0:T(8,128)(2,1)S(1)}, bf16[64,1024]{1,0:T(8,128)(2,1)S(1)}, u32[]{:S(2)}, u32[]{:S(2)}) collective-permute-start(bf16[64,1024]{1,0:T(8,128)(2,1)S(1)} %embed_group.1.embedded_ref), channel_id=1, source_target_pairs={{0,8},{1,12},{2,0},{3,4},{4,9},{5,13},{6,1},{7,5},{8,10},{9,14},{1... | collective-permute-start | bytes 393224 | tf_op jit(solution)/shard_map/ppermute | solution.py:421
  5.0 4.5 %collective-permute-start.4 = (bf16[64,1024]{1,0:T(8,128)(2,1)S(1)}, bf16[64,1024]{1,0:T(8,128)(2,1)S(1)}, u32[]{:S(2)}, u32[]{:S(2)}) collective-permute-start(bf16[64,1024]{1,0:T(8,128)(2,1)S(1)} %embed_group.1.embedded_ref), channel_id=1, source_target_pairs={{0,0},{1,4},{2,8},{3,12},{4,1},{5,5},{6,9},{7,13},{8,2},{9,6},{10,... | collective-permute-start | bytes 393224 | tf_op jit(solution)/shard_map/ppermute | solution.py:421
  9.5 2.2 %weights.1 = (f32[64,128]{1,0:T(8,128)S(1)}, f32[4,64,128]{2,1,0:T(8,128)S(1)}, f32[4,64,128]{2,1,0:T(8,128)S(1)}, bf16[2048,256]{1,0:T(8,128)(2,1)S(1)}, bf16[6...) custom-call(s32[1,256]{1,0:T(1,128)} %bitcast.9, ...), custom_call_target="tpu_custom_call" | custom-call | tf_op jit(solution)/shard_map/weights/pallas_call | solution.py:481
  11.7 0.0 collective-permute-done.2.other_ref
  11.7 0.3 project_left.1.rest_0_.left_ref
  12.1 1.1 %collective-permute-done.3.right_ref = bf16[64,1024]{1,0:T(8,128)(2,1)S(1)} collective-permute-done((bf16[64,1024]{1,0:T(8,128)(2,1)S(1)}, bf16[64,1024]{1,0:T(8,128)(2,1)S(1)}, u32[]{:S(2)}, u32[]{:S(2)}) %collective-permute-start.3) | collective-permute-done | bytes 131104 | tf_op jit(solution)/shard_map/ppermute | solution.py:421
  13.1 0.3 project_right.2.right_ref
  13.5 4.4 %pairs.2 = (bf16[64,32,128]{2,1,0:T(8,128)(2,1)S(1)}, bf16[32,4096]{1,0:T(8,128)(2,1)S(1)}) custom-call(bf16[128,4096]{1,0:T(8,128)(2,1)S(1)} %project_left.1.rest_0_.left_ref, bf16[512,128]{1,0:T(8,128)(2,1)S(1)} %project_right.2.right_ref, bf16[64,64,128]{2,1,0:T(8,128)(2,1)S(1)} %get-tuple-element.28.pair_ref, f32[64,128]{1,0:T(8,128)S(1)} %get-tuple-element.29.first_ref, ...), custom_call_target="tpu_custom_call" | custom-call | flops 5000000000 | bytes 16000000 | tf_op jit(solution)/shard_map/pairs/pallas_call | solution.py:563
  17.8 0.1 collective-permute-start.5
  17.9 0.3 project_right.3.right_ref
  18.2 4.4 %pairs.3 = (bf16[64,32,128]{2,1,0:T(8,128)(2,1)S(1)}, bf16[32,4096]{1,0:T(8,128)(2,1)S(1)}) custom-call(bf16[128,4096]{1,0:T(8,128)(2,1)S(1)} %project_left.1.rest_0_.left_ref, bf16[512,128]{1,0:T(8,128)(2,1)S(1)} %project_right.3.right_ref, bf16[64,64,128]{2,1,0:T(8,128)(2,1)S(1)} %get-tuple-element.28.pair_ref, f32[64,128]{1,0:T(8,128)S(1)} %get-tuple-element.29.first_ref, ...), custom_call_target="tpu_custom_call" | custom-call | flops 5000000000 | bytes 16000000 | tf_op jit(solution)/shard_map/pairs/pallas_call | solution.py:563
  22.6 4.1 %collective-permute-start.7 = (bf16[32,4096]{1,0:T(8,128)(2,1)S(1)}, bf16[32,4096]{1,0:T(8,128)(2,1)S(1)}, u32[]{:S(2)}, u32[]{:S(2)}) collective-permute-start(bf16[32,4096]{1,0:T(8,128)(2,1)S(1)} %get-tuple-element.40.refs_3_), channel_id=1, source_target_pairs={{0,0},{1,4},{2,8},{3,12},{4,1},{5,5},{6,9},{7,13},{8,2},{9,6},{10,... | collective-permute-start | bytes 786440 | tf_op jit(solution)/shard_map/ppermute | solution.py:421
  26.7 0.1 collective-permute-start.6
  26.8 1.2 %own.1 = (bf16[64,64,128]{2,1,0:T(8,128)(2,1)}, f32[32,64,128]{2,1,0:T(8,128)S(1)}) custom-call(bf16[64,32,128]{2,1,0:T(8,128)(2,1)S(1)} %get-tuple-element.37.refs_0_, bf16[64,32,128]{2,1,0:T(8,128)(2,1)S(1)} %get-tuple-element.39.refs_1_, bf16[32,4096]{1,0:T(8,128)(2,1)S(1)} %get-tuple-element.38.rest_0_.refs_2_, ...), custom_call_target="tpu_custom_call" | custom-call | tf_op jit(solution)/shard_map/own/pallas_call | solution.py:599
  28.0 12.5 %collective-permute-done.7.refs_1_ = bf16[32,4096]{1,0:T(8,128)(2,1)S(1)} collective-permute-done((bf16[32,4096]{1,0:T(8,128)(2,1)S(1)}, bf16[32,4096]{1,0:T(8,128)(2,1)S(1)}, u32[]{:S(2)}, u32[]{:S(2)}) %collective-permute-start.7) | collective-permute-done | bytes 262176 | tf_op jit(solution)/shard_map/ppermute | solution.py:421
  40.5 0.2 collective-permute-done.6.refs_0_
  40.7 0.9 %final.1 = bf16[64,4096]{1,0:T(8,128)(2,1)} custom-call(f32[32,64,128]{2,1,0:T(8,128)S(1)} %get-tuple-element.42.own_ref, f32[1,128]{1,0:T(1,128)S(1)} %get-tuple-element.43.bias_ref, bf16[32,4096]{1,0:T(8,128)(2,1)S(1)} %collective-permute-done.6.refs_0_, bf16[32,4096]{1,0:T(8,128)(2,1)S(1)} %collective-permute-done.7.refs_1_), custom_call_target="tpu_custom_call" | custom-call | tf_op jit(solution)/shard_map/final/pallas_call | solution.py:612
  (2 shorter events, 0.0 us)
Async XLA Ops:
  0.6 2.0 %collective-permute-start = (bf16[64,512]{1,0:T(8,128)(2,1)}, bf16[64,512]{1,0:T(8,128)(2,1)S(1)}, u32[]{:S(2)}, u32[]{:S(2)}) collective-permute-start(bf16[64,512]{1,0:T(8,128)(2,1)} %state_hbm.1), channel_id=1, source_target_pairs={{0,1},{1,0},{2,3},{3,2},{4,5},{5,4},{6,7},{7,6},{8,9},{9,8},{10,11... | collective-permute-start | bytes 196616 | tf_op jit(solution)/shard_map/ppermute | solution.py:421
  0.7 1.9 %collective-permute-start.1 = (s32[16,64]{1,0:T(8,128)}, s32[16,64]{1,0:T(8,128)S(1)}, u32[]{:S(2)}, u32[]{:S(2)}) collective-permute-start(s32[16,64]{1,0:T(8,128)} %bitcast.7), channel_id=1, source_target_pairs={{0,1},{1,0},{2,3},{3,2},{4,5},{5,4},{6,7},{7,6},{8,9},{9,8},{10,11... | collective-permute-start | bytes 12296 | tf_op jit(solution)/shard_map/ppermute | solution.py:421
  2.9 8.8 %collective-permute-start.2 = (bf16[64,1024]{1,0:T(8,128)(2,1)S(1)}, bf16[64,1024]{1,0:T(8,128)(2,1)S(1)}, u32[]{:S(2)}, u32[]{:S(2)}) collective-permute-start(bf16[64,1024]{1,0:T(8,128)(2,1)S(1)} %embed_group.1.embedded_ref), channel_id=1, source_target_pairs={{0,2},{1,3},{2,0},{3,1},{4,6},{5,7},{6,4},{7,5},{8,10},{9,11},{10,... | collective-permute-start | bytes 393224 | tf_op jit(solution)/shard_map/ppermute | solution.py:421
  3.0 10.1 %collective-permute-start.3 = (bf16[64,1024]{1,0:T(8,128)(2,1)S(1)}, bf16[64,1024]{1,0:T(8,128)(2,1)S(1)}, u32[]{:S(2)}, u32[]{:S(2)}) collective-permute-start(bf16[64,1024]{1,0:T(8,128)(2,1)S(1)} %embed_group.1.embedded_ref), channel_id=1, source_target_pairs={{0,8},{1,12},{2,0},{3,4},{4,9},{5,13},{6,1},{7,5},{8,10},{9,14},{1... | collective-permute-start | bytes 393224 | tf_op jit(solution)/shard_map/ppermute | solution.py:421
  5.0 12.9 %collective-permute-start.4 = (bf16[64,1024]{1,0:T(8,128)(2,1)S(1)}, bf16[64,1024]{1,0:T(8,128)(2,1)S(1)}, u32[]{:S(2)}, u32[]{:S(2)}) collective-permute-start(bf16[64,1024]{1,0:T(8,128)(2,1)S(1)} %embed_group.1.embedded_ref), channel_id=1, source_target_pairs={{0,0},{1,4},{2,8},{3,12},{4,1},{5,5},{6,9},{7,13},{8,2},{9,6},{10,... | collective-permute-start | bytes 393224 | tf_op jit(solution)/shard_map/ppermute | solution.py:421
  17.8 8.9 %collective-permute-start.5 = (bf16[32,4096]{1,0:T(8,128)(2,1)S(1)}, bf16[32,4096]{1,0:T(8,128)(2,1)S(1)}, u32[]{:S(2)}, u32[]{:S(2)}) collective-permute-start(bf16[32,4096]{1,0:T(8,128)(2,1)S(1)} %get-tuple-element.38.rest_0_.refs_2_), channel_id=1, source_target_pairs={{0,2},{1,3},{2,0},{3,1},{4,6},{5,7},{6,4},{7,5},{8,10},{9,11},{10,... | collective-permute-start | bytes 786440 | tf_op jit(solution)/shard_map/ppermute | solution.py:421
  22.6 17.9 %collective-permute-start.7 = (bf16[32,4096]{1,0:T(8,128)(2,1)S(1)}, bf16[32,4096]{1,0:T(8,128)(2,1)S(1)}, u32[]{:S(2)}, u32[]{:S(2)}) collective-permute-start(bf16[32,4096]{1,0:T(8,128)(2,1)S(1)} %get-tuple-element.40.refs_3_), channel_id=1, source_target_pairs={{0,0},{1,4},{2,8},{3,12},{4,1},{5,5},{6,9},{7,13},{8,2},{9,6},{10,... | collective-permute-start | bytes 786440 | tf_op jit(solution)/shard_map/ppermute | solution.py:421
  26.7 14.0 %collective-permute-start.6 = (bf16[32,4096]{1,0:T(8,128)(2,1)S(1)}, bf16[32,4096]{1,0:T(8,128)(2,1)S(1)}, u32[]{:S(2)}, u32[]{:S(2)}) collective-permute-start(bf16[32,4096]{1,0:T(8,128)(2,1)S(1)} %collective-permute-done.5), channel_id=1, source_target_pairs={{0,8},{1,12},{2,0},{3,4},{4,9},{5,13},{6,1},{7,5},{8,10},{9,14},{1... | collective-permute-start | bytes 786440 | tf_op jit(solution)/shard_map/ppermute | solution.py:421

commit v6 on v5

--- a/solution.py
+++ b/solution.py
@@ -13,7 +13,7 @@
 NT = (((1,), (1,)), ((), ()))
 TN = (((0,), (0,)), ((), ()))
 MIB = 1024 * 1024
-ORDER = (1, 0)
+PARTS = ((1, 0, 8), (0, 0, 6), (0, 6, 2))
 
 
 def iota(shape, dim):
@@ -239,19 +239,15 @@
     project_left([(1, other_ref)], weight_ref, left_out)
 
 
-def project_right_kernel(right_ref, right_weight_ref, *rest):
-    right_out = rest[-1]
-    project_right(right_ref, right_weight_ref, right_out)
-
-
 def half_of(axis, k, size):
     return pl.multiple_of(lax.rem(lax.axis_index(axis) // (lax.axis_size(axis) // 2) + k, 2) * size, size)
 
 
 def pair_kernel(
-    k,
+    part,
     left_ref,
-    right_ref,
+    embedded_ref,
+    right_weight_ref,
     pair_ref,
     first_ref,
     mask_ref,
@@ -263,18 +259,21 @@
     distance_ref,
     *rest,
 ):
-    pair_out, dist_out, outer, start = rest[-4:]
-    length, size, channels = pair_out.shape
-    block_rows = length // mask_ref.shape[0]
+    pair_out, dist_out, right_ref, outer, start = rest[-5:]
+    project_right(embedded_ref, right_weight_ref, right_ref)
+    rows, size, channels = pair_out.shape
+    block_rows = pair_ref.shape[0] // mask_ref.shape[0]
+    k, eighth, _ = part
     second = pl.ds(half_of("row", k, size), size)
-    pairs = length // 2
+    pairs = rows // 2
+    first_pair = eighth * pair_ref.shape[0] // 16
     depth, lanes = right_ref.shape[1] // 2, right_ref.shape[1]
     groups = right_ref.shape[0] // size
     step = min(groups, 256 // size)
     hid = down_ref.shape[0]
     bins = distance_ref.shape[0] // 2
     for p in range(0, pairs, 2):
-        weight = left_ref[:, p * lanes : (p + 2) * lanes]
+        weight = left_ref[:, (first_pair + p) * lanes : (first_pair + p + 2) * lanes]
         for g in range(0, groups, step):
             got = dot(right_ref[g * size : (g + step) * size, :], weight).astype(BF16)
             for q in range(2):
@@ -282,24 +281,24 @@
                     outer[(p + q) * size : (p + q + 1) * size, (g + h) * lanes : (g + h + 1) * lanes] = got[
                         h * size : (h + 1) * size, q * lanes : (q + 1) * lanes
                     ]
-    part_rows = max(size, outer.shape[0] // 8)
+    part_rows = max(128, outer.shape[0] // 8)
     update = [
         dot(outer[n : n + part_rows], outer_ref[...]) for n in range(0, outer.shape[0], part_rows)
     ]
     for p in range(pairs):
-        block = 2 * p // block_rows
+        block = 2 * (first_pair + p) // block_rows
         mask = mask_ref[block, second, :] * (1.0 / depth)
         base = base_ref[block, second, :]
         at = p * size % part_rows
         part = update[p * size // part_rows][at : at + size]
         for q in range(2):
-            i = 2 * p + q
+            i = 2 * (first_pair + p) + q
             start[q, p * size : (p + 1) * size, :] = (
                 pair_ref[i, second, :].astype(F32)
                 + (first_ref[i : i + 1, :] + base)
                 + mask * part[:, q * channels : (q + 1) * channels]
             )
-    half = min(start.shape[1], 512)
+    half = start.shape[1] if start.shape[1] < 1024 else 512
     for q, at in ((q, slice(n, n + half)) for q in range(2) for n in range(0, start.shape[1], half)):
         value = start[q, at]
         mean = jnp.mean(value, axis=-1, keepdims=True)
@@ -321,45 +320,50 @@
         dist_out[:, 2 * p * bins : 2 * (p + 1) * bins] = dist[p * size : (p + 1) * size]
 
 
-def own_kernel(order, *refs):
-    count = len(order)
-    parts, dists = refs[:count], refs[count : 2 * count]
+def own_kernel(*refs):
+    count = len(PARTS)
+    pairs_in, dists = refs[:count], refs[count : 2 * count]
     pair_out, own_ref, sems = refs[2 * count :]
-    length, size, _ = parts[0].shape
-    firsts = [half_of("row", k, size) for k in order]
-    copies = fetch(parts, [pair_out.at[:, pl.ds(first, size)] for first in firsts], sems)
-    pairs = length // 2
-    lanes = dists[0].shape[1] // pairs
-    low = iota((pairs, lanes), 1) < lanes // 2
-    for k, dist in zip(order, dists, strict=True):
+    targets = []
+    length = pair_out.shape[0]
+    for (k, eighth, _), part in zip(PARTS, pairs_in, strict=True):
+        rows, size, _ = part.shape
+        targets.append(pair_out.at[pl.ds(eighth * length // 8, rows), pl.ds(half_of("row", k, size), size)])
+    copies = fetch(pairs_in, targets, sems)
+    lanes = own_ref.shape[2]
+    for (k, eighth, _), part, dist in zip(PARTS, pairs_in, dists, strict=True):
+        rows, size, _ = part.shape
+        pairs = rows // 2
+        above = eighth * length // 8
+        low = iota((pairs, lanes), 1) < lanes // 2
         first = half_of("row", k, size // 2)
         tiles = jnp.stack([dist[:, p * lanes : (p + 1) * lanes].astype(F32) for p in range(pairs)])
         turned = jnp.swapaxes(tiles, 0, 1)
         for j in range(0, size, 2):
             one, two = turned[j], turned[j + 1]
-            own_ref[first + j // 2, pl.ds(0, pairs, stride=2), :] = jnp.where(
+            own_ref[first + j // 2, pl.ds(above, pairs, stride=2), :] = jnp.where(
                 low, one, pltpu.roll(two, lanes // 2, 1)
             )
-            own_ref[first + j // 2, pl.ds(1, pairs, stride=2), :] = jnp.where(
+            own_ref[first + j // 2, pl.ds(above + 1, pairs, stride=2), :] = jnp.where(
                 low, pltpu.roll(one, lanes // 2, 1), two
             )
     for copy in copies:
         copy.wait()
 
 
-def final_kernel(order, own_ref, bias_ref, *refs):
-    out_ref = refs[len(order)]
+def final_kernel(own_ref, bias_ref, *refs):
+    out_ref = refs[len(PARTS)]
     lanes = bias_ref.shape[1]
 
     def write(swapped):
-        for k, part in zip(order, refs, strict=False):
+        for (k, eighth, _), part in zip(PARTS, refs, strict=False):
             size, width = part.shape
             first = (k + swapped) % 2 * size
             rows = slice(first, first + size)
             for t in range(width // lanes):
-                at = slice(t * lanes, (t + 1) * lanes)
-                value = own_ref[t, rows, :] + part[:, at].astype(F32) + bias_ref[...]
-                out_ref[rows, at] = value.astype(BF16)
+                tile = eighth * out_ref.shape[1] // (8 * lanes) + t
+                value = own_ref[tile, rows, :] + part[:, t * lanes : (t + 1) * lanes].astype(F32) + bias_ref[...]
+                out_ref[rows, tile * lanes : (tile + 1) * lanes] = value.astype(BF16)
 
     half = lax.axis_index("col") // (lax.axis_size("col") // 2)
     pl.when(half == 0)(functools.partial(write, 0))
@@ -457,7 +461,7 @@
     )(own_embedded, wide_table, *other_states, *other_indices)
 
     rights = {
-        k: moved(embedded, lambda r, c, k=k: ((c - size * k) % row_count, r)) for k in ORDER
+        k: moved(embedded, lambda r, c, k=k: ((c - size * k) % row_count, r)) for k in (1, 0)
     }
     other = moved(embedded, lambda r, c: (r, (c + size) % col_count))
 
@@ -536,7 +540,6 @@
     )
 
     half = length // 2
-    right_shape = jax.ShapeDtypeStruct((e_width // 2 * half, 2 * depth), BF16)
     pair_parts, dist_parts, mirror_parts = [], [], []
     left_tiles = pl.pallas_call(
         project_left_kernel,
@@ -548,36 +551,32 @@
         cost_estimate=COST,
         name="project_left",
     )(other, left_weight, left_tiles)
-    for n, k in enumerate(ORDER):
-        after = [left_tiles] if n == 0 else []
-        right_tiles = pl.pallas_call(
-            project_right_kernel,
-            out_shape=right_shape,
-            in_specs=[VMEM] * (2 + len(after)),
-            out_specs=VMEM,
-            compiler_params=params(4),
-            cost_estimate=COST,
-            name="project_right",
-        )(rights[k], right_weight, *after)
+    for n, part in enumerate(PARTS):
+        k, _, eighths = part
+        rows = length * eighths // 8
         before = dist_parts[-1:]
+        if n > 1:
+            before = before + [crossed]
         pair_part, dist_part = pl.pallas_call(
-            functools.partial(pair_kernel, k),
+            functools.partial(pair_kernel, part),
             out_shape=(
-                jax.ShapeDtypeStruct((length, half, channels), BF16),
-                jax.ShapeDtypeStruct((half, length * bins), BF16),
+                jax.ShapeDtypeStruct((rows, half, channels), BF16),
+                jax.ShapeDtypeStruct((half, rows * bins), BF16),
             ),
-            in_specs=[VMEM] * (11 + len(before)),
+            in_specs=[VMEM] * (12 + len(before)),
             out_specs=(VMEM,) * 2,
             scratch_shapes=[
-                pltpu.VMEM((length // 2 * half, 2 * c_width * e_width), BF16),
-                pltpu.VMEM((2, length // 2 * half, channels), F32),
+                pltpu.VMEM((e_width // 2 * half, 2 * depth), BF16),
+                pltpu.VMEM((rows // 2 * half, 2 * c_width * e_width), BF16),
+                pltpu.VMEM((2, rows // 2 * half, channels), F32),
             ],
             compiler_params=params(24),
             cost_estimate=PAIR_COST,
             name="pairs",
         )(
             left_tiles,
-            right_tiles,
+            rights[k],
+            right_weight,
             pair_in,
             first_rows,
             masks,
@@ -597,7 +596,7 @@
         else:
             mirror_parts.append(moved(dist_part, lambda r, c: (c, r)))
     pair_out, own = pl.pallas_call(
-        functools.partial(own_kernel, ORDER),
+        own_kernel,
         out_shape=(
             jax.ShapeDtypeStruct(pair_state.shape, BF16),
             jax.ShapeDtypeStruct((length // 2, length, 2 * bins), F32),
@@ -610,9 +609,9 @@
         name="own",
     )(*pair_parts, *dist_parts)
     distogram = pl.pallas_call(
-        functools.partial(final_kernel, ORDER),
+        final_kernel,
         out_shape=jax.ShapeDtypeStruct((length, length * bins), BF16),
-        in_specs=[VMEM] * 4,
+        in_specs=[VMEM] * (2 + len(mirror_parts)),
         out_specs=VMEM,
         compiler_params=params(4),
         cost_estimate=COST,

time: 41.8 us -> 41.2 us (0.986)
  waiting for transfers between devices: 13.7 us -> 7.37 us
  starting transfers between devices: 11.3 us -> 15.7 us
  Pallas kernels: 15.8 us -> 17.2 us
    ppermute x8 -> x9, waiting for transfers between devices: 13.7 us -> 7.37 us  [moved(): return lax.ppermute(value, axes, pairs)]
    ppermute x8 -> x9, starting transfers between devices: 11.3 us -> 15.7 us  [moved(): return lax.ppermute(value, axes, pairs)]
    pallas_call x6 -> x5, Pallas kernels: 11.5 us -> 12.9 us  [the longest x3 10.7 us: local(): pl.pallas_call(functools.partial(pair_kernel, part), out_shape=(jax.Shape...]
  transfers between devices with their start and end apart: 8 -> 9, of which waited for: 3 -> 4; matrix products, arithmetic and copies ran while one was open for 0% -> 0% of each run, Pallas kernels for 35% -> 39%
where the time goes in v6:
time: 41.2 us; the launch traced here: 41 us
  Pallas kernels  17.2 us (42%)
  starting transfers between devices  15.7 us (38%)
  waiting for transfers between devices  7.37 us (18%)
  between operations  0.77 us (2%)
    ppermute x9, starting transfers between devices, moved(): return lax.ppermute(value, axes, pairs)  15.7 us
    pallas_call x3, Pallas kernels, local(): pl.pallas_call(functools.partial(pair_kernel, part), out_shape=(jax.Shape...  10.7 us
    ppermute x9, waiting for transfers between devices, moved(): return lax.ppermute(value, axes, pairs)  7.37 us
    pallas_call x1, Pallas kernels, local(): pl.pallas_call(weights_kernel, out_shape=(jax.ShapeDtypeStruct((length, c...  2.25 us
    pallas_call x1, Pallas kernels, local(): pl.pallas_call(embed_own_kernel, out_shape=(jax.ShapeDtypeStruct(alignmen...  1.37 us
    pallas_call x1, Pallas kernels, local(): pl.pallas_call(own_kernel, out_shape=(jax.ShapeDtypeStruct(pair_state.sha...  1.25 us
    pallas_call x1, Pallas kernels, local(): pl.pallas_call(final_kernel, out_shape=jax.ShapeDtypeStruct((length, leng...  0.95 us
  transfers between devices with their start and end apart: 9, of which 4 were waited for; matrix products, arithmetic and copies ran while one was open for 0% of the time, Pallas kernels for 39%

profile of v6, /device:TPU:2, one launch (start us, length us, event | category | flops | bytes accessed | tf_op | source)
XLA Modules:
  0.0 41.0 jit_solution(7346141210351011577)
XLA Ops:
  0.6 0.1 collective-permute-start
  0.7 0.5 %collective-permute-start.1 = (s32[16,64]{1,0:T(8,128)}, s32[16,64]{1,0:T(8,128)S(1)}, u32[]{:S(2)}, u32[]{:S(2)}) collective-permute-start(s32[16,64]{1,0:T(8,128)} %bitcast.7), channel_id=1, source_target_pairs={{0,1},{1,0},{2,3},{3,2},{4,5},{5,4},{6,7},{7,6},{8,9},{9,8},{10,11... | collective-permute-start | bytes 12296 | tf_op jit(solution)/shard_map/ppermute | solution.py:425
  1.2 1.4 %embed_own.1 = (bf16[64,512]{1,0:T(8,128)(2,1)S(1)}, bf16[256,256]{1,0:T(8,128)(2,1)S(1)}) custom-call(bf16[64,512]{1,0:T(8,128)(2,1)} %state_hbm.1, s32[16,64]{1,0:T(8,128)} %bitcast.8, bf16[32,32]{1,0:T(8,128)(2,1)} %table_hbm.1), custom_call_target="tpu_custom_call" | custom-call | tf_op jit(solution)/shard_map/embed_own/pallas_call | solution.py:435
  2.6 0.0 collective-permute-done.1.refs_1_
  2.6 0.3 embed_group.1.embedded_ref
  2.9 0.1 collective-permute-start.2
  3.0 2.0 %collective-permute-start.3 = (bf16[64,1024]{1,0:T(8,128)(2,1)S(1)}, bf16[64,1024]{1,0:T(8,128)(2,1)S(1)}, u32[]{:S(2)}, u32[]{:S(2)}) collective-permute-start(bf16[64,1024]{1,0:T(8,128)(2,1)S(1)} %embed_group.1.embedded_ref), channel_id=1, source_target_pairs={{0,8},{1,12},{2,0},{3,4},{4,9},{5,13},{6,1},{7,5},{8,10},{9,14},{1... | collective-permute-start | bytes 393224 | tf_op jit(solution)/shard_map/ppermute | solution.py:425
  5.0 4.5 %collective-permute-start.4 = (bf16[64,1024]{1,0:T(8,128)(2,1)S(1)}, bf16[64,1024]{1,0:T(8,128)(2,1)S(1)}, u32[]{:S(2)}, u32[]{:S(2)}) collective-permute-start(bf16[64,1024]{1,0:T(8,128)(2,1)S(1)} %embed_group.1.embedded_ref), channel_id=1, source_target_pairs={{0,0},{1,4},{2,8},{3,12},{4,1},{5,5},{6,9},{7,13},{8,2},{9,6},{10,... | collective-permute-start | bytes 393224 | tf_op jit(solution)/shard_map/ppermute | solution.py:425
  9.5 2.2 %weights.1 = (f32[64,128]{1,0:T(8,128)S(1)}, f32[4,64,128]{2,1,0:T(8,128)S(1)}, f32[4,64,128]{2,1,0:T(8,128)S(1)}, bf16[2048,256]{1,0:T(8,128)(2,1)S(1)}, bf16[6...) custom-call(s32[1,256]{1,0:T(1,128)} %bitcast.9, ...), custom_call_target="tpu_custom_call" | custom-call | tf_op jit(solution)/shard_map/weights/pallas_call | solution.py:485
  11.7 0.0 collective-permute-done.2.other_ref
  11.7 0.3 project_left.1.left_ref
  12.1 1.1 %collective-permute-done.3.embedded_ref = bf16[64,1024]{1,0:T(8,128)(2,1)S(1)} collective-permute-done((bf16[64,1024]{1,0:T(8,128)(2,1)S(1)}, bf16[64,1024]{1,0:T(8,128)(2,1)S(1)}, u32[]{:S(2)}, u32[]{:S(2)}) %collective-permute-start.3) | collective-permute-done | bytes 131104 | tf_op jit(solution)/shard_map/ppermute | solution.py:425
  13.1 4.7 %pairs.3 = (bf16[64,32,128]{2,1,0:T(8,128)(2,1)S(1)}, bf16[32,4096]{1,0:T(8,128)(2,1)S(1)}) custom-call(bf16[128,4096]{1,0:T(8,128)(2,1)S(1)} %project_left.1.left_ref, bf16[64,1024]{1,0:T(8,128)(2,1)S(1)} %collective-permute-done.3.embedded_ref, bf16[256,256]{1,0:T(8,128)(2,1)S(1)} %get-tuple-element.29.right_weight_ref, ...), custom_call_target="tpu_custom_call" | custom-call | flops 5000000000 | bytes 16000000 | tf_op jit(solution)/shard_map/pairs/pallas_call | solution.py:560
  17.8 0.1 collective-permute-start.5
  17.9 4.1 %pairs.4 = (bf16[48,32,128]{2,1,0:T(8,128)(2,1)S(1)}, bf16[32,3072]{1,0:T(8,128)(2,1)S(1)}) custom-call(bf16[128,4096]{1,0:T(8,128)(2,1)S(1)} %project_left.1.left_ref, bf16[64,1024]{1,0:T(8,128)(2,1)S(1)} %collective-permute-done.4.embedded_ref, bf16[256,256]{1,0:T(8,128)(2,1)S(1)} %get-tuple-element.29.right_weight_ref, ...), custom_call_target="tpu_custom_call" | custom-call | flops 5000000000 | bytes 16000000 | tf_op jit(solution)/shard_map/pairs/pallas_call | solution.py:560
  22.0 4.1 %collective-permute-start.7 = (bf16[32,3072]{1,0:T(8,128)(2,1)S(1)}, bf16[32,3072]{1,0:T(8,128)(2,1)S(1)}, u32[]{:S(2)}, u32[]{:S(2)}) collective-permute-start(bf16[32,3072]{1,0:T(8,128)(2,1)S(1)} %get-tuple-element.42.rest_0_.refs_4_), channel_id=1, source_target_pairs={{0,0},{1,4},{2,8},{3,12},{4,1},{5,5},{6,9},{7,13},{8,2},{9,6},{10,... | collective-permute-start | bytes 589832 | tf_op jit(solution)/shard_map/ppermute | solution.py:425
  26.1 0.1 collective-permute-start.6
  26.2 2.0 %pairs.5 = (bf16[16,32,128]{2,1,0:T(8,128)(2,1)S(1)}, bf16[32,1024]{1,0:T(8,128)(2,1)S(1)}) custom-call(bf16[128,4096]{1,0:T(8,128)(2,1)S(1)} %project_left.1.left_ref, bf16[64,1024]{1,0:T(8,128)(2,1)S(1)} %collective-permute-done.4.embedded_ref, bf16[256,256]{1,0:T(8,128)(2,1)S(1)} %get-tuple-element.29.right_weight_ref, ...), custom_call_target="tpu_custom_call" | custom-call | flops 5000000000 | bytes 16000000 | tf_op jit(solution)/shard_map/pairs/pallas_call | solution.py:560
  28.2 4.3 %collective-permute-start.8 = (bf16[32,1024]{1,0:T(8,128)(2,1)S(1)}, bf16[32,1024]{1,0:T(8,128)(2,1)S(1)}, u32[]{:S(2)}, u32[]{:S(2)}) collective-permute-start(bf16[32,1024]{1,0:T(8,128)(2,1)S(1)} %get-tuple-element.44.refs_5_), channel_id=1, source_target_pairs={{0,0},{1,4},{2,8},{3,12},{4,1},{5,5},{6,9},{7,13},{8,2},{9,6},{10,... | collective-permute-start | bytes 196616 | tf_op jit(solution)/shard_map/ppermute | solution.py:425
  32.5 1.2 %own.1 = (bf16[64,64,128]{2,1,0:T(8,128)(2,1)}, f32[32,64,128]{2,1,0:T(8,128)S(1)}) custom-call(bf16[64,32,128]{2,1,0:T(8,128)(2,1)S(1)} %get-tuple-element.39.refs_0_, bf16[48,32,128]{2,1,0:T(8,128)(2,1)S(1)} %get-tuple-element.41.refs_1_, bf16[16,32,128]{2,1,0:T(8,128)(2,1)S(1)} %get-tuple-element.43.refs_2_, ...), custom_call_target="tpu_custom_call" | custom-call | tf_op jit(solution)/shard_map/own/pallas_call | solution.py:598
  33.8 4.8 %collective-permute-done.7.refs_1_ = bf16[32,3072]{1,0:T(8,128)(2,1)S(1)} collective-permute-done((bf16[32,3072]{1,0:T(8,128)(2,1)S(1)}, bf16[32,3072]{1,0:T(8,128)(2,1)S(1)}, u32[]{:S(2)}, u32[]{:S(2)}) %collective-permute-start.7) | collective-permute-done | bytes 196640 | tf_op jit(solution)/shard_map/ppermute | solution.py:425
  38.5 1.4 %collective-permute-done.8.refs_2_ = bf16[32,1024]{1,0:T(8,128)(2,1)S(1)} collective-permute-done((bf16[32,1024]{1,0:T(8,128)(2,1)S(1)}, bf16[32,1024]{1,0:T(8,128)(2,1)S(1)}, u32[]{:S(2)}, u32[]{:S(2)}) %collective-permute-start.8) | collective-permute-done | bytes 65568 | tf_op jit(solution)/shard_map/ppermute | solution.py:425
  39.9 0.1 collective-permute-done.6.refs_0_
  40.0 0.9 %final.1 = bf16[64,4096]{1,0:T(8,128)(2,1)} custom-call(f32[32,64,128]{2,1,0:T(8,128)S(1)} %get-tuple-element.46.own_ref, f32[1,128]{1,0:T(1,128)S(1)} %get-tuple-element.47.bias_ref, bf16[32,4096]{1,0:T(8,128)(2,1)S(1)} %collective-permute-done.6.refs_0_, bf16[32,3072]{1,0:T(8,128)(2,1)S(1)} %collective-permute-done.7.refs_1_, ...), custom_call_target="tpu_custom_call" | custom-call | tf_op jit(solution)/shard_map/final/pallas_call | solution.py:611
  (3 shorter events, 0.0 us)
Async XLA Ops:
  0.6 2.0 %collective-permute-start = (bf16[64,512]{1,0:T(8,128)(2,1)}, bf16[64,512]{1,0:T(8,128)(2,1)S(1)}, u32[]{:S(2)}, u32[]{:S(2)}) collective-permute-start(bf16[64,512]{1,0:T(8,128)(2,1)} %state_hbm.1), channel_id=1, source_target_pairs={{0,1},{1,0},{2,3},{3,2},{4,5},{5,4},{6,7},{7,6},{8,9},{9,8},{10,11... | collective-permute-start | bytes 196616 | tf_op jit(solution)/shard_map/ppermute | solution.py:425
  0.7 1.9 %collective-permute-start.1 = (s32[16,64]{1,0:T(8,128)}, s32[16,64]{1,0:T(8,128)S(1)}, u32[]{:S(2)}, u32[]{:S(2)}) collective-permute-start(s32[16,64]{1,0:T(8,128)} %bitcast.7), channel_id=1, source_target_pairs={{0,1},{1,0},{2,3},{3,2},{4,5},{5,4},{6,7},{7,6},{8,9},{9,8},{10,11... | collective-permute-start | bytes 12296 | tf_op jit(solution)/shard_map/ppermute | solution.py:425
  2.9 8.8 %collective-permute-start.2 = (bf16[64,1024]{1,0:T(8,128)(2,1)S(1)}, bf16[64,1024]{1,0:T(8,128)(2,1)S(1)}, u32[]{:S(2)}, u32[]{:S(2)}) collective-permute-start(bf16[64,1024]{1,0:T(8,128)(2,1)S(1)} %embed_group.1.embedded_ref), channel_id=1, source_target_pairs={{0,2},{1,3},{2,0},{3,1},{4,6},{5,7},{6,4},{7,5},{8,10},{9,11},{10,... | collective-permute-start | bytes 393224 | tf_op jit(solution)/shard_map/ppermute | solution.py:425
  3.0 10.1 %collective-permute-start.3 = (bf16[64,1024]{1,0:T(8,128)(2,1)S(1)}, bf16[64,1024]{1,0:T(8,128)(2,1)S(1)}, u32[]{:S(2)}, u32[]{:S(2)}) collective-permute-start(bf16[64,1024]{1,0:T(8,128)(2,1)S(1)} %embed_group.1.embedded_ref), channel_id=1, source_target_pairs={{0,8},{1,12},{2,0},{3,4},{4,9},{5,13},{6,1},{7,5},{8,10},{9,14},{1... | collective-permute-start | bytes 393224 | tf_op jit(solution)/shard_map/ppermute | solution.py:425
  5.0 12.9 %collective-permute-start.4 = (bf16[64,1024]{1,0:T(8,128)(2,1)S(1)}, bf16[64,1024]{1,0:T(8,128)(2,1)S(1)}, u32[]{:S(2)}, u32[]{:S(2)}) collective-permute-start(bf16[64,1024]{1,0:T(8,128)(2,1)S(1)} %embed_group.1.embedded_ref), channel_id=1, source_target_pairs={{0,0},{1,4},{2,8},{3,12},{4,1},{5,5},{6,9},{7,13},{8,2},{9,6},{10,... | collective-permute-start | bytes 393224 | tf_op jit(solution)/shard_map/ppermute | solution.py:425
  17.8 8.2 %collective-permute-start.5 = (bf16[32,4096]{1,0:T(8,128)(2,1)S(1)}, bf16[32,4096]{1,0:T(8,128)(2,1)S(1)}, u32[]{:S(2)}, u32[]{:S(2)}) collective-permute-start(bf16[32,4096]{1,0:T(8,128)(2,1)S(1)} %get-tuple-element.40.rest_0_.refs_3_), channel_id=1, source_target_pairs={{0,2},{1,3},{2,0},{3,1},{4,6},{5,7},{6,4},{7,5},{8,10},{9,11},{10,... | collective-permute-start | bytes 786440 | tf_op jit(solution)/shard_map/ppermute | solution.py:425
  22.0 16.5 %collective-permute-start.7 = (bf16[32,3072]{1,0:T(8,128)(2,1)S(1)}, bf16[32,3072]{1,0:T(8,128)(2,1)S(1)}, u32[]{:S(2)}, u32[]{:S(2)}) collective-permute-start(bf16[32,3072]{1,0:T(8,128)(2,1)S(1)} %get-tuple-element.42.rest_0_.refs_4_), channel_id=1, source_target_pairs={{0,0},{1,4},{2,8},{3,12},{4,1},{5,5},{6,9},{7,13},{8,2},{9,6},{10,... | collective-permute-start | bytes 589832 | tf_op jit(solution)/shard_map/ppermute | solution.py:425
  26.1 14.0 %collective-permute-start.6 = (bf16[32,4096]{1,0:T(8,128)(2,1)S(1)}, bf16[32,4096]{1,0:T(8,128)(2,1)S(1)}, u32[]{:S(2)}, u32[]{:S(2)}) collective-permute-start(bf16[32,4096]{1,0:T(8,128)(2,1)S(1)} %collective-permute-done.5.rest_1_), channel_id=1, source_target_pairs={{0,8},{1,12},{2,0},{3,4},{4,9},{5,13},{6,1},{7,5},{8,10},{9,14},{1... | collective-permute-start | bytes 786440 | tf_op jit(solution)/shard_map/ppermute | solution.py:425
  28.2 11.7 %collective-permute-start.8 = (bf16[32,1024]{1,0:T(8,128)(2,1)S(1)}, bf16[32,1024]{1,0:T(8,128)(2,1)S(1)}, u32[]{:S(2)}, u32[]{:S(2)}) collective-permute-start(bf16[32,1024]{1,0:T(8,128)(2,1)S(1)} %get-tuple-element.44.refs_5_), channel_id=1, source_target_pairs={{0,0},{1,4},{2,8},{3,12},{4,1},{5,5},{6,9},{7,13},{8,2},{9,6},{10,... | collective-permute-start | bytes 196616 | tf_op jit(solution)/shard_map/ppermute | solution.py:425

commit v7 on v6

--- a/solution.py
+++ b/solution.py
@@ -298,9 +298,14 @@
                 + (first_ref[i : i + 1, :] + base)
                 + mask * part[:, q * channels : (q + 1) * channels]
             )
-    half = start.shape[1] if start.shape[1] < 1024 else 512
-    for q, at in ((q, slice(n, n + half)) for q in range(2) for n in range(0, start.shape[1], half)):
-        value = start[q, at]
+    count = start.shape[1]
+    if count <= 256:
+        blocks = [[(0, slice(0, count)), (1, slice(0, count))]]
+    else:
+        step = count // pl.cdiv(count, 512)
+        blocks = [[(q, slice(n, n + step))] for q in range(2) for n in range(0, count, step)]
+    for block in blocks:
+        value = jnp.concatenate([start[q, at] for q, at in block], axis=0)
         mean = jnp.mean(value, axis=-1, keepdims=True)
         centered = value - mean
         variance = jnp.mean(centered * centered, axis=-1, keepdims=True)
@@ -308,7 +313,10 @@
         gate_up = dot(normed, gate_up_ref[...])
         gate, up = gate_up[:, :hid], gate_up[:, hid:]
         hidden = (0.5 * gate * (1.0 + jnp.tanh(0.5 * gate)) * up).astype(BF16)
-        start[q, at] = value + dot(hidden, down_ref[...])
+        value = value + dot(hidden, down_ref[...])
+        for n, (q, at) in enumerate(block):
+            rows_here = at.stop - at.start
+            start[q, at] = value[n * rows_here : (n + 1) * rows_here]
     result = [start[q].astype(BF16) for q in range(2)]
     for p in range(pairs):
         for q in range(2):

time: 41.2 us -> 40.8 us (level)
  transfers between devices with their start and end apart: 9 -> 9, of which waited for: 4 -> 4; matrix products, arithmetic and copies ran while one was open for 0% -> 0% of each run, Pallas kernels for 39% -> 38%
where the time goes in v7:
time: 40.8 us; the launch traced here: 40.6 us
  Pallas kernels  16.8 us (41%)
  starting transfers between devices  16 us (39%)
  waiting for transfers between devices  7.02 us (17%)
  between operations  0.77 us (2%)
    ppermute x9, starting transfers between devices, moved(): return lax.ppermute(value, axes, pairs)  16 us
    pallas_call x3, Pallas kernels, local(): pl.pallas_call(functools.partial(pair_kernel, part), out_shape=(jax.Shape...  10.3 us
    ppermute x9, waiting for transfers between devices, moved(): return lax.ppermute(value, axes, pairs)  7.02 us
    pallas_call x1, Pallas kernels, local(): pl.pallas_call(weights_kernel, out_shape=(jax.ShapeDtypeStruct((length, c...  2.25 us
    pallas_call x1, Pallas kernels, local(): pl.pallas_call(embed_own_kernel, out_shape=(jax.ShapeDtypeStruct(alignmen...  1.37 us
    pallas_call x1, Pallas kernels, local(): pl.pallas_call(own_kernel, out_shape=(jax.ShapeDtypeStruct(pair_state.sha...  1.25 us
    pallas_call x1, Pallas kernels, local(): pl.pallas_call(final_kernel, out_shape=jax.ShapeDtypeStruct((length, leng...  0.95 us
  transfers between devices with their start and end apart: 9, of which 4 were waited for; matrix products, arithmetic and copies ran while one was open for 0% of the time, Pallas kernels for 38%

profile of v7, /device:TPU:2, one launch (start us, length us, event | category | flops | bytes accessed | tf_op | source)
XLA Modules:
  0.0 40.6 jit_solution(5687488716735717155)
XLA Ops:
  0.6 0.1 collective-permute-start
  0.7 0.5 %collective-permute-start.1 = (s32[16,64]{1,0:T(8,128)}, s32[16,64]{1,0:T(8,128)S(1)}, u32[]{:S(2)}, u32[]{:S(2)}) collective-permute-start(s32[16,64]{1,0:T(8,128)} %bitcast.7), channel_id=1, source_target_pairs={{0,1},{1,0},{2,3},{3,2},{4,5},{5,4},{6,7},{7,6},{8,9},{9,8},{10,11... | collective-permute-start | bytes 12296 | tf_op jit(solution)/shard_map/ppermute | solution.py:433
  1.2 1.4 %embed_own.1 = (bf16[64,512]{1,0:T(8,128)(2,1)S(1)}, bf16[256,256]{1,0:T(8,128)(2,1)S(1)}) custom-call(bf16[64,512]{1,0:T(8,128)(2,1)} %state_hbm.1, s32[16,64]{1,0:T(8,128)} %bitcast.8, bf16[32,32]{1,0:T(8,128)(2,1)} %table_hbm.1), custom_call_target="tpu_custom_call" | custom-call | tf_op jit(solution)/shard_map/embed_own/pallas_call | solution.py:443
  2.6 0.0 collective-permute-done.1.refs_1_
  2.6 0.3 embed_group.1.embedded_ref
  2.9 0.1 collective-permute-start.2
  3.0 2.0 %collective-permute-start.3 = (bf16[64,1024]{1,0:T(8,128)(2,1)S(1)}, bf16[64,1024]{1,0:T(8,128)(2,1)S(1)}, u32[]{:S(2)}, u32[]{:S(2)}) collective-permute-start(bf16[64,1024]{1,0:T(8,128)(2,1)S(1)} %embed_group.1.embedded_ref), channel_id=1, source_target_pairs={{0,8},{1,12},{2,0},{3,4},{4,9},{5,13},{6,1},{7,5},{8,10},{9,14},{1... | collective-permute-start | bytes 393224 | tf_op jit(solution)/shard_map/ppermute | solution.py:433
  5.0 4.5 %collective-permute-start.4 = (bf16[64,1024]{1,0:T(8,128)(2,1)S(1)}, bf16[64,1024]{1,0:T(8,128)(2,1)S(1)}, u32[]{:S(2)}, u32[]{:S(2)}) collective-permute-start(bf16[64,1024]{1,0:T(8,128)(2,1)S(1)} %embed_group.1.embedded_ref), channel_id=1, source_target_pairs={{0,0},{1,4},{2,8},{3,12},{4,1},{5,5},{6,9},{7,13},{8,2},{9,6},{10,... | collective-permute-start | bytes 393224 | tf_op jit(solution)/shard_map/ppermute | solution.py:433
  9.5 2.2 %weights.1 = (f32[64,128]{1,0:T(8,128)S(1)}, f32[4,64,128]{2,1,0:T(8,128)S(1)}, f32[4,64,128]{2,1,0:T(8,128)S(1)}, bf16[2048,256]{1,0:T(8,128)(2,1)S(1)}, bf16[6...) custom-call(s32[1,256]{1,0:T(1,128)} %bitcast.9, ...), custom_call_target="tpu_custom_call" | custom-call | tf_op jit(solution)/shard_map/weights/pallas_call | solution.py:493
  11.7 0.0 collective-permute-done.2.other_ref
  11.7 0.3 project_left.1.left_ref
  12.1 1.1 %collective-permute-done.3.embedded_ref = bf16[64,1024]{1,0:T(8,128)(2,1)S(1)} collective-permute-done((bf16[64,1024]{1,0:T(8,128)(2,1)S(1)}, bf16[64,1024]{1,0:T(8,128)(2,1)S(1)}, u32[]{:S(2)}, u32[]{:S(2)}) %collective-permute-start.3) | collective-permute-done | bytes 131104 | tf_op jit(solution)/shard_map/ppermute | solution.py:433
  13.1 4.7 %pairs.3 = (bf16[64,32,128]{2,1,0:T(8,128)(2,1)S(1)}, bf16[32,4096]{1,0:T(8,128)(2,1)S(1)}) custom-call(bf16[128,4096]{1,0:T(8,128)(2,1)S(1)} %project_left.1.left_ref, bf16[64,1024]{1,0:T(8,128)(2,1)S(1)} %collective-permute-done.3.embedded_ref, bf16[256,256]{1,0:T(8,128)(2,1)S(1)} %get-tuple-element.29.right_weight_ref, ...), custom_call_target="tpu_custom_call" | custom-call | flops 5000000000 | bytes 16000000 | tf_op jit(solution)/shard_map/pairs/pallas_call | solution.py:568
  17.8 0.1 collective-permute-start.5
  17.9 3.7 %pairs.4 = (bf16[48,32,128]{2,1,0:T(8,128)(2,1)S(1)}, bf16[32,3072]{1,0:T(8,128)(2,1)S(1)}) custom-call(bf16[128,4096]{1,0:T(8,128)(2,1)S(1)} %project_left.1.left_ref, bf16[64,1024]{1,0:T(8,128)(2,1)S(1)} %collective-permute-done.4.embedded_ref, bf16[256,256]{1,0:T(8,128)(2,1)S(1)} %get-tuple-element.29.right_weight_ref, ...), custom_call_target="tpu_custom_call" | custom-call | flops 5000000000 | bytes 16000000 | tf_op jit(solution)/shard_map/pairs/pallas_call | solution.py:568
  21.6 4.1 %collective-permute-start.7 = (bf16[32,3072]{1,0:T(8,128)(2,1)S(1)}, bf16[32,3072]{1,0:T(8,128)(2,1)S(1)}, u32[]{:S(2)}, u32[]{:S(2)}) collective-permute-start(bf16[32,3072]{1,0:T(8,128)(2,1)S(1)} %get-tuple-element.42.rest_0_.refs_4_), channel_id=1, source_target_pairs={{0,0},{1,4},{2,8},{3,12},{4,1},{5,5},{6,9},{7,13},{8,2},{9,6},{10,... | collective-permute-start | bytes 589832 | tf_op jit(solution)/shard_map/ppermute | solution.py:433
  25.7 0.5 %collective-permute-start.6 = (bf16[32,4096]{1,0:T(8,128)(2,1)S(1)}, bf16[32,4096]{1,0:T(8,128)(2,1)S(1)}, u32[]{:S(2)}, u32[]{:S(2)}) collective-permute-start(bf16[32,4096]{1,0:T(8,128)(2,1)S(1)} %collective-permute-done.5.rest_1_), channel_id=1, source_target_pairs={{0,8},{1,12},{2,0},{3,4},{4,9},{5,13},{6,1},{7,5},{8,10},{9,14},{1... | collective-permute-start | bytes 786440 | tf_op jit(solution)/shard_map/ppermute | solution.py:433
  26.2 2.0 %pairs.5 = (bf16[16,32,128]{2,1,0:T(8,128)(2,1)S(1)}, bf16[32,1024]{1,0:T(8,128)(2,1)S(1)}) custom-call(bf16[128,4096]{1,0:T(8,128)(2,1)S(1)} %project_left.1.left_ref, bf16[64,1024]{1,0:T(8,128)(2,1)S(1)} %collective-permute-done.4.embedded_ref, bf16[256,256]{1,0:T(8,128)(2,1)S(1)} %get-tuple-element.29.right_weight_ref, ...), custom_call_target="tpu_custom_call" | custom-call | flops 5000000000 | bytes 16000000 | tf_op jit(solution)/shard_map/pairs/pallas_call | solution.py:568
  28.2 4.3 %collective-permute-start.8 = (bf16[32,1024]{1,0:T(8,128)(2,1)S(1)}, bf16[32,1024]{1,0:T(8,128)(2,1)S(1)}, u32[]{:S(2)}, u32[]{:S(2)}) collective-permute-start(bf16[32,1024]{1,0:T(8,128)(2,1)S(1)} %get-tuple-element.44.refs_5_), channel_id=1, source_target_pairs={{0,0},{1,4},{2,8},{3,12},{4,1},{5,5},{6,9},{7,13},{8,2},{9,6},{10,... | collective-permute-start | bytes 196616 | tf_op jit(solution)/shard_map/ppermute | solution.py:433
  32.5 1.2 %own.1 = (bf16[64,64,128]{2,1,0:T(8,128)(2,1)}, f32[32,64,128]{2,1,0:T(8,128)S(1)}) custom-call(bf16[64,32,128]{2,1,0:T(8,128)(2,1)S(1)} %get-tuple-element.39.refs_0_, bf16[48,32,128]{2,1,0:T(8,128)(2,1)S(1)} %get-tuple-element.41.refs_1_, bf16[16,32,128]{2,1,0:T(8,128)(2,1)S(1)} %get-tuple-element.43.refs_2_, ...), custom_call_target="tpu_custom_call" | custom-call | tf_op jit(solution)/shard_map/own/pallas_call | solution.py:606
  33.7 4.4 %collective-permute-done.7.refs_1_ = bf16[32,3072]{1,0:T(8,128)(2,1)S(1)} collective-permute-done((bf16[32,3072]{1,0:T(8,128)(2,1)S(1)}, bf16[32,3072]{1,0:T(8,128)(2,1)S(1)}, u32[]{:S(2)}, u32[]{:S(2)}) %collective-permute-start.7) | collective-permute-done | bytes 196640 | tf_op jit(solution)/shard_map/ppermute | solution.py:433
  38.1 1.4 %collective-permute-done.8.refs_2_ = bf16[32,1024]{1,0:T(8,128)(2,1)S(1)} collective-permute-done((bf16[32,1024]{1,0:T(8,128)(2,1)S(1)}, bf16[32,1024]{1,0:T(8,128)(2,1)S(1)}, u32[]{:S(2)}, u32[]{:S(2)}) %collective-permute-start.8) | collective-permute-done | bytes 65568 | tf_op jit(solution)/shard_map/ppermute | solution.py:433
  39.5 0.1 collective-permute-done.6.refs_0_
  39.6 0.9 %final.1 = bf16[64,4096]{1,0:T(8,128)(2,1)} custom-call(f32[32,64,128]{2,1,0:T(8,128)S(1)} %get-tuple-element.46.own_ref, f32[1,128]{1,0:T(1,128)S(1)} %get-tuple-element.47.bias_ref, bf16[32,4096]{1,0:T(8,128)(2,1)S(1)} %collective-permute-done.6.refs_0_, bf16[32,3072]{1,0:T(8,128)(2,1)S(1)} %collective-permute-done.7.refs_1_, ...), custom_call_target="tpu_custom_call" | custom-call | tf_op jit(solution)/shard_map/final/pallas_call | solution.py:619
  (3 shorter events, 0.0 us)
Async XLA Ops:
  0.6 2.0 %collective-permute-start = (bf16[64,512]{1,0:T(8,128)(2,1)}, bf16[64,512]{1,0:T(8,128)(2,1)S(1)}, u32[]{:S(2)}, u32[]{:S(2)}) collective-permute-start(bf16[64,512]{1,0:T(8,128)(2,1)} %state_hbm.1), channel_id=1, source_target_pairs={{0,1},{1,0},{2,3},{3,2},{4,5},{5,4},{6,7},{7,6},{8,9},{9,8},{10,11... | collective-permute-start | bytes 196616 | tf_op jit(solution)/shard_map/ppermute | solution.py:433
  0.7 1.9 %collective-permute-start.1 = (s32[16,64]{1,0:T(8,128)}, s32[16,64]{1,0:T(8,128)S(1)}, u32[]{:S(2)}, u32[]{:S(2)}) collective-permute-start(s32[16,64]{1,0:T(8,128)} %bitcast.7), channel_id=1, source_target_pairs={{0,1},{1,0},{2,3},{3,2},{4,5},{5,4},{6,7},{7,6},{8,9},{9,8},{10,11... | collective-permute-start | bytes 12296 | tf_op jit(solution)/shard_map/ppermute | solution.py:433
  2.9 8.8 %collective-permute-start.2 = (bf16[64,1024]{1,0:T(8,128)(2,1)S(1)}, bf16[64,1024]{1,0:T(8,128)(2,1)S(1)}, u32[]{:S(2)}, u32[]{:S(2)}) collective-permute-start(bf16[64,1024]{1,0:T(8,128)(2,1)S(1)} %embed_group.1.embedded_ref), channel_id=1, source_target_pairs={{0,2},{1,3},{2,0},{3,1},{4,6},{5,7},{6,4},{7,5},{8,10},{9,11},{10,... | collective-permute-start | bytes 393224 | tf_op jit(solution)/shard_map/ppermute | solution.py:433
  3.0 10.1 %collective-permute-start.3 = (bf16[64,1024]{1,0:T(8,128)(2,1)S(1)}, bf16[64,1024]{1,0:T(8,128)(2,1)S(1)}, u32[]{:S(2)}, u32[]{:S(2)}) collective-permute-start(bf16[64,1024]{1,0:T(8,128)(2,1)S(1)} %embed_group.1.embedded_ref), channel_id=1, source_target_pairs={{0,8},{1,12},{2,0},{3,4},{4,9},{5,13},{6,1},{7,5},{8,10},{9,14},{1... | collective-permute-start | bytes 393224 | tf_op jit(solution)/shard_map/ppermute | solution.py:433
  5.0 12.9 %collective-permute-start.4 = (bf16[64,1024]{1,0:T(8,128)(2,1)S(1)}, bf16[64,1024]{1,0:T(8,128)(2,1)S(1)}, u32[]{:S(2)}, u32[]{:S(2)}) collective-permute-start(bf16[64,1024]{1,0:T(8,128)(2,1)S(1)} %embed_group.1.embedded_ref), channel_id=1, source_target_pairs={{0,0},{1,4},{2,8},{3,12},{4,1},{5,5},{6,9},{7,13},{8,2},{9,6},{10,... | collective-permute-start | bytes 393224 | tf_op jit(solution)/shard_map/ppermute | solution.py:433
  17.8 7.9 %collective-permute-start.5 = (bf16[32,4096]{1,0:T(8,128)(2,1)S(1)}, bf16[32,4096]{1,0:T(8,128)(2,1)S(1)}, u32[]{:S(2)}, u32[]{:S(2)}) collective-permute-start(bf16[32,4096]{1,0:T(8,128)(2,1)S(1)} %get-tuple-element.40.rest_0_.refs_3_), channel_id=1, source_target_pairs={{0,2},{1,3},{2,0},{3,1},{4,6},{5,7},{6,4},{7,5},{8,10},{9,11},{10,... | collective-permute-start | bytes 786440 | tf_op jit(solution)/shard_map/ppermute | solution.py:433
  21.6 16.5 %collective-permute-start.7 = (bf16[32,3072]{1,0:T(8,128)(2,1)S(1)}, bf16[32,3072]{1,0:T(8,128)(2,1)S(1)}, u32[]{:S(2)}, u32[]{:S(2)}) collective-permute-start(bf16[32,3072]{1,0:T(8,128)(2,1)S(1)} %get-tuple-element.42.rest_0_.refs_4_), channel_id=1, source_target_pairs={{0,0},{1,4},{2,8},{3,12},{4,1},{5,5},{6,9},{7,13},{8,2},{9,6},{10,... | collective-permute-start | bytes 589832 | tf_op jit(solution)/shard_map/ppermute | solution.py:433
  25.7 14.0 %collective-permute-start.6 = (bf16[32,4096]{1,0:T(8,128)(2,1)S(1)}, bf16[32,4096]{1,0:T(8,128)(2,1)S(1)}, u32[]{:S(2)}, u32[]{:S(2)}) collective-permute-start(bf16[32,4096]{1,0:T(8,128)(2,1)S(1)} %collective-permute-done.5.rest_1_), channel_id=1, source_target_pairs={{0,8},{1,12},{2,0},{3,4},{4,9},{5,13},{6,1},{7,5},{8,10},{9,14},{1... | collective-permute-start | bytes 786440 | tf_op jit(solution)/shard_map/ppermute | solution.py:433
  28.2 11.3 %collective-permute-start.8 = (bf16[32,1024]{1,0:T(8,128)(2,1)S(1)}, bf16[32,1024]{1,0:T(8,128)(2,1)S(1)}, u32[]{:S(2)}, u32[]{:S(2)}) collective-permute-start(bf16[32,1024]{1,0:T(8,128)(2,1)S(1)} %get-tuple-element.44.refs_5_), channel_id=1, source_target_pairs={{0,0},{1,4},{2,8},{3,12},{4,1},{5,5},{6,9},{7,13},{8,2},{9,6},{10,... | collective-permute-start | bytes 196616 | tf_op jit(solution)/shard_map/ppermute | solution.py:433
